TPU v7x, 256 devices: a whole 4x4x8 slice. The times are simulated.
256 devices in a mesh: patch: 16 (over z_lo, x, core), latent: 16 (over z_hi, y).
Axes of the slice: x: 4, y: 4, z: 8 (z_hi: 4, z_lo: 2; z = z_hi * 2 + z_lo), core: 2. Of those that a mesh axis runs over, the one named last changes fastest.
Arguments:
- queries: bfloat16 [1024, 1536], P('latent', 'patch'), may hold values from -54 to 54
- tile_keys: bfloat16 [12288, 1536], P('patch'), may hold values from -6 to 6
- tile_values: bfloat16 [12288, 1536], P('patch'), may hold values from -6 to 6
- region_ids: int32 [12288], P('patch'), may hold values from 0 to 15
- block_list: int32 [16, 80], P('latent'), may hold values from 0 to 95, as said below
- region_bias: float32 [16, 16], P('latent'), may hold values from -2 to 2
- grad_out: bfloat16 [1024, 1536], P('latent', 'patch'), may hold values from -6 to 6
Outputs:
- attended: bfloat16 [1024, 1536], P('latent', 'patch')
- grad_queries: bfloat16 [1024, 1536], P('latent', 'patch')
- grad_keys: bfloat16 [1536, 12288], P('latent', 'patch')
- grad_values: bfloat16 [1536, 12288], P('latent', 'patch')
Inputs may be any that keep to these rules, and one draw needn't show every extreme that they name: `block_list`: each row names 80 different tile blocks.
All inputs are finite; a program needn't handle non-finite values.
Results may differ from a plain program's by a relative error of at most 0.0035.
The roundings to bfloat16 on the way count: a program that leaves them out, or rounds other values in their place, can miss the bound.
Values may be sent and summed in bfloat16 or wider, within the bound.
No kernel may reach another device: no remote copies, remote signals or barrier semaphores. Data moves between devices by JAX's collectives and lax.ppermute only.
A program may use at most 64 MiB of HBM per device.

v0:
```python
import jax
import jax.numpy as jnp
from jax import lax
from jax.sharding import PartitionSpec as P

BLOCK = 128


def combined_all(value, axis, join):
    pieces = jax.tree.map(lambda part: lax.all_gather(part, axis), value)
    head = jax.tree.map(lambda part: part[0], pieces)
    tail = jax.tree.map(lambda part: part[1:], pieces)
    running, _ = lax.scan(lambda running, piece: (join(running, piece), None), head, tail)
    return running


def merge_stats(first, second):
    top_a, total_a = first
    top_b, total_b = second
    row_top = jnp.maximum(top_a, top_b)
    return (row_top, total_a * jnp.exp(top_a - row_top) + total_b * jnp.exp(top_b - row_top))


def shards(queries, tile_keys, tile_values, region_ids, block_list, region_bias, grad_out):
    query_full, grad_full = (
        lax.all_gather(queries, "patch", axis=1, tiled=True),
        lax.all_gather(grad_out, "patch", axis=1, tiled=True),
    )
    row_count, feat_width = query_full.shape
    block_count = tile_keys.shape[0] // BLOCK
    tile_count = block_count * BLOCK
    score_scale = feat_width ** (-0.5)
    my_patch = lax.axis_index("patch")
    owned_ids = my_patch * block_count + jnp.arange(block_count, dtype=jnp.int32)
    chosen = jnp.any(block_list[0][:, None] == owned_ids[None, :], axis=0)
    tile_mask = jnp.repeat(chosen, BLOCK)
    labels = jnp.arange(region_bias.shape[1], dtype=jnp.int32)
    tile_bias = jnp.sum(
        jnp.where(region_ids[:, None] == labels[None, :], region_bias[0][None, :], 0.0), axis=1
    )
    contract_last = (((1,), (1,)), ((), ()))
    contract_first = (((0,), (0,)), ((), ()))

    def score_step(block_index, score_all):

        def score_take(buffer):
            begin_row = block_index * BLOCK
            key_block = lax.dynamic_slice_in_dim(tile_keys, begin_row, BLOCK, 0)
            bias_piece = lax.dynamic_slice_in_dim(tile_bias, begin_row, BLOCK, 0)
            scores = (
                lax.dot_general(
                    query_full, key_block, contract_last, preferred_element_type=jnp.float32
                )
                * score_scale
            )
            return lax.dynamic_update_slice_in_dim(
                buffer, scores + bias_piece[None, :], begin_row, 1
            )

        return lax.cond(chosen[block_index], score_take, lambda buffer: buffer, score_all)

    score_all = lax.fori_loop(
        0, block_count, score_step, jnp.full((row_count, tile_count), -1e30, jnp.float32)
    )
    local_top = jnp.max(score_all, axis=1)
    local_total = jnp.sum(
        jnp.where(tile_mask[None, :], jnp.exp(score_all - local_top[:, None]), 0.0), axis=1
    )
    row_peak, row_whole = combined_all((local_top, local_total), "patch", merge_stats)
    weights = jnp.where(
        tile_mask[None, :], jnp.exp(score_all - row_peak[:, None]) / row_whole[:, None], 0.0
    )
    weights_low = weights.astype(jnp.bfloat16)

    def mix_step(block_index, mixed_now):

        def mix_take(current):
            begin_row = block_index * BLOCK
            value_block = lax.dynamic_slice_in_dim(tile_values, begin_row, BLOCK, 0)
            weight_block = lax.dynamic_slice_in_dim(weights_low, begin_row, BLOCK, 1)
            return current + jnp.dot(weight_block, value_block, preferred_element_type=jnp.float32)

        return lax.cond(chosen[block_index], mix_take, lambda current: current, mixed_now)

    mixed_part = lax.fori_loop(
        0, block_count, mix_step, jnp.zeros((row_count, feat_width), jnp.float32)
    )
    col_share = feat_width // lax.axis_size("patch")
    full_rows = lax.psum(mixed_part, "patch")
    row_delta = jnp.sum(grad_full.astype(jnp.float32) * full_rows, axis=1)
    result = lax.dynamic_slice_in_dim(full_rows, my_patch * col_share, col_share, 1)
    attended = result.astype(jnp.bfloat16)

    def block_terms(block_index, query_sum):

        def block_take(query_now):
            begin_row = block_index * BLOCK
            key_block = lax.dynamic_slice_in_dim(tile_keys, begin_row, BLOCK, 0)
            value_block = lax.dynamic_slice_in_dim(tile_values, begin_row, BLOCK, 0)
            weight_block = lax.dynamic_slice_in_dim(weights, begin_row, BLOCK, 1)
            weight_low_block = lax.dynamic_slice_in_dim(weights_low, begin_row, BLOCK, 1)
            dweights = lax.dot_general(
                grad_full, value_block, contract_last, preferred_element_type=jnp.float32
            )
            dscores = (weight_block * (dweights - row_delta[:, None])).astype(jnp.bfloat16)
            query_now = (
                query_now
                + jnp.dot(dscores, key_block, preferred_element_type=jnp.float32) * score_scale
            )
            key_term = (
                lax.dot_general(
                    query_full, dscores, contract_first, preferred_element_type=jnp.float32
                )
                * score_scale
            )
            value_term = lax.dot_general(
                grad_full, weight_low_block, contract_first, preferred_element_type=jnp.float32
            )
            return (query_now, key_term, value_term)

        def skip(query_now):
            zero_block = jnp.zeros((feat_width, BLOCK), jnp.float32)
            return (query_now, zero_block, zero_block)

        return lax.cond(chosen[block_index], block_take, skip, query_sum)

    query_start = jnp.zeros((row_count, feat_width), jnp.float32)

    def after_step(block_index, current):
        query_sum, key_all, value_all = current
        query_sum, key_term, value_term = block_terms(block_index, query_sum)
        key_all = lax.dynamic_update_slice_in_dim(key_all, key_term, block_index * BLOCK, 1)
        value_all = lax.dynamic_update_slice_in_dim(value_all, value_term, block_index * BLOCK, 1)
        return (query_sum, key_all, value_all)

    zero_terms = jnp.zeros((feat_width, tile_count), jnp.float32)
    query_sum, key_all, value_all = lax.fori_loop(
        0, block_count, after_step, (query_start, zero_terms, zero_terms)
    )
    key_part, value_part = (
        lax.psum_scatter(key_all, "latent", scatter_dimension=0, tiled=True),
        lax.psum_scatter(value_all, "latent", scatter_dimension=0, tiled=True),
    )
    grad_keys = key_part.astype(jnp.bfloat16)
    grad_values = value_part.astype(jnp.bfloat16)
    grad_queries = lax.psum_scatter(query_sum, "patch", scatter_dimension=1, tiled=True).astype(
        jnp.bfloat16
    )
    return (attended, grad_queries, grad_keys, grad_values)


def solution(mesh):
    in_specs = (
        P("latent", "patch"),
        P("patch", None),
        P("patch", None),
        P("patch"),
        P("latent", None),
        P("latent", None),
        P("latent", "patch"),
    )
    out_specs = (
        P("latent", "patch"),
        P("latent", "patch"),
        P("latent", "patch"),
        P("latent", "patch"),
    )
    return jax.shard_map(shards, mesh=mesh, in_specs=in_specs, out_specs=out_specs, check_vma=False)
```

profile of v0, /device:TPU:1, one launch (start us, length us, event | category | flops | bytes accessed | tf_op | source)
XLA Modules:
  0.0 532.2 jit_solution(3095899879336360681)
XLA Ops:
  7.2 0.8 compare_reduce_fusion
  8.2 22.3 %all-gather.2 = bf16[16,96,64]{1,2,0:T(8,128)(2,1)S(1)} all-gather(bf16[1,96,64]{1,2,0:T(8,128)(2,1)} %bitcast.68), channel_id=1, replica_groups=mesh['patch'=16,'latent'=16] {'patch'}, dimensions={0}, use_global_device_ids=true | all-gather | bytes 208896 | tf_op jit(solution)/shard_map/all_gather | solution.py:26
  30.9 0.8 select_reduce_fusion.1
  31.7 12.4 %while.64 = (s32[]{:T(128)}, f32[64,768]{1,0:T(8,128)S(1)}, pred[6]{0:T(512)(128)(4,1)S(1)}, bf16[768,1536]{1,0:T(8,128)(2,1)}, bf16[64,1536]{1,0:T(8,128)(2,1)S(1)}, /*index=5*/f32[768]{0:T(1024)S(1)}, s32[]{:T(128)}) while((s32[]{:T(128)}, f32[64,768]{1,0:T(8,128)S(1)}, pred[6]{0:T(512)(128)(4,1)S(1)}, bf16[768,1536]{1,0:T(8,128)(2,1)}, ...), condition=%wide.region_5.6_spmd, body=%wide.region_2.5_spmd.sunk | while | flops 25182216 | bytes 625346 | solution.py:62
  34.5 1.3 conditional.6
  34.6 1.2 fusion.2
  38.6 1.4 conditional.6
  38.7 1.2 fusion.2
  42.8 1.3 conditional.6
  42.9 1.2 fusion.2
  46.2 28.4 %all-reduce.2 = (f32[1024]{0:T(1024)S(1)}, f32[1024]{0:T(1024)S(1)}) all-reduce(f32[1024]{0:T(1024)S(1)} %dynamic-update-slice, f32[1024]{0:T(1024)S(1)} %dynamic-update-slice.1), channel_id=2, replica_groups=mesh['patch'=16,'latent'=16] {'patch'}, use_global_device_ids=true, to_apply=%add | all-reduce | flops 2048 | bytes 16384
  75.7 11.3 %while.66 = (s32[]{:T(128)}, f32[64,1536]{1,0:T(8,128)S(1)}, pred[6]{0:T(512)(128)(4,1)S(1)}, bf16[64,768]{1,0:T(8,128)(2,1)S(1)}, bf16[768,1536]{1,0:T(8,128)(2,1)}, /*index=5*/s32[]{:T(128)}) while((s32[]{:T(128)}, f32[64,1536]{1,0:T(8,128)S(1)}, pred[6]{0:T(512)(128)(4,1)S(1)}, bf16[64,768]{1,0:T(8,128)(2,1)S(1)}, ...), condition=%wide.region_13.14_spmd, body=%wide.region_10.13_spmd.sunk | while | flops 25264136 | bytes 1197230 | solution.py:85
  78.2 1.2 conditional.7
  78.2 1.2 convolution_add_fusion
  82.0 1.2 conditional.7
  82.0 1.2 convolution_add_fusion
  85.8 1.2 conditional.7
  85.8 1.2 convolution_add_fusion
  87.0 0.7 copy-done
  87.8 20.0 %all-gather.3 = bf16[16,96,64]{1,2,0:T(8,128)(2,1)S(1)} all-gather(bf16[1,96,64]{1,2,0:T(8,128)(2,1)S(1)} %bitcast.69), channel_id=1, replica_groups=mesh['patch'=16,'latent'=16] {'patch'}, dimensions={0}, use_global_device_ids=true | all-gather | bytes 208896 | tf_op jit(solution)/shard_map/all_gather | solution.py:27
  108.3 106.9 %all-reduce.5.cloned.1.call-done = f32[64,1536]{1,0:T(8,128)} async-done(((f32[64,1536]{1,0:T(8,128)}), f32[64,1536]{1,0:T(8,128)}) %all-reduce.5.cloned.1.call-update) | async-done | bytes 393232 | tf_op jit(solution)/shard_map/psum | solution.py:89
  215.3 1.1 multiply_reduce_fusion
  216.4 2.5 broadcast_in_dim.57.clone2
  218.9 2.4 broadcast_in_dim.57.clone
  221.3 28.7 %while.67 = (s32[]{:T(128)}, f32[64,1536]{1,0:T(8,128)S(1)}, f32[1536,768]{1,0:T(8,128)}, f32[1536,768]{1,0:T(8,128)}, pred[6]{0:T(512)(128)(4,1)S(1)}, /*index=...) while((s32[]{:T(128)}, f32[64,1536]{1,0:T(8,128)S(1)}, ...), condition=%wide.region_19.20_spmd, body=%wide.region_16.19_spmd.sunk | while | flops 101081088 | bytes 10126960 | solution.py:137
  223.3 1.4 constant_dynamic-update-slice_fusion.3
  225.9 3.1 conditional.8
  225.9 1.3 fusion.17
  227.2 1.2 fusion.14
  229.5 1.3 constant_dynamic-update-slice_fusion.3
  232.8 1.4 constant_dynamic-update-slice_fusion.3
  235.4 3.1 conditional.8
  235.5 1.3 fusion.17
  236.7 1.2 fusion.14
  239.1 1.4 constant_dynamic-update-slice_fusion.3
  242.4 1.4 constant_dynamic-update-slice_fusion.3
  245.1 3.1 conditional.8
  245.1 1.3 fusion.17
  246.4 1.2 fusion.14
  248.7 1.4 constant_dynamic-update-slice_fusion.3
  250.1 1.2 copy.25
  252.6 1.5 dynamic-slice_convert_fusion
  254.1 66.5 %reduce-scatter.10.cloned.1.call-done = f32[96,64]{1,0:T(8,128)} async-done(((f32[1536,64]{1,0:T(8,128)}), f32[96,64]{1,0:T(8,128)}) %reduce-scatter.10.cloned.1.call-update) | async-done | bytes 24592
  320.6 1.5 copy.26
  322.1 102.1 %reduce-scatter.8.cloned.1.call-done = f32[96,768]{1,0:T(8,128)} async-done(((f32[1536,768]{1,0:T(8,128)}), f32[96,768]{1,0:T(8,128)}) %reduce-scatter.8.cloned.1.call-update) | async-done | bytes 294928 | tf_op jit(solution)/shard_map/reduce_scatter | solution.py:142
  424.2 1.6 convert_element_type.56
  425.8 98.2 %reduce-scatter.6.cloned.1.call-done = f32[96,768]{1,0:T(8,128)} async-done(((f32[1536,768]{1,0:T(8,128)}), f32[96,768]{1,0:T(8,128)}) %reduce-scatter.6.cloned.1.call-update) | async-done | bytes 294928 | tf_op jit(solution)/shard_map/reduce_scatter | solution.py:141
  524.0 1.6 convert_element_type.55
  (106 shorter events, 22.3 us)
Async XLA Ops:
  7.2 37.0 %copy-start.2 = (u32[256]{0:T(256)S(1)}, u32[256]{0:T(256)}, u32[]{:S(2)}) copy-start(u32[256]{0:T(256)} %constant.136) | copy-start | bytes 3076
  7.2 208.1 %all-reduce.5.cloned.1.call-start = ((), (), s32[]{:S(2)}) async-start(), calls=%async_computation.3 | async-start | bytes 786432 | tf_op jit(solution)/shard_map/psum | solution.py:89
  44.1 43.7 %copy-start.1 = (bf16[64,96]{1,0:T(8,128)(2,1)S(1)}, bf16[64,96]{1,0:T(8,128)(2,1)}, u32[]{:S(2)}) copy-start(bf16[64,96]{1,0:T(8,128)(2,1)} %param.27) | copy-start | bytes 36868
  87.0 0.7 copy-start
  87.8 232.8 %reduce-scatter.10.cloned.1.call-start = ((), (), s32[]{:S(2)}) async-start(), calls=%async_computation.6 | async-start | bytes 835584
  251.3 172.9 %reduce-scatter.8.cloned.1.call-start = ((), (), s32[]{:S(2)}) async-start(), calls=%async_computation.5 | async-start | bytes 5013504 | tf_op jit(solution)/shard_map/reduce_scatter | solution.py:142
  252.0 272.0 %reduce-scatter.6.cloned.1.call-start = ((), (), s32[]{:S(2)}) async-start(), calls=%async_computation.4 | async-start | bytes 5013504 | tf_op jit(solution)/shard_map/reduce_scatter | solution.py:141
Sparse Core Ops, SparseCore 0:
  87.9 127.3 all-reduce.4
  251.4 69.1 reduce-scatter.9
  324.3 99.8 reduce-scatter.7
  427.6 96.3 reduce-scatter.5
where the time goes:
time: 534 us; the launch traced here: 532 us
  waiting for transfers between devices  375 us (70%)
  blocking collectives  70.8 us (13%)
  local copies, waits for them, and re-layouts  35.3 us (7%)
  matrix products  16.5 us (3%)
  between operations  14.6 us (3%)
  loops' own time  13.1 us (2%)
  other arithmetic  6.88 us (1%)
    psum x1, waiting for transfers between devices, shards(): full_rows = lax.psum(mixed_part, 'patch')  107 us
    reduce_scatter x1, waiting for transfers between devices, shards(): lax.psum_scatter(value_all, 'latent', scatter_dimension=0, tiled=True)  102 us
    reduce_scatter x1, waiting for transfers between devices, shards(): lax.psum_scatter(key_all, 'latent', scatter_dimension=0, tiled=True)  98.2 us
    unnamed x5, waiting for transfers between devices  67.7 us
    unnamed x1, blocking collectives  28.4 us
    all_gather x1, blocking collectives, shards(): lax.all_gather(queries, 'patch', axis=1, tiled=True)  22.3 us
    all_gather x1, blocking collectives, shards(): lax.all_gather(grad_out, 'patch', axis=1, tiled=True)  20 us
  transfers between devices with their start and end apart: 4, of which 4 were waited for; matrix products, arithmetic and copies ran while one was open for 1% of the time, Pallas kernels for 0%

commit v1 on v0

v1 whole, which is shorter than its diff:
```python
import jax
import jax.numpy as jnp
from jax import lax
from jax.experimental import pallas as pl
from jax.experimental.pallas import tpu as pltpu
from jax.sharding import Mesh, PartitionSpec as P

BLOCK = 128
D = 1536
TILES = 768
ROWS = 64
FEAT = 96
NB = 6
WIDE = 256
PATCH = ("zlo", "x", "core")
LATENT = ("zhi", "y")
SCALE = D ** (-0.5)
F32 = jnp.float32
BF16 = jnp.bfloat16
NT = (((1,), (1,)), ((), ()))
TN = (((0,), (0,)), ((), ()))
MIB = 1024 * 1024


def iota(shape, dim):
    return lax.broadcasted_iota(jnp.int32, shape, dim)


def pack_kernel(list_ref, bias_ref, q_ref, g_ref, out_ref):
    lane = iota((1, 128), 1)
    mask = jnp.zeros((1, 128), F32)
    for i in range(list_ref.shape[1]):
        mask = jnp.where(lane == list_ref[0, i], 1.0, mask)
    bias = jnp.zeros((1, 128), F32)
    for i in range(16):
        bias = jnp.where(lane == i, bias_ref[0, i], bias)
    high = bias.astype(BF16).astype(F32)
    middle = (bias - high).astype(BF16).astype(F32)
    last = bias - high - middle
    row = iota((16, 128), 0)
    meta = jnp.where(row == 0, mask, jnp.where(row == 1, high, jnp.where(row == 2, middle, jnp.where(row == 3, last, 0.0))))
    meta = meta.astype(BF16)
    for to in range(8):
        out_ref[to, 0:64, 0:96] = q_ref[...]
        out_ref[to, 64:128, 0:96] = g_ref[...]
        out_ref[to, 128:144, :] = meta


def turn_kernel(got_ref, q_ref, g_ref):
    for zlo in range(2):
        rows = pl.ds(zlo * FEAT, FEAT)
        for pair in range(2):
            lanes = pl.ds(pair * 128, 128)
            first, second = (pair * 2) * 2 + zlo, (pair * 2 + 1) * 2 + zlo
            for begin, ref in ((0, q_ref), (64, g_ref)):
                both = jnp.concatenate([got_ref[first, begin : begin + 64, :], got_ref[second, begin : begin + 64, :]], axis=0)
                ref[rows, lanes] = both.T[:FEAT, :]
    for zhi in range(4):
        q_ref[192 + 16 * zhi : 208 + 16 * zhi, 0:128] = got_ref[zhi * 2, 128:144, :]


def load(refs, full_ref, sems, place):
    by_slot = [[], [], [], []]
    for source in range(8):
        for inner in range(4):
            for zlo in range(2):
                slot, row = place(source, inner, zlo)
                copy = pltpu.make_async_copy(
                    refs[source].at[inner, pl.ds(zlo * FEAT, FEAT)],
                    full_ref.at[slot, pl.ds(pl.multiple_of(row, 32), FEAT)],
                    sems.at[source * 8 + inner * 2 + zlo],
                )
                copy.start()
                by_slot[slot].append(copy)
    return by_slot


def score_kernel(ids_ref, *refs):
    q_refs, (meta_ref, key_ref, hot_ref, e_ref, stat_ref, mine_ref, full_ref, sems) = refs[:8], refs[8:]
    x, y, core, latent = ids_ref[0], ids_ref[1], ids_ref[2], ids_ref[3]

    def place(source, inner, zlo):
        at = lax.rem(x + 4 - source % 4, 4)
        side = core if source < 4 else 1 - core
        return inner, ((zlo * 4 + at) * 2 + side) * FEAT

    slots = load(q_refs, full_ref, sems, place)
    group = iota((1, WIDE), 1) // ROWS
    for k in range(4):
        for copy in slots[k]:
            copy.wait()
        at = lax.rem(y + 4 - k, 4)
        parts = []
        for kind in range(4):
            height = 96 if kind == 0 else 16
            part = jnp.zeros((height, WIDE), F32)
            for zhi in range(4):
                column = meta_ref[k, 16 * zhi : 16 * zhi + 16, 0:128].astype(F32).T[:height, kind : kind + 1]
                part = jnp.where(group == zhi, column, part)
            parts.append((part - 1.0) * 1e30 if kind == 0 else part)
        table = jnp.concatenate(parts, axis=0).astype(BF16)
        s = jnp.dot(key_ref[...], full_ref[k], preferred_element_type=F32) * SCALE
        s = s + jnp.dot(hot_ref[...], table, preferred_element_type=F32)
        top = jnp.max(s, axis=0, keepdims=True)
        e = jnp.where(s > -1e29, jnp.exp(s - top), 0.0)
        e_ref[at] = e
        stat_ref[pl.ds(at, 1), :] = top
        stat_ref[pl.ds(4 + at, 1), :] = jnp.sum(e, axis=0, keepdims=True)
        mine_ref[at] = full_ref[k, pl.ds(pl.multiple_of(latent * FEAT, 32), FEAT), :]


def dweight_kernel(ids_ref, *refs):
    g_refs, (value_ref, dw_ref, mine_ref, full_ref, sems) = refs[:8], refs[8:]
    x, y, core, latent = ids_ref[0], ids_ref[1], ids_ref[2], ids_ref[3]

    def place(source, inner, zlo):
        at = lax.rem(x + 4 - inner, 4)
        side = core if source < 4 else 1 - core
        return source % 4, ((zlo * 4 + at) * 2 + side) * FEAT

    slots = load(g_refs, full_ref, sems, place)
    for k in range(4):
        for copy in slots[k]:
            copy.wait()
        at = lax.rem(y + 4 - k, 4)
        dw_ref[at] = jnp.dot(value_ref[...], full_ref[k], preferred_element_type=F32)
        mine_ref[at] = full_ref[k, pl.ds(pl.multiple_of(latent * FEAT, 32), FEAT), :]


def delta_kernel(e_ref, dw_ref, stat_ref, all_ref, delta_ref, factor_ref, low_ref):
    tops = all_ref[:, 0:4, :]
    peak = jnp.max(tops, axis=0)
    whole = jnp.sum(all_ref[:, 4:8, :] * jnp.exp(tops - peak[None]), axis=0)
    factor_ref[...] = jnp.exp(stat_ref[0:4, :] - peak) / whole

    def body(k, _):
        low = (e_ref[k] * factor_ref[pl.ds(k, 1), :]).astype(BF16)
        low_ref[k] = low
        delta_ref[pl.ds(k, 1), :] = jnp.sum(low.astype(F32) * dw_ref[k], axis=0, keepdims=True)
        return 0

    lax.fori_loop(0, 4, body, 0)


def own_rows(ids_ref, values_ref, other_ref):
    y, zhi = ids_ref[1], ids_ref[4]
    lanes = pl.ds(pl.multiple_of(lax.div(zhi, 2) * 128, 128), 128)
    both = lax.dot_general(values_ref[y, :, lanes], other_ref[...], TN, preferred_element_type=F32)
    return jnp.where(lax.rem(zhi, 2) == 1, both[ROWS:], both[:ROWS])


def mixed_kernel(ids_ref, low_ref, value_ref, mine_ref, mixed_ref, gv_ref):
    mixed_ref[...] = own_rows(ids_ref, low_ref, value_ref)
    total = jnp.zeros((FEAT, TILES), F32)
    for k in range(4):
        total = total + lax.dot_general(mine_ref[k], low_ref[k], NT, preferred_element_type=F32)
    gv_ref[...] = total.astype(BF16)


def back_kernel(ids_ref, e_ref, dw_ref, factor_ref, deltas_ref, key_ref, mixed_ref, terms_ref, ds_ref):
    delta = jnp.sum(deltas_ref[...], axis=0)
    for k in range(4):
        w = e_ref[k] * factor_ref[k : k + 1, :]
        ds_ref[k] = (w * (dw_ref[k] - delta[k : k + 1, :])).astype(BF16)
    grads = own_rows(ids_ref, ds_ref, key_ref) * SCALE
    terms_ref[...] = jnp.concatenate([mixed_ref[...], grads], axis=0).T


def grad_key_kernel(mine_ref, ds_ref, gk_ref):
    total = jnp.zeros((FEAT, TILES), F32)
    for k in range(4):
        total = total + lax.dot_general(mine_ref[k], ds_ref[k], NT, preferred_element_type=F32)
    gk_ref[...] = (total * SCALE).astype(BF16)


def last_kernel(terms_ref, attended_ref, gq_ref):
    both = jnp.sum(terms_ref[...], axis=0).T
    attended_ref[...] = both[:ROWS].astype(BF16)
    gq_ref[...] = both[ROWS:].astype(BF16)


def call(kernel, outs, ins, scratch=(), flops=0, moved=0, limit=16):
    vmem = pl.BlockSpec(memory_space=pltpu.VMEM)
    places = {
        "v": vmem,
        "s": pl.BlockSpec(memory_space=pltpu.SMEM),
        "a": pl.BlockSpec(memory_space=pl.ANY),
    }
    return pl.pallas_call(
        kernel,
        out_shape=[jax.ShapeDtypeStruct(shape, kind) for shape, kind in outs],
        in_specs=[places[c] for c in ins],
        out_specs=[vmem] * len(outs),
        scratch_shapes=list(scratch),
        compiler_params=pltpu.CompilerParams(vmem_limit_bytes=limit * MIB),
        cost_estimate=pl.CostEstimate(flops=flops, bytes_accessed=moved, transcendentals=0),
    )


def around(value, axis):
    return [value] + [lax.ppermute(value, axis, [(i, (i + k) % 4) for i in range(4)]) for k in (1, 2, 3)]


def swap(value):
    return lax.ppermute(value, "core", [(0, 1), (1, 0)])


def spread(value, axis, size):
    return lax.all_to_all(jnp.broadcast_to(value[None], (size,) + value.shape), axis, 0, 0)


def shards(queries, tile_keys, tile_values, region_ids, block_list, region_bias, grad_out):
    patch = lax.axis_index(PATCH)
    ids = jnp.stack([lax.axis_index(n) for n in ("x", "y", "core")] + [lax.axis_index(LATENT), lax.axis_index("zhi")])
    ids = ids.astype(jnp.int32)

    packed = call(pack_kernel, [((8, 144, 128), BF16)], "ssvv")(block_list, region_bias, queries, grad_out)[0]
    got = lax.all_to_all(packed, ("zhi", "zlo"), 0, 0)
    q_block, g_block = call(turn_kernel, [((256, WIDE), BF16), ((192, WIDE), BF16)], "v")(got)

    q_row = jnp.stack(around(q_block, "y"))
    g_row = jnp.stack(around(g_block, "x"))
    q_all = around(q_row[:, :192], "x")
    g_all = around(g_row, "y")
    q_all = q_all + [swap(part) for part in q_all]
    g_all = g_all + [swap(part) for part in g_all]

    labels = jnp.arange(144, dtype=jnp.int32)[None, :]
    block_at = patch * NB + jnp.arange(TILES, dtype=jnp.int32)[:, None] // BLOCK
    hot = (labels == block_at) | ((labels >= 96) & (labels % 16 == region_ids[:, None]))
    hot = hot.astype(BF16)

    wide = (4, TILES, WIDE)
    full = [pltpu.VMEM((4, D, WIDE), BF16), pltpu.SemaphoreType.DMA((64,))]
    flops = 2 * TILES * 1024 * D
    e, stat, q_mine = call(
        score_kernel,
        [(wide, F32), ((8, WIDE), F32), ((4, FEAT, WIDE), BF16)],
        "s" + "a" * 8 + "vvv",
        full,
        flops,
        10_000_000,
        24,
    )(ids, *q_all, q_row[:, 192:], tile_keys, hot)
    stats = spread(stat, PATCH, 16)
    dw, g_mine = call(
        dweight_kernel,
        [(wide, F32), ((4, FEAT, WIDE), BF16)],
        "s" + "a" * 8 + "v",
        full,
        flops,
        10_000_000,
        24,
    )(ids, *g_all, tile_values)
    delta, factor, low = call(
        delta_kernel, [((4, WIDE), F32), ((4, WIDE), F32), (wide, BF16)], "vvvv", (), 4 * TILES * 1024, 8_000_000
    )(e, dw, stat, stats)
    deltas = spread(delta, PATCH, 16)
    mixed, grad_values = call(
        mixed_kernel,
        [((ROWS, D), F32), ((FEAT, TILES), BF16)],
        "svvv",
        (),
        2 * TILES * 1024 * FEAT,
        5_000_000,
    )(ids, low, tile_values, g_mine)
    terms, ds = call(
        back_kernel, [((D, 128), F32), (wide, BF16)], "svvvvvv", (), 4 * TILES * 128 * D, 10_000_000
    )(ids, e, dw, factor, deltas, tile_keys, mixed)
    sums = lax.all_to_all(terms.reshape(16, FEAT, 128), PATCH, 0, 0)
    (grad_keys,) = call(
        grad_key_kernel, [((FEAT, TILES), BF16)], "vv", (), 2 * TILES * 1024 * FEAT, 2_000_000
    )(q_mine, ds)
    attended, grad_queries = call(last_kernel, [((ROWS, FEAT), BF16)] * 2, "v")(sums)
    return (attended, grad_queries, grad_keys, grad_values)


def solution(mesh):
    fine = Mesh(mesh.devices.reshape(2, 4, 2, 4, 4), PATCH + LATENT)
    in_specs = (
        P(LATENT, PATCH),
        P(PATCH, None),
        P(PATCH, None),
        P(PATCH),
        P(LATENT, None),
        P(LATENT, None),
        P(LATENT, PATCH),
    )
    out_specs = (P(LATENT, PATCH),) * 4
    return jax.shard_map(shards, mesh=fine, in_specs=in_specs, out_specs=out_specs, check_vma=False)
```

time: 534 us -> 153 us (0.29)
  waiting for transfers between devices: 375 us -> 24.3 us
  blocking collectives: 70.8 us -> 19.7 us
  starting transfers between devices: 0.16 us -> 38.6 us
  Pallas kernels: 0 us -> 27.8 us
  matrix products: 16.5 us -> 0 us
  between operations: 14.6 us -> 0.89 us
  loops' own time: 13.1 us -> 0 us
    reduce_scatter x2 -> x0, waiting for transfers between devices: 200 us -> none  [the longest x1 102 us: shards(): lax.psum_scatter(value_all, 'latent', scatter_dimension=0, tiled=True)]
    psum x1 -> x0, waiting for transfers between devices: 107 us -> none  [shards(): full_rows = lax.psum(mixed_part, 'patch')]
    unnamed x5 -> x0, waiting for transfers between devices: 67.7 us -> none
    all_gather x2 -> x0, blocking collectives: 42.3 us -> none  [the longest x1 22.3 us: shards(): lax.all_gather(queries, 'patch', axis=1, tiled=True)]
    unnamed x15 -> x74, local copies, waits for them, and re-layouts: 4.95 us -> 34.9 us
    unnamed x1 -> x0, blocking collectives: 28.4 us -> none
    pallas_call x0 -> x9, Pallas kernels: none -> 27.8 us  [the longest x1 11.9 us: shards(): call(score_kernel, [(wide, F32), ((8, WIDE), F32), ((4, FEAT, WIDE), BF16...]
    ppermute x0 -> x20, starting transfers between devices: none -> 23.1 us  [the longest x12 16.6 us: around(): lax.ppermute(value, axis, [(i, (i + k) % 4) for i in range(4)])]
  transfers between devices with their start and end apart: 4 -> 23, of which waited for: 4 -> 5; matrix products, arithmetic and copies ran while one was open for 1% -> 2% of each run, Pallas kernels for 0% -> 16%
where the time goes in v1:
time: 153 us; the launch traced here: 150 us
  starting transfers between devices  38.6 us (25%)
  local copies, waits for them, and re-layouts  36.3 us (24%)
  Pallas kernels  27.8 us (18%)
  waiting for transfers between devices  24.3 us (16%)
  blocking collectives  19.7 us (13%)
  other arithmetic  2.7 us (2%)
    unnamed x74, local copies, waits for them, and re-layouts  34.9 us
    all_to_all x1, blocking collectives, shards(): got = lax.all_to_all(packed, ('zhi', 'zlo'), 0, 0)  19.7 us
    ppermute x12, starting transfers between devices, around(): lax.ppermute(value, axis, [(i, (i + k) % 4) for i in range(4)])  16.6 us
    ppermute x12, waiting for transfers between devices, around(): lax.ppermute(value, axis, [(i, (i + k) % 4) for i in range(4)])  13.5 us
    pallas_call x1, Pallas kernels, shards(): call(score_kernel, [(wide, F32), ((8, WIDE), F32), ((4, FEAT, WIDE), BF16...  11.9 us
    all_to_all x1, waiting for transfers between devices, shards(): sums = lax.all_to_all(terms.reshape(16, FEAT, 128), PATCH, 0, 0)  10.8 us
    all_to_all x2, starting transfers between devices, spread(): lax.all_to_all(jnp.broadcast_to(value[None], (size,) + value.shape), axis...  9.58 us
    pallas_call x1, Pallas kernels, shards(): call(dweight_kernel, [(wide, F32), ((4, FEAT, WIDE), BF16)], 's' + 'a' *...  8.14 us
  transfers between devices with their start and end apart: 23, of which 5 were waited for; matrix products, arithmetic and copies ran while one was open for 2% of the time, Pallas kernels for 16%

profile of v1, /device:TPU:1, one launch (start us, length us, event | category | flops | bytes accessed | tf_op | source)
XLA Modules:
  0.0 150.3 jit_solution(8647144533880162494)
XLA Ops:
  4.0 19.7 %all_to_all.20.got_ref = bf16[8,144,128]{2,1,0:T(8,128)(2,1)S(1)} all-to-all(bf16[8,144,128]{2,1,0:T(8,128)(2,1)S(1)} %shard_map.102), channel_id=1, replica_groups=mesh['zlo'=2,'x'=4,'core'=2,'zhi'=4,'y'=4] {'zhi','zlo'}, dimensions={0} | all-to-all | bytes 589824 | tf_op jit(solution)/shard_map/all_to_all | solution.py:218
  23.8 2.6 %collective-permute-start.12 = (bf16[192,256]{1,0:T(8,128)(2,1)S(1)}, bf16[192,256]{1,0:T(8,128)(2,1)S(1)}, u32[]{:S(2)}, u32[]{:S(2)}) collective-permute-start(bf16[192,256]{1,0:T(8,128)(2,1)S(1)} %get-tuple-element.22), channel_id=1, source_target_pairs={{0,96},{32,0},{64,32},{96,64},{1,97},{33,1},{65,33},{97,65},{2,98}... | collective-permute-start | bytes 294920 | tf_op jit(solution)/shard_map/ppermute | solution.py:201
  27.5 2.7 %collective-permute-start.2 = (bf16[256,256]{1,0:T(8,128)(2,1)S(1)}, bf16[256,256]{1,0:T(8,128)(2,1)S(1)}, u32[]{:S(2)}, u32[]{:S(2)}) collective-permute-start(bf16[256,256]{1,0:T(8,128)(2,1)S(1)} %get-tuple-element.20), channel_id=1, source_target_pairs={{0,3},{1,0},{2,1},{3,2},{4,7},{5,4},{6,5},{7,6},{8,11},{9,8},{10,9... | collective-permute-start | bytes 393224 | tf_op jit(solution)/shard_map/ppermute | solution.py:201
  31.4 1.0 collective-permute-done.10
  32.4 0.8 pad_maximum_fusion.1.refs_0_
  33.2 1.3 collective-permute-start.13
  34.5 2.6 %collective-permute-start.14 = (bf16[4,192,256]{2,1,0:T(8,128)(2,1)}, bf16[4,192,256]{2,1,0:T(8,128)(2,1)}, u32[]{:S(2)}, u32[]{:S(2)}) collective-permute-start(bf16[4,192,256]{2,1,0:T(8,128)(2,1)} %pad_maximum_fusion.1.refs_0_), channel_id=1, source_target_pairs={{0,2},{1,3},{2,0},{3,1},{4,6},{5,7},{6,4},{7,5},{8,10},{9,11},{10,... | collective-permute-start | bytes 1179656 | tf_op jit(solution)/shard_map/ppermute | solution.py:201
  37.8 1.3 collective-permute-start.3
  39.1 1.7 %collective-permute-start.4 = (bf16[4,192,256]{2,1,0:T(8,128)(2,1)S(1)}, bf16[4,192,256]{2,1,0:T(8,128)(2,1)S(1)}, u32[]{:S(2)}, u32[]{:S(2)}) collective-permute-start(bf16[4,192,256]{2,1,0:T(8,128)(2,1)S(1)} %slice.8.refs_0_), channel_id=1, source_target_pairs={{0,64},{32,96},{64,0},{96,32},{1,65},{33,97},{65,1},{97,33},{2,66}... | collective-permute-start | bytes 1179656 | tf_op jit(solution)/shard_map/ppermute | solution.py:201
  41.5 4.3 %collective-permute-done.13.refs_1_ = bf16[4,192,256]{2,1,0:T(8,128)(2,1)} collective-permute-done((bf16[4,192,256]{2,1,0:T(8,128)(2,1)}, bf16[4,192,256]{2,1,0:T(8,128)(2,1)}, u32[]{:S(2)}, u32[]{:S(2)}) %collective-permute-start.13) | collective-permute-done | bytes 393248 | tf_op jit(solution)/shard_map/ppermute | solution.py:201
  45.7 1.5 collective-permute-start.15
  47.2 8.1 %collective-permute-done.14.refs_2_ = bf16[4,192,256]{2,1,0:T(8,128)(2,1)} collective-permute-done((bf16[4,192,256]{2,1,0:T(8,128)(2,1)}, bf16[4,192,256]{2,1,0:T(8,128)(2,1)}, u32[]{:S(2)}, u32[]{:S(2)}) %collective-permute-start.14) | collective-permute-done | bytes 393248 | tf_op jit(solution)/shard_map/ppermute | solution.py:201
  55.4 3.3 %collective-permute-start.6 = (bf16[4,192,256]{2,1,0:T(8,128)(2,1)S(1)}, bf16[4,192,256]{2,1,0:T(8,128)(2,1)S(1)}, u32[]{:S(2)}, u32[]{:S(2)}) collective-permute-start(bf16[4,192,256]{2,1,0:T(8,128)(2,1)S(1)} %slice.8.refs_0_), channel_id=1, source_target_pairs={{0,16},{16,0},{1,17},{17,1},{2,18},{18,2},{3,19},{19,3},{4,20},{20... | collective-permute-start | bytes 1179656 | tf_op jit(solution)/shard_map/ppermute | solution.py:205
  58.8 2.0 %collective-permute-start.8 = (bf16[4,192,256]{2,1,0:T(8,128)(2,1)S(1)}, bf16[4,192,256]{2,1,0:T(8,128)(2,1)S(1)}, u32[]{:S(2)}, u32[]{:S(2)}) collective-permute-start(bf16[4,192,256]{2,1,0:T(8,128)(2,1)S(1)} %collective-permute-done.4.refs_2_), channel_id=1, source_target_pairs={{0,16},{16,0},{1,17},{17,1},{2,18},{18,2},{3,19},{19,3},{4,20},{20... | collective-permute-start | bytes 1179656 | tf_op jit(solution)/shard_map/ppermute | solution.py:205
  62.2 0.8 copy-done.27
  64.2 0.8 copy-done.31
  65.0 1.0 fusion.1.refs_10_
  66.1 0.8 pad_maximum_fusion.2.refs_8_
  67.7 1.7 %copy-done.5 = bf16[768,1536]{1,0:T(8,128)(2,1)S(1)} copy-done((bf16[768,1536]{1,0:T(8,128)(2,1)S(1)}, bf16[768,1536]{1,0:T(8,128)(2,1)}, u32[]{:S(2)}) %copy-start.5) | copy-done | bytes 2359320
  69.3 1.0 copy-done.12
  70.3 1.0 copy-done.22
  71.3 1.0 copy-done.24
  72.3 1.0 copy-done.26
  73.3 1.0 copy-done.28
  74.3 1.0 copy-done.30
  75.3 1.0 copy-done.32
  76.3 1.0 copy-done.34
  77.3 11.9 %shard_map.104 = (f32[4,768,256]{2,1,0:T(8,128)S(1)}, f32[8,256]{1,0:T(8,128)S(1)}, bf16[4,96,256]{2,1,0:T(8,128)(2,1)S(1)}) custom-call(s32[5]{0:T(128)S(1)} %stack.53.ids_ref, bf16[4,192,256]{2,1,0:T(8,128)(2,1)S(1)} %slice.8.refs_0_, bf16[4,192,256]{2,1,0:T(8,128)(2,1)S(1)} %copy-done.22, bf16[4,192,256]{2,1,0:T(8,128)(2,1)S(1)} %copy-done.24, ...), custom_call_target="tpu_custom_call" | custom-call | flops 2415919104 | bytes 10000000 | tf_op jit(solution)/shard_map/pallas_call | solution.py:236
  90.6 3.8 %all-to-all-start.1 = ((f32[16,8,256]{2,1,0:T(8,128)}), f32[16,8,256]{2,1,0:T(8,128)S(1)}, u32[]{:S(2)}, u32[]{:S(2)}) async-start(f32[16,8,256]{2,1,0:T(8,128)} %broadcast_in_dim.4), calls=%async_computation.1 | async-start | bytes 262144 | tf_op jit(solution)/shard_map/all_to_all | solution.py:209
  94.4 1.7 %copy-done.3 = bf16[768,1536]{1,0:T(8,128)(2,1)S(1)} copy-done((bf16[768,1536]{1,0:T(8,128)(2,1)S(1)}, bf16[768,1536]{1,0:T(8,128)(2,1)}, u32[]{:S(2)}) %copy-start.3) | copy-done | bytes 2359320
  96.1 8.1 %shard_map.105 = (f32[4,768,256]{2,1,0:T(8,128)S(1)}, bf16[4,96,256]{2,1,0:T(8,128)(2,1)S(1)}) custom-call(s32[5]{0:T(128)S(1)} %stack.53.ids_ref, bf16[4,192,256]{2,1,0:T(8,128)(2,1)} %pad_maximum_fusion.1.refs_0_, bf16[4,192,256]{2,1,0:T(8,128)(2,1)} %collective-permute-done.13.refs_1_, bf16[4,192,256]{2,1,0:T(8,128)(2,1)} %collective-permute-done.14.refs_2_, ...), custom_call_target="tpu_custom_call" | custom-call | flops 2415919104 | bytes 10000000 | tf_op jit(solution)/shard_map/pallas_call | solution.py:246
  104.2 1.6 %copy-done = f32[4,768,256]{2,1,0:T(8,128)} copy-done((f32[4,768,256]{2,1,0:T(8,128)}, f32[4,768,256]{2,1,0:T(8,128)S(1)}, u32[]{:S(2)}) %copy-start) | copy-done | bytes 3145752
  106.5 1.9 %copy-done.1 = f32[4,768,256]{2,1,0:T(8,128)S(1)} copy-done((f32[4,768,256]{2,1,0:T(8,128)S(1)}, f32[4,768,256]{2,1,0:T(8,128)}, u32[]{:S(2)}) %copy-start.1) | copy-done | bytes 3145752
  109.1 1.2 copy-done.7
  110.9 5.8 %all-to-all-start.2 = ((f32[16,4,256]{2,1,0:T(4,128)}), f32[16,4,256]{2,1,0:T(4,128)}, u32[]{:S(2)}, u32[]{:S(2)}) async-start(f32[16,4,256]{2,1,0:T(4,128)} %broadcast_in_dim.5), calls=%async_computation.2 | async-start | bytes 131072 | tf_op jit(solution)/shard_map/all_to_all | solution.py:209
  116.7 1.7 %copy-done.4 = bf16[768,1536]{1,0:T(8,128)(2,1)S(1)} copy-done((bf16[768,1536]{1,0:T(8,128)(2,1)S(1)}, bf16[768,1536]{1,0:T(8,128)(2,1)}, u32[]{:S(2)}) %copy-start.4) | copy-done | bytes 2359320
  118.3 1.4 copy-done.8
  119.7 0.9 copy-done.14
  120.7 2.2 %shard_map.107 = (f32[64,1536]{1,0:T(8,128)S(1)}, bf16[96,768]{1,0:T(8,128)(2,1)}) custom-call(s32[5]{0:T(128)S(1)} %stack.53.ids_ref, bf16[4,768,256]{2,1,0:T(8,128)(2,1)S(1)} %copy-done.8, bf16[768,1536]{1,0:T(8,128)(2,1)S(1)} %copy-done.4, bf16[4,96,256]{2,1,0:T(8,128)(2,1)S(1)} %copy-done.14), custom_call_target="tpu_custom_call" | custom-call | flops 150994944 | bytes 5000000 | tf_op jit(solution)/shard_map/pallas_call | solution.py:259
  122.8 1.9 %copy-done.2 = f32[4,768,256]{2,1,0:T(8,128)S(1)} copy-done((f32[4,768,256]{2,1,0:T(8,128)S(1)}, f32[4,768,256]{2,1,0:T(8,128)}, u32[]{:S(2)}) %copy-start.2) | copy-done | bytes 3145752
  124.7 1.7 %copy-done.6 = bf16[768,1536]{1,0:T(8,128)(2,1)S(1)} copy-done((bf16[768,1536]{1,0:T(8,128)(2,1)S(1)}, bf16[768,1536]{1,0:T(8,128)(2,1)}, u32[]{:S(2)}) %copy-start.6) | copy-done | bytes 2359320
  126.4 2.3 %shard_map.108 = (f32[1536,128]{1,0:T(8,128)S(1)}, bf16[4,768,256]{2,1,0:T(8,128)(2,1)S(1)}) custom-call(s32[5]{0:T(128)S(1)} %stack.53.ids_ref, f32[4,768,256]{2,1,0:T(8,128)S(1)} %get-tuple-element.21.e_ref, f32[4,768,256]{2,1,0:T(8,128)S(1)} %copy-done.2, f32[4,256]{1,0:T(4,128)S(1)} %get-tuple-element.25.factor_ref, ...), custom_call_target="tpu_custom_call" | custom-call | flops 603979776 | bytes 10000000 | tf_op jit(solution)/shard_map/pallas_call | solution.py:267
  128.7 1.2 copy-done.9
  129.9 0.9 copy-done.11
  130.7 5.9 %all-to-all-start.3 = ((f32[16,96,128]{2,1,0:T(8,128)}), f32[16,96,128]{2,1,0:T(8,128)S(1)}, u32[]{:S(2)}, u32[]{:S(2)}) async-start(f32[16,96,128]{2,1,0:T(8,128)} %bitcast.14), calls=%async_computation.3 | async-start | bytes 1572864 | tf_op jit(solution)/shard_map/all_to_all | solution.py:270
  136.6 0.9 copy-done.16
  137.5 1.3 shard_map.110
  138.8 10.8 %all-to-all-done.3.terms_ref = f32[16,96,128]{2,1,0:T(8,128)S(1)} async-done(((f32[16,96,128]{2,1,0:T(8,128)}), f32[16,96,128]{2,1,0:T(8,128)S(1)}, u32[]{:S(2)}, u32[]{:S(2)}) %all-to-all-start.3) | async-done | bytes 786464 | tf_op jit(solution)/shard_map/all_to_all | solution.py:270
  (93 shorter events, 14.8 us)
Async XLA Ops:
  3.4 61.6 %copy-start.36 = (s32[768]{0:T(1024)S(1)}, s32[768]{0:T(1024)}, u32[]{:S(2)}) copy-start(s32[768]{0:T(1024)} %param.10) | copy-start | bytes 9220
  23.8 6.8 %collective-permute-start.12 = (bf16[192,256]{1,0:T(8,128)(2,1)S(1)}, bf16[192,256]{1,0:T(8,128)(2,1)S(1)}, u32[]{:S(2)}, u32[]{:S(2)}) collective-permute-start(bf16[192,256]{1,0:T(8,128)(2,1)S(1)} %get-tuple-element.22), channel_id=1, source_target_pairs={{0,96},{32,0},{64,32},{96,64},{1,97},{33,1},{65,33},{97,65},{2,98}... | collective-permute-start | bytes 294920 | tf_op jit(solution)/shard_map/ppermute | solution.py:201
  26.3 5.1 %collective-permute-start.11 = (bf16[192,256]{1,0:T(8,128)(2,1)S(1)}, bf16[192,256]{1,0:T(8,128)(2,1)S(1)}, u32[]{:S(2)}, u32[]{:S(2)}) collective-permute-start(bf16[192,256]{1,0:T(8,128)(2,1)S(1)} %get-tuple-element.22), channel_id=1, source_target_pairs={{0,64},{32,96},{64,0},{96,32},{1,65},{33,97},{65,1},{97,33},{2,66}... | collective-permute-start | bytes 294920 | tf_op jit(solution)/shard_map/ppermute | solution.py:201
  26.8 5.5 %collective-permute-start.10 = (bf16[192,256]{1,0:T(8,128)(2,1)S(1)}, bf16[192,256]{1,0:T(8,128)(2,1)S(1)}, u32[]{:S(2)}, u32[]{:S(2)}) collective-permute-start(bf16[192,256]{1,0:T(8,128)(2,1)S(1)} %get-tuple-element.22), channel_id=1, source_target_pairs={{0,32},{32,64},{64,96},{96,0},{1,33},{33,65},{65,97},{97,1},{2,34}... | collective-permute-start | bytes 294920 | tf_op jit(solution)/shard_map/ppermute | solution.py:201
  27.5 9.6 %collective-permute-start.2 = (bf16[256,256]{1,0:T(8,128)(2,1)S(1)}, bf16[256,256]{1,0:T(8,128)(2,1)S(1)}, u32[]{:S(2)}, u32[]{:S(2)}) collective-permute-start(bf16[256,256]{1,0:T(8,128)(2,1)S(1)} %get-tuple-element.20), channel_id=1, source_target_pairs={{0,3},{1,0},{2,1},{3,2},{4,7},{5,4},{6,5},{7,6},{8,11},{9,8},{10,9... | collective-permute-start | bytes 393224 | tf_op jit(solution)/shard_map/ppermute | solution.py:201
  30.2 6.9 %collective-permute-start.1 = (bf16[256,256]{1,0:T(8,128)(2,1)S(1)}, bf16[256,256]{1,0:T(8,128)(2,1)S(1)}, u32[]{:S(2)}, u32[]{:S(2)}) collective-permute-start(bf16[256,256]{1,0:T(8,128)(2,1)S(1)} %get-tuple-element.20), channel_id=1, source_target_pairs={{0,2},{1,3},{2,0},{3,1},{4,6},{5,7},{6,4},{7,5},{8,10},{9,11},{10,... | collective-permute-start | bytes 393224 | tf_op jit(solution)/shard_map/ppermute | solution.py:201
  30.5 6.6 %collective-permute-start = (bf16[256,256]{1,0:T(8,128)(2,1)S(1)}, bf16[256,256]{1,0:T(8,128)(2,1)S(1)}, u32[]{:S(2)}, u32[]{:S(2)}) collective-permute-start(bf16[256,256]{1,0:T(8,128)(2,1)S(1)} %get-tuple-element.20), channel_id=1, source_target_pairs={{0,1},{1,2},{2,3},{3,0},{4,5},{5,6},{6,7},{7,4},{8,9},{9,10},{10,1... | collective-permute-start | bytes 393224 | tf_op jit(solution)/shard_map/ppermute | solution.py:201
  33.2 12.6 %collective-permute-start.13 = (bf16[4,192,256]{2,1,0:T(8,128)(2,1)}, bf16[4,192,256]{2,1,0:T(8,128)(2,1)}, u32[]{:S(2)}, u32[]{:S(2)}) collective-permute-start(bf16[4,192,256]{2,1,0:T(8,128)(2,1)} %pad_maximum_fusion.1.refs_0_), channel_id=1, source_target_pairs={{0,1},{1,2},{2,3},{3,0},{4,5},{5,6},{6,7},{7,4},{8,9},{9,10},{10,1... | collective-permute-start | bytes 1179656 | tf_op jit(solution)/shard_map/ppermute | solution.py:201
  34.5 20.9 %collective-permute-start.14 = (bf16[4,192,256]{2,1,0:T(8,128)(2,1)}, bf16[4,192,256]{2,1,0:T(8,128)(2,1)}, u32[]{:S(2)}, u32[]{:S(2)}) collective-permute-start(bf16[4,192,256]{2,1,0:T(8,128)(2,1)} %pad_maximum_fusion.1.refs_0_), channel_id=1, source_target_pairs={{0,2},{1,3},{2,0},{3,1},{4,6},{5,7},{6,4},{7,5},{8,10},{9,11},{10,... | collective-permute-start | bytes 1179656 | tf_op jit(solution)/shard_map/ppermute | solution.py:201
  37.8 20.9 %collective-permute-start.3 = (bf16[4,192,256]{2,1,0:T(8,128)(2,1)S(1)}, bf16[4,192,256]{2,1,0:T(8,128)(2,1)S(1)}, u32[]{:S(2)}, u32[]{:S(2)}) collective-permute-start(bf16[4,192,256]{2,1,0:T(8,128)(2,1)S(1)} %slice.8.refs_0_), channel_id=1, source_target_pairs={{0,32},{32,64},{64,96},{96,0},{1,33},{33,65},{65,97},{97,1},{2,34}... | collective-permute-start | bytes 1179656 | tf_op jit(solution)/shard_map/ppermute | solution.py:201
  39.1 19.7 %collective-permute-start.4 = (bf16[4,192,256]{2,1,0:T(8,128)(2,1)S(1)}, bf16[4,192,256]{2,1,0:T(8,128)(2,1)S(1)}, u32[]{:S(2)}, u32[]{:S(2)}) collective-permute-start(bf16[4,192,256]{2,1,0:T(8,128)(2,1)S(1)} %slice.8.refs_0_), channel_id=1, source_target_pairs={{0,64},{32,96},{64,0},{96,32},{1,65},{33,97},{65,1},{97,33},{2,66}... | collective-permute-start | bytes 1179656 | tf_op jit(solution)/shard_map/ppermute | solution.py:201
  40.8 20.0 %collective-permute-start.5 = (bf16[4,192,256]{2,1,0:T(8,128)(2,1)S(1)}, bf16[4,192,256]{2,1,0:T(8,128)(2,1)S(1)}, u32[]{:S(2)}, u32[]{:S(2)}) collective-permute-start(bf16[4,192,256]{2,1,0:T(8,128)(2,1)S(1)} %slice.8.refs_0_), channel_id=1, source_target_pairs={{0,96},{32,0},{64,32},{96,64},{1,97},{33,1},{65,33},{97,65},{2,98}... | collective-permute-start | bytes 1179656 | tf_op jit(solution)/shard_map/ppermute | solution.py:201
  45.7 15.9 %collective-permute-start.15 = (bf16[4,192,256]{2,1,0:T(8,128)(2,1)}, bf16[4,192,256]{2,1,0:T(8,128)(2,1)}, u32[]{:S(2)}, u32[]{:S(2)}) collective-permute-start(bf16[4,192,256]{2,1,0:T(8,128)(2,1)} %pad_maximum_fusion.1.refs_0_), channel_id=1, source_target_pairs={{0,3},{1,0},{2,1},{3,2},{4,7},{5,4},{6,5},{7,6},{8,11},{9,8},{10,9... | collective-permute-start | bytes 1179656 | tf_op jit(solution)/shard_map/ppermute | solution.py:201
  55.4 6.8 %collective-permute-start.6 = (bf16[4,192,256]{2,1,0:T(8,128)(2,1)S(1)}, bf16[4,192,256]{2,1,0:T(8,128)(2,1)S(1)}, u32[]{:S(2)}, u32[]{:S(2)}) collective-permute-start(bf16[4,192,256]{2,1,0:T(8,128)(2,1)S(1)} %slice.8.refs_0_), channel_id=1, source_target_pairs={{0,16},{16,0},{1,17},{17,1},{2,18},{18,2},{3,19},{19,3},{4,20},{20... | collective-permute-start | bytes 1179656 | tf_op jit(solution)/shard_map/ppermute | solution.py:205
  58.7 8.2 %copy-start.21 = (bf16[4,192,256]{2,1,0:T(8,128)(2,1)}, bf16[4,192,256]{2,1,0:T(8,128)(2,1)S(1)}, u32[]{:S(2)}) copy-start(bf16[4,192,256]{2,1,0:T(8,128)(2,1)S(1)} %collective-permute-done.3.refs_1_) | copy-start | bytes 1179652
  58.7 4.2 %collective-permute-start.7 = (bf16[4,192,256]{2,1,0:T(8,128)(2,1)S(1)}, bf16[4,192,256]{2,1,0:T(8,128)(2,1)S(1)}, u32[]{:S(2)}, u32[]{:S(2)}) collective-permute-start(bf16[4,192,256]{2,1,0:T(8,128)(2,1)S(1)} %collective-permute-done.3.refs_1_), channel_id=1, source_target_pairs={{0,16},{16,0},{1,17},{17,1},{2,18},{18,2},{3,19},{19,3},{4,20},{20... | collective-permute-start | bytes 1179656 | tf_op jit(solution)/shard_map/ppermute | solution.py:205
  58.8 8.1 %copy-start.23 = (bf16[4,192,256]{2,1,0:T(8,128)(2,1)}, bf16[4,192,256]{2,1,0:T(8,128)(2,1)S(1)}, u32[]{:S(2)}) copy-start(bf16[4,192,256]{2,1,0:T(8,128)(2,1)S(1)} %collective-permute-done.4.refs_2_) | copy-start | bytes 1179652
  58.8 5.4 %collective-permute-start.8 = (bf16[4,192,256]{2,1,0:T(8,128)(2,1)S(1)}, bf16[4,192,256]{2,1,0:T(8,128)(2,1)S(1)}, u32[]{:S(2)}, u32[]{:S(2)}) collective-permute-start(bf16[4,192,256]{2,1,0:T(8,128)(2,1)S(1)} %collective-permute-done.4.refs_2_), channel_id=1, source_target_pairs={{0,16},{16,0},{1,17},{17,1},{2,18},{18,2},{3,19},{19,3},{4,20},{20... | collective-permute-start | bytes 1179656 | tf_op jit(solution)/shard_map/ppermute | solution.py:205
  60.8 6.1 %collective-permute-start.9 = (bf16[4,192,256]{2,1,0:T(8,128)(2,1)S(1)}, bf16[4,192,256]{2,1,0:T(8,128)(2,1)S(1)}, u32[]{:S(2)}, u32[]{:S(2)}) collective-permute-start(bf16[4,192,256]{2,1,0:T(8,128)(2,1)S(1)} %collective-permute-done.5.refs_3_), channel_id=1, source_target_pairs={{0,16},{16,0},{1,17},{17,1},{2,18},{18,2},{3,19},{19,3},{4,20},{20... | collective-permute-start | bytes 1179656 | tf_op jit(solution)/shard_map/ppermute | solution.py:205
  61.7 32.7 %collective-permute-start.16 = (bf16[4,192,256]{2,1,0:T(8,128)(2,1)}, bf16[4,192,256]{2,1,0:T(8,128)(2,1)}, u32[]{:S(2)}, u32[]{:S(2)}) collective-permute-start(bf16[4,192,256]{2,1,0:T(8,128)(2,1)} %pad_maximum_fusion.1.refs_0_), channel_id=1, source_target_pairs={{0,16},{16,0},{1,17},{17,1},{2,18},{18,2},{3,19},{19,3},{4,20},{20... | collective-permute-start | bytes 1179656 | tf_op jit(solution)/shard_map/ppermute | solution.py:205
  62.9 31.4 %collective-permute-start.17 = (bf16[4,192,256]{2,1,0:T(8,128)(2,1)}, bf16[4,192,256]{2,1,0:T(8,128)(2,1)}, u32[]{:S(2)}, u32[]{:S(2)}) collective-permute-start(bf16[4,192,256]{2,1,0:T(8,128)(2,1)} %collective-permute-done.13.refs_1_), channel_id=1, source_target_pairs={{0,16},{16,0},{1,17},{17,1},{2,18},{18,2},{3,19},{19,3},{4,20},{20... | collective-permute-start | bytes 1179656 | tf_op jit(solution)/shard_map/ppermute | solution.py:205
  63.7 30.7 %collective-permute-start.18 = (bf16[4,192,256]{2,1,0:T(8,128)(2,1)}, bf16[4,192,256]{2,1,0:T(8,128)(2,1)}, u32[]{:S(2)}, u32[]{:S(2)}) collective-permute-start(bf16[4,192,256]{2,1,0:T(8,128)(2,1)} %collective-permute-done.14.refs_2_), channel_id=1, source_target_pairs={{0,16},{16,0},{1,17},{17,1},{2,18},{18,2},{3,19},{19,3},{4,20},{20... | collective-permute-start | bytes 1179656 | tf_op jit(solution)/shard_map/ppermute | solution.py:205
  65.0 29.4 %collective-permute-start.19 = (bf16[4,192,256]{2,1,0:T(8,128)(2,1)}, bf16[4,192,256]{2,1,0:T(8,128)(2,1)}, u32[]{:S(2)}, u32[]{:S(2)}) collective-permute-start(bf16[4,192,256]{2,1,0:T(8,128)(2,1)} %collective-permute-done.15.refs_3_), channel_id=1, source_target_pairs={{0,16},{16,0},{1,17},{17,1},{2,18},{18,2},{3,19},{19,3},{4,20},{20... | collective-permute-start | bytes 1179656 | tf_op jit(solution)/shard_map/ppermute | solution.py:205
  67.7 1.7 %copy-start.5 = (bf16[768,1536]{1,0:T(8,128)(2,1)S(1)}, bf16[768,1536]{1,0:T(8,128)(2,1)}, u32[]{:S(2)}) copy-start(bf16[768,1536]{1,0:T(8,128)(2,1)} %key_ref.1) | copy-start | bytes 7077892
  69.3 1.0 copy-start.12
  70.3 1.0 copy-start.22
  71.3 1.0 copy-start.24
  72.3 1.0 copy-start.26
  73.3 1.0 copy-start.28
  74.3 1.0 copy-start.30
  75.3 1.0 copy-start.32
  76.3 1.0 copy-start.34
  90.6 16.0 %all-to-all-start.1 = ((f32[16,8,256]{2,1,0:T(8,128)}), f32[16,8,256]{2,1,0:T(8,128)S(1)}, u32[]{:S(2)}, u32[]{:S(2)}) async-start(f32[16,8,256]{2,1,0:T(8,128)} %broadcast_in_dim.4), calls=%async_computation.1 | async-start | bytes 262144 | tf_op jit(solution)/shard_map/all_to_all | solution.py:209
  94.4 1.7 %copy-start.3 = (bf16[768,1536]{1,0:T(8,128)(2,1)S(1)}, bf16[768,1536]{1,0:T(8,128)(2,1)}, u32[]{:S(2)}) copy-start(bf16[768,1536]{1,0:T(8,128)(2,1)} %value_ref.1) | copy-start | bytes 7077892
  104.2 1.6 %copy-start = (f32[4,768,256]{2,1,0:T(8,128)}, f32[4,768,256]{2,1,0:T(8,128)S(1)}, u32[]{:S(2)}) copy-start(f32[4,768,256]{2,1,0:T(8,128)S(1)} %get-tuple-element.23.dw_ref) | copy-start | bytes 9437188
  106.5 1.9 %copy-start.1 = (f32[4,768,256]{2,1,0:T(8,128)S(1)}, f32[4,768,256]{2,1,0:T(8,128)}, u32[]{:S(2)}) copy-start(f32[4,768,256]{2,1,0:T(8,128)} %copy-done) | copy-start | bytes 9437188
  109.0 1.2 copy-start.7
  110.9 12.0 %all-to-all-start.2 = ((f32[16,4,256]{2,1,0:T(4,128)}), f32[16,4,256]{2,1,0:T(4,128)}, u32[]{:S(2)}, u32[]{:S(2)}) async-start(f32[16,4,256]{2,1,0:T(4,128)} %broadcast_in_dim.5), calls=%async_computation.2 | async-start | bytes 131072 | tf_op jit(solution)/shard_map/all_to_all | solution.py:209
  116.7 1.7 %copy-start.4 = (bf16[768,1536]{1,0:T(8,128)(2,1)S(1)}, bf16[768,1536]{1,0:T(8,128)(2,1)}, u32[]{:S(2)}) copy-start(bf16[768,1536]{1,0:T(8,128)(2,1)} %value_ref.1) | copy-start | bytes 7077892
  118.3 1.4 copy-start.8
  119.7 0.9 copy-start.14
  122.8 1.9 %copy-start.2 = (f32[4,768,256]{2,1,0:T(8,128)S(1)}, f32[4,768,256]{2,1,0:T(8,128)}, u32[]{:S(2)}) copy-start(f32[4,768,256]{2,1,0:T(8,128)} %copy-done) | copy-start | bytes 9437188
  124.7 1.7 %copy-start.6 = (bf16[768,1536]{1,0:T(8,128)(2,1)S(1)}, bf16[768,1536]{1,0:T(8,128)(2,1)}, u32[]{:S(2)}) copy-start(bf16[768,1536]{1,0:T(8,128)(2,1)} %key_ref.1) | copy-start | bytes 7077892
  128.7 1.2 copy-start.9
  129.9 0.9 copy-start.11
  130.7 5.9 %copy-start.10 = (bf16[4,768,256]{2,1,0:T(8,128)(2,1)S(1)}, bf16[4,768,256]{2,1,0:T(8,128)(2,1)}, u32[]{:S(2)}) copy-start(bf16[4,768,256]{2,1,0:T(8,128)(2,1)} %copy-done.9) | copy-start | bytes 4718596
  130.7 18.8 %all-to-all-start.3 = ((f32[16,96,128]{2,1,0:T(8,128)}), f32[16,96,128]{2,1,0:T(8,128)S(1)}, u32[]{:S(2)}, u32[]{:S(2)}) async-start(f32[16,96,128]{2,1,0:T(8,128)} %bitcast.14), calls=%async_computation.3 | async-start | bytes 1572864 | tf_op jit(solution)/shard_map/all_to_all | solution.py:270
  136.6 0.9 copy-start.16
  (12 other events, 8.6 us)

commit v2 on v1

v2 whole, which is shorter than its diff:
```python
import jax
import jax.numpy as jnp
from jax import lax
from jax.experimental import pallas as pl
from jax.experimental.pallas import tpu as pltpu
from jax.sharding import Mesh, PartitionSpec as P

BLOCK = 128
D = 1536
TILES = 768
ROWS = 64
FEAT = 96
NB = 6
WIDE = 256
PART = 384
HIGH = 400
PATCH = ("zlo", "x", "core")
LATENT = ("zhi", "y")
SCALE = D ** (-0.5)
F32 = jnp.float32
BF16 = jnp.bfloat16
NT = (((1,), (1,)), ((), ()))
TN = (((0,), (0,)), ((), ()))
MIB = 1024 * 1024


def iota(shape, dim):
    return lax.broadcasted_iota(jnp.int32, shape, dim)


def pack_kernel(list_ref, bias_ref, q_ref, g_ref, out_ref, list_s, bias_s, q_v, g_v, sems):
    copies = [
        pltpu.make_async_copy(src, dst, sems.at[i])
        for i, (src, dst) in enumerate(((list_ref, list_s), (bias_ref, bias_s), (q_ref, q_v), (g_ref, g_v)))
    ]
    for copy in copies:
        copy.start()
    for copy in copies:
        copy.wait()
    lane = iota((1, 128), 1)
    mask = jnp.zeros((1, 128), F32)
    for i in range(list_ref.shape[1]):
        mask = jnp.where(lane == list_s[0, i], 1.0, mask)
    bias = jnp.zeros((1, 128), F32)
    for i in range(16):
        bias = jnp.where(lane == i, bias_s[0, i], bias)
    high = bias.astype(BF16).astype(F32)
    middle = (bias - high).astype(BF16).astype(F32)
    last = bias - high - middle
    kind = iota((16, 128), 0) % 4
    meta = jnp.where(kind == 0, mask, jnp.where(kind == 1, high, jnp.where(kind == 2, middle, last)))
    meta = meta.astype(BF16)
    for to in range(16):
        out_ref[to, 0:64, 0:96] = q_v[...] if to % 2 == 0 else g_v[...]
        out_ref[to, 64:80, :] = meta


def turn_kernel(got_ref, out_ref):
    for part in range(4):
        for pair in range(2):
            both = jnp.concatenate([got_ref[pair * 8 + part, 0:64, :], got_ref[pair * 8 + 4 + part, 0:64, :]], axis=0)
            out_ref[part * FEAT : part * FEAT + FEAT, pair * 128 : pair * 128 + 128] = both.T[:FEAT, :]
    owner = iota((16, 128), 0) // 4
    meta = jnp.zeros((16, 128), F32)
    for zhi in range(4):
        meta = jnp.where(owner == zhi, got_ref[zhi * 4, 64:80, :].astype(F32), meta)
    out_ref[PART:HIGH, 0:128] = meta.astype(BF16)
    out_ref[PART:HIGH, 128:256] = meta.astype(BF16)


def stack_kernel(*refs):
    for k in range(4):
        refs[4][k] = refs[k][...]


def prepare_kernel(ids_ref, key_ref, value_ref, region_ref, key_out, value_out, hot_ref, sems):
    copies = [
        pltpu.make_async_copy(key_ref, key_out, sems.at[0]),
        pltpu.make_async_copy(value_ref, value_out, sems.at[1]),
    ]
    for copy in copies:
        copy.start()
    for block in range(NB):
        label = iota((256, BLOCK), 0)
        region = region_ref[:, block * BLOCK : (block + 1) * BLOCK]
        at = ids_ref[5] * NB + block
        hot = (label == at) | ((label >= 96) & (label < 144) & (label % 16 == region))
        hot_ref[block * BLOCK : (block + 1) * BLOCK, :] = jnp.where(hot, 1.0, 0.0).T.astype(BF16)
    for copy in copies:
        copy.wait()


def load(refs, full_ref, sems, first, place):
    by_slot = [[], [], [], []]
    for step in range(4):
        for inner in range(4):
            for zlo in range(2):
                slot, at = place(step, inner)
                row = pl.multiple_of((zlo * 4 + at) * 2 * FEAT, 64)
                copies = [
                    pltpu.make_async_copy(
                        refs[step + half].at[inner, pl.ds(zlo * 2 * FEAT, 2 * FEAT)],
                        full_ref.at[slot, pl.ds(row, 2 * FEAT)],
                        sems.at[step * 8 + inner * 2 + zlo],
                    )
                    for half in (0, 4)
                ]
                pl.when(first)(copies[0].start)
                pl.when(jnp.logical_not(first))(copies[1].start)
                by_slot[slot].append(copies[0])
    return by_slot


def score_kernel(ids_ref, *refs):
    q_refs, (key_ref, hot_ref, e_ref, stat_ref, mine_ref, full_ref, meta_ref, sems) = refs[:8], refs[8:]
    x, y, core, latent = ids_ref[0], ids_ref[1], ids_ref[2], ids_ref[3]
    slots = load(q_refs, full_ref, sems, core == 0, lambda step, inner: (inner, lax.rem(x + 4 - step, 4)))
    metas = [pltpu.make_async_copy(q_refs[half].at[:, pl.ds(PART, 16)], meta_ref, sems.at[32]) for half in (0, 4)]
    pl.when(core == 0)(metas[0].start)
    pl.when(core != 0)(metas[1].start)
    metas[0].wait()
    group = iota((1, WIDE), 1) // ROWS
    for k in range(4):
        at = lax.rem(y + 4 - k, 4)
        meta = meta_ref[k, :, 0:128].astype(F32).T
        parts = []
        for kind in range(4):
            height = 96 if kind == 0 else 16
            part = jnp.zeros((height, WIDE), F32)
            for zhi in range(4):
                part = jnp.where(group == zhi, meta[:height, zhi * 4 + kind : zhi * 4 + kind + 1], part)
            parts.append((part - 1.0) * 1e30 if kind == 0 else part)
        table = jnp.concatenate(parts + [jnp.zeros((112, WIDE), F32)], axis=0).astype(BF16)
        for copy in slots[k]:
            copy.wait()
        s = jnp.dot(key_ref[...], full_ref[k], preferred_element_type=F32) * SCALE
        s = s + jnp.dot(hot_ref[...], table, preferred_element_type=F32)
        top = jnp.max(s, axis=0, keepdims=True)
        e = jnp.where(s > -1e29, jnp.exp(s - top), 0.0)
        e_ref[at] = e
        total = jnp.sum(e, axis=0, keepdims=True)
        for to in range(16):
            stat_ref[to, pl.ds(at, 1), :] = top
            stat_ref[to, pl.ds(4 + at, 1), :] = total
        mine_ref[at] = full_ref[k, pl.ds(pl.multiple_of(latent * FEAT, 32), FEAT), :]


def dweight_kernel(ids_ref, *refs):
    g_refs, (value_ref, dw_ref, mine_ref, full_ref, sems) = refs[:8], refs[8:]
    x, y, core, latent = ids_ref[0], ids_ref[1], ids_ref[2], ids_ref[3]
    slots = load(g_refs, full_ref, sems, core == 1, lambda step, inner: (step, lax.rem(x + 4 - inner, 4)))
    for k in range(4):
        for copy in slots[k]:
            copy.wait()
        at = lax.rem(y + 4 - k, 4)
        dw_ref[at] = jnp.dot(value_ref[...], full_ref[k], preferred_element_type=F32)
        mine_ref[at] = full_ref[k, pl.ds(pl.multiple_of(latent * FEAT, 32), FEAT), :]


def delta_kernel(e_ref, dw_ref, stat_ref, all_ref, delta_ref, factor_ref, low_ref):
    tops = all_ref[:, 0:4, :]
    peak = jnp.max(tops, axis=0)
    whole = jnp.sum(all_ref[:, 4:8, :] * jnp.exp(tops - peak[None]), axis=0)
    factor_ref[...] = jnp.exp(stat_ref[0, 0:4, :] - peak) / whole

    def body(k, _):
        low = (e_ref[k] * factor_ref[pl.ds(k, 1), :]).astype(BF16)
        low_ref[k] = low
        delta = jnp.sum(low.astype(F32) * dw_ref[k], axis=0, keepdims=True)
        for to in range(16):
            delta_ref[to, pl.ds(k, 1), :] = delta
        return 0

    lax.fori_loop(0, 4, body, 0)


def own_rows(ids_ref, values_ref, other_ref):
    y, zhi = ids_ref[1], ids_ref[4]
    lanes = pl.ds(pl.multiple_of(lax.div(zhi, 2) * 128, 128), 128)
    both = lax.dot_general(values_ref[y, :, lanes], other_ref[...], TN, preferred_element_type=F32)
    return jnp.where(lax.rem(zhi, 2) == 1, both[ROWS:], both[:ROWS])


def mixed_kernel(ids_ref, low_ref, value_ref, mine_ref, mixed_ref, gv_ref):
    mixed_ref[...] = own_rows(ids_ref, low_ref, value_ref)
    total = jnp.zeros((FEAT, TILES), F32)
    for k in range(4):
        total = total + lax.dot_general(mine_ref[k], low_ref[k], NT, preferred_element_type=F32)
    gv_ref[...] = total.astype(BF16)


def back_kernel(ids_ref, e_ref, dw_ref, factor_ref, deltas_ref, key_ref, mixed_ref, terms_ref, ds_ref):
    delta = jnp.sum(deltas_ref[...], axis=0)
    for k in range(4):
        w = e_ref[k] * factor_ref[k : k + 1, :]
        ds_ref[k] = (w * (dw_ref[k] - delta[k : k + 1, :])).astype(BF16)
    grads = own_rows(ids_ref, ds_ref, key_ref) * SCALE
    terms_ref[...] = jnp.concatenate([mixed_ref[...], grads], axis=0).T


def grad_key_kernel(mine_ref, ds_ref, gk_ref):
    total = jnp.zeros((FEAT, TILES), F32)
    for k in range(4):
        total = total + lax.dot_general(mine_ref[k], ds_ref[k], NT, preferred_element_type=F32)
    gk_ref[...] = (total * SCALE).astype(BF16)


def last_kernel(terms_ref, attended_ref, gq_ref):
    both = jnp.sum(terms_ref[...], axis=0).T
    attended_ref[...] = both[:ROWS].astype(BF16)
    gq_ref[...] = both[ROWS:].astype(BF16)


def call(kernel, outs, ins, args, scratch=(), flops=0, moved=0, limit=16):
    vmem = pl.BlockSpec(memory_space=pltpu.VMEM)
    specs = {"v": vmem, "V": vmem, "s": pl.BlockSpec(memory_space=pltpu.SMEM), "H": pl.BlockSpec(memory_space=pl.ANY)}
    pins = {"V": pltpu.VMEM, "H": pltpu.HBM}
    shapes = [pltpu.VMEM(shape, kind) if c == "V" else jax.ShapeDtypeStruct(shape, kind) for c, shape, kind in outs]
    args = [pltpu.with_memory_space_constraint(a, pins[c]) if c in pins else a for c, a in zip(ins, args)]
    return pl.pallas_call(
        kernel,
        out_shape=shapes,
        in_specs=[specs[c] for c in ins],
        out_specs=[vmem] * len(outs),
        scratch_shapes=list(scratch),
        compiler_params=pltpu.CompilerParams(vmem_limit_bytes=limit * MIB),
        cost_estimate=pl.CostEstimate(flops=flops, bytes_accessed=moved, transcendentals=0),
    )(*args)


PLANE = [(x, core, y) for x in range(4) for core in range(2) for y in range(4)]


def along(value, stage, step):
    pairs = []
    for i, (x, core, y) in enumerate(PLANE):
        to = (x, core, (y + step) % 4) if core == stage else ((x + step) % 4, core, y)
        pairs.append((i, PLANE.index(to)))
    return lax.ppermute(value, ("x", "core", "y"), pairs)


def swap(value):
    return lax.ppermute(value, "core", [(0, 1), (1, 0)])


def shards(queries, tile_keys, tile_values, region_ids, block_list, region_bias, grad_out):
    ids = [lax.axis_index(n) for n in ("x", "y", "core", LATENT, "zhi", PATCH)]
    ids = jnp.stack(ids).astype(jnp.int32)
    dma = pltpu.SemaphoreType.DMA
    wide = (4, TILES, WIDE)
    slices = (4, FEAT, WIDE)

    (packed,) = call(
        pack_kernel,
        [("v", (16, 80, 128), BF16)],
        "HHHH",
        (block_list, region_bias, queries, grad_out),
        [
            pltpu.SMEM(block_list.shape, jnp.int32),
            pltpu.SMEM(region_bias.shape, F32),
            pltpu.VMEM((ROWS, FEAT), BF16),
            pltpu.VMEM((ROWS, FEAT), BF16),
            dma((4,)),
        ],
    )
    got = lax.all_to_all(packed, ("zhi", "zlo", "core"), 0, 0)
    key_in, value_in, hot = call(
        prepare_kernel,
        [("V", (TILES, D), BF16), ("V", (TILES, D), BF16), ("V", (TILES, 256), BF16)],
        "sHHv",
        (ids, tile_keys, tile_values, region_ids.reshape(1, TILES)),
        [dma((2,))],
        0,
        10_000_000,
    )
    (block,) = call(turn_kernel, [("v", (HIGH, WIDE), BF16)], "v", (got,))
    (line,) = call(
        stack_kernel,
        [("v", (4, HIGH, WIDE), BF16)],
        "vvvv",
        [block] + [along(block, 0, k) for k in (1, 2, 3)],
    )
    near = [line] + [along(line, 1, k) for k in (1, 2, 3)]
    planes = near + [swap(part) for part in near]

    full = [pltpu.VMEM((4, D, WIDE), BF16)]
    flops = 2 * TILES * 1024 * D
    e, stat, q_mine = call(
        score_kernel,
        [("V", wide, F32), ("v", (16, 8, WIDE), F32), ("V", slices, BF16)],
        "s" + "H" * 8 + "VV",
        (ids, *planes, key_in, hot),
        full + [pltpu.VMEM((4, 16, WIDE), BF16), dma((33,))],
        flops,
        10_000_000,
    )
    stats = lax.all_to_all(stat, PATCH, 0, 0)
    dw, g_mine = call(
        dweight_kernel,
        [("V", wide, F32), ("V", slices, BF16)],
        "s" + "H" * 8 + "V",
        (ids, *planes, value_in),
        full + [dma((32,))],
        flops,
        10_000_000,
    )
    delta, factor, low = call(
        delta_kernel,
        [("v", (16, 4, WIDE), F32), ("V", (4, WIDE), F32), ("V", wide, BF16)],
        "VVvv",
        (e, dw, stat, stats),
        (),
        4 * TILES * 1024,
        8_000_000,
    )
    deltas = lax.all_to_all(delta, PATCH, 0, 0)
    mixed, grad_values = call(
        mixed_kernel,
        [("V", (ROWS, D), F32), ("v", (FEAT, TILES), BF16)],
        "sVVV",
        (ids, low, value_in, g_mine),
        (),
        2 * TILES * 1024 * FEAT,
        5_000_000,
    )
    terms, ds = call(
        back_kernel,
        [("v", (D, 128), F32), ("V", wide, BF16)],
        "sVVVvVV",
        (ids, e, dw, factor, deltas, key_in, mixed),
        (),
        4 * TILES * 128 * D,
        10_000_000,
    )
    sums = lax.all_to_all(terms.reshape(16, FEAT, 128), PATCH, 0, 0)
    (grad_keys,) = call(
        grad_key_kernel,
        [("v", (FEAT, TILES), BF16)],
        "VV",
        (q_mine, ds),
        (),
        2 * TILES * 1024 * FEAT,
        2_000_000,
    )
    attended, grad_queries = call(last_kernel, [("v", (ROWS, FEAT), BF16)] * 2, "v", (sums,))
    return (attended, grad_queries, grad_keys, grad_values)


def solution(mesh):
    fine = Mesh(mesh.devices.reshape(2, 4, 2, 4, 4), PATCH + LATENT)
    in_specs = (
        P(LATENT, PATCH),
        P(PATCH, None),
        P(PATCH, None),
        P(PATCH),
        P(LATENT, None),
        P(LATENT, None),
        P(LATENT, PATCH),
    )
    out_specs = (P(LATENT, PATCH),) * 4
    return jax.shard_map(shards, mesh=fine, in_specs=in_specs, out_specs=out_specs, check_vma=False)
```

time: 153 us -> 138 us (0.902); the launches traced: 150 us -> 137 us
  local copies, waits for them, and re-layouts: 36.3 us -> 19.9 us
  waiting for transfers between devices: 24.3 us -> 35.4 us
  starting transfers between devices: 38.6 us -> 27.8 us
  blocking collectives: 19.7 us -> 22.8 us
  Pallas kernels: 27.8 us -> 30.7 us
  other arithmetic: 2.7 us -> 0 us
    unnamed x74 -> x44, local copies, waits for them, and re-layouts: 34.9 us -> 19.8 us
    ppermute x12 -> x6, waiting for transfers between devices: 13.5 us -> 24.6 us  [along(): return lax.ppermute(value, ('x', 'core', 'y'), pairs)]
    ppermute x12 -> x6, starting transfers between devices: 16.6 us -> 7.24 us  [along(): return lax.ppermute(value, ('x', 'core', 'y'), pairs)]
    all_to_all x1, blocking collectives: 19.7 us -> 22.8 us  [shards(): got = lax.all_to_all(packed, ('zhi', 'zlo', 'core'), 0, 0)]
    pallas_call x9 -> x11, Pallas kernels: 27.8 us -> 30.7 us  [call(): pl.pallas_call(kernel, out_shape=shapes, in_specs=[specs[c] for c in ins]...]
    ppermute x8 -> x4, starting transfers between devices: 6.55 us -> 5.61 us  [swap(): return lax.ppermute(value, 'core', [(0, 1), (1, 0)])]
  transfers between devices with their start and end apart: 23 -> 13, of which waited for: 5 -> 6; matrix products, arithmetic and copies ran while one was open for 2% -> 0% of each run, Pallas kernels for 16% -> 10%
where the time goes in v2:
time: 138 us; the launch traced here: 137 us
  waiting for transfers between devices  35.4 us (26%)
  Pallas kernels  30.7 us (22%)
  starting transfers between devices  27.8 us (20%)
  blocking collectives  22.8 us (17%)
  local copies, waits for them, and re-layouts  19.9 us (14%)
    pallas_call x11, Pallas kernels, call(): pl.pallas_call(kernel, out_shape=shapes, in_specs=[specs[c] for c in ins]...  30.7 us
    ppermute x6, waiting for transfers between devices, along(): return lax.ppermute(value, ('x', 'core', 'y'), pairs)  24.6 us
    all_to_all x1, blocking collectives, shards(): got = lax.all_to_all(packed, ('zhi', 'zlo', 'core'), 0, 0)  22.8 us
    unnamed x44, local copies, waits for them, and re-layouts  19.8 us
    all_to_all x1, waiting for transfers between devices, shards(): sums = lax.all_to_all(terms.reshape(16, FEAT, 128), PATCH, 0, 0)  10.8 us
    ppermute x6, starting transfers between devices, along(): return lax.ppermute(value, ('x', 'core', 'y'), pairs)  7.24 us
    all_to_all x1, starting transfers between devices, shards(): sums = lax.all_to_all(terms.reshape(16, FEAT, 128), PATCH, 0, 0)  5.86 us
    all_to_all x1, starting transfers between devices, shards(): deltas = lax.all_to_all(delta, PATCH, 0, 0)  5.71 us
  transfers between devices with their start and end apart: 13, of which 6 were waited for; matrix products, arithmetic and copies ran while one was open for 0% of the time, Pallas kernels for 10%

profile of v2, /device:TPU:1, one launch (start us, length us, event | category | flops | bytes accessed | tf_op | source)
XLA Modules:
  0.0 137.4 jit_solution(11457007762062077236)
XLA Ops:
  0.6 0.9 shard_map.102
  1.6 22.8 %all_to_all.20.got_ref = bf16[16,80,128]{2,1,0:T(8,128)(2,1)S(1)} all-to-all(bf16[16,80,128]{2,1,0:T(8,128)(2,1)S(1)} %shard_map.102), channel_id=1, replica_groups=mesh['zlo'=2,'x'=4,'core'=2,'zhi'=4,'y'=4] {'zhi','zlo','core'}, dimensions={0} | all-to-all | bytes 655360 | tf_op jit(solution)/shard_map/all_to_all | solution.py:266
  24.4 0.1 shard_map.103.refs_0_
  24.5 2.6 %collective-permute-start.2 = (bf16[400,256]{1,0:T(8,128)(2,1)S(1)}, bf16[400,256]{1,0:T(8,128)(2,1)S(1)}, u32[]{:S(2)}, u32[]{:S(2)}) collective-permute-start(bf16[400,256]{1,0:T(8,128)(2,1)S(1)} %shard_map.103.refs_0_), channel_id=1, source_target_pairs={{0,3},{1,0},{2,1},{3,2},{16,112},{17,113},{18,114},{19,115},{32,35... | collective-permute-start | bytes 614408 | tf_op jit(solution)/shard_map/ppermute | solution.py:239
  27.1 0.5 collective-permute-start.1
  27.6 0.6 collective-permute-start
  28.2 3.8 %collective-permute-done.2.refs_3_ = bf16[400,256]{1,0:T(8,128)(2,1)S(1)} collective-permute-done((bf16[400,256]{1,0:T(8,128)(2,1)S(1)}, bf16[400,256]{1,0:T(8,128)(2,1)S(1)}, u32[]{:S(2)}, u32[]{:S(2)}) %collective-permute-start.2) | collective-permute-done | bytes 204832 | tf_op jit(solution)/shard_map/ppermute | solution.py:239
  32.0 1.6 %collective-permute-done.1.refs_2_ = bf16[400,256]{1,0:T(8,128)(2,1)S(1)} collective-permute-done((bf16[400,256]{1,0:T(8,128)(2,1)S(1)}, bf16[400,256]{1,0:T(8,128)(2,1)S(1)}, u32[]{:S(2)}, u32[]{:S(2)}) %collective-permute-start.1) | collective-permute-done | bytes 204832 | tf_op jit(solution)/shard_map/ppermute | solution.py:239
  33.5 2.2 %collective-permute-done.refs_1_ = bf16[400,256]{1,0:T(8,128)(2,1)S(1)} collective-permute-done((bf16[400,256]{1,0:T(8,128)(2,1)S(1)}, bf16[400,256]{1,0:T(8,128)(2,1)S(1)}, u32[]{:S(2)}, u32[]{:S(2)}) %collective-permute-start) | collective-permute-done | bytes 204832 | tf_op jit(solution)/shard_map/ppermute | solution.py:239
  35.7 0.1 shard_map.104.refs_0_
  35.7 2.5 %collective-permute-start.5 = (bf16[4,400,256]{2,1,0:T(8,128)(2,1)S(1)}, bf16[4,400,256]{2,1,0:T(8,128)(2,1)S(1)}, u32[]{:S(2)}, u32[]{:S(2)}) collective-permute-start(bf16[4,400,256]{2,1,0:T(8,128)(2,1)S(1)} %shard_map.104.refs_0_), channel_id=1, source_target_pairs={{0,96},{1,97},{2,98},{3,99},{16,19},{17,16},{18,17},{19,18},{32,0}... | collective-permute-start | bytes 2457608 | tf_op jit(solution)/shard_map/ppermute | solution.py:239
  38.3 0.3 collective-permute-start.4
  38.6 0.7 collective-permute-start.3
  39.3 1.8 %collective-permute-start.6 = (bf16[4,400,256]{2,1,0:T(8,128)(2,1)S(1)}, bf16[4,400,256]{2,1,0:T(8,128)(2,1)}, u32[]{:S(2)}, u32[]{:S(2)}) collective-permute-start(bf16[4,400,256]{2,1,0:T(8,128)(2,1)S(1)} %shard_map.104.refs_0_), channel_id=1, source_target_pairs={{0,16},{16,0},{1,17},{17,1},{2,18},{18,2},{3,19},{19,3},{4,20},{20... | collective-permute-start | bytes 2457608 | tf_op jit(solution)/shard_map/ppermute | solution.py:243
  41.1 15.2 %collective-permute-done.5.refs_3_ = bf16[4,400,256]{2,1,0:T(8,128)(2,1)S(1)} collective-permute-done((bf16[4,400,256]{2,1,0:T(8,128)(2,1)S(1)}, bf16[4,400,256]{2,1,0:T(8,128)(2,1)S(1)}, u32[]{:S(2)}, u32[]{:S(2)}) %collective-permute-start.5) | collective-permute-done | bytes 819232 | tf_op jit(solution)/shard_map/ppermute | solution.py:239
  56.3 1.7 %collective-permute-start.9 = (bf16[4,400,256]{2,1,0:T(8,128)(2,1)S(1)}, bf16[4,400,256]{2,1,0:T(8,128)(2,1)}, u32[]{:S(2)}, u32[]{:S(2)}) collective-permute-start(bf16[4,400,256]{2,1,0:T(8,128)(2,1)S(1)} %collective-permute-done.5.refs_3_), channel_id=1, source_target_pairs={{0,16},{16,0},{1,17},{17,1},{2,18},{18,2},{3,19},{19,3},{4,20},{20... | collective-permute-start | bytes 2457608 | tf_op jit(solution)/shard_map/ppermute | solution.py:243
  58.1 0.1 collective-permute-start.8
  58.2 1.9 %collective-permute-done.3.refs_1_ = bf16[4,400,256]{2,1,0:T(8,128)(2,1)S(1)} collective-permute-done((bf16[4,400,256]{2,1,0:T(8,128)(2,1)S(1)}, bf16[4,400,256]{2,1,0:T(8,128)(2,1)S(1)}, u32[]{:S(2)}, u32[]{:S(2)}) %collective-permute-start.3) | collective-permute-done | bytes 819232 | tf_op jit(solution)/shard_map/ppermute | solution.py:239
  60.0 2.0 %collective-permute-start.7 = (bf16[4,400,256]{2,1,0:T(8,128)(2,1)S(1)}, bf16[4,400,256]{2,1,0:T(8,128)(2,1)}, u32[]{:S(2)}, u32[]{:S(2)}) collective-permute-start(bf16[4,400,256]{2,1,0:T(8,128)(2,1)S(1)} %collective-permute-done.3.refs_1_), channel_id=1, source_target_pairs={{0,16},{16,0},{1,17},{17,1},{2,18},{18,2},{3,19},{19,3},{4,20},{20... | collective-permute-start | bytes 2457608 | tf_op jit(solution)/shard_map/ppermute | solution.py:243
  62.0 0.1 stack.27.ids_ref
  62.1 2.9 %shard_map.105 = (bf16[768,1536]{1,0:T(8,128)(2,1)S(1)}, bf16[768,1536]{1,0:T(8,128)(2,1)S(1)}, bf16[768,256]{1,0:T(8,128)(2,1)S(1)}) custom-call(s32[6]{0:T(128)S(1)} %stack.27.ids_ref, bf16[768,1536]{1,0:T(8,128)(2,1)} %key_ref.1, bf16[768,1536]{1,0:T(8,128)(2,1)} %value_ref.1, s32[1,768]{1,0:T(1,128)S(1)} %reshape.14.region_ref), custom_call_target="tpu_custom_call" | custom-call | bytes 10000000 | tf_op jit(solution)/shard_map/pallas_call | solution.py:220
  65.1 1.5 %copy-done.6 = bf16[768,1536]{1,0:T(8,128)(2,1)} copy-done((bf16[768,1536]{1,0:T(8,128)(2,1)}, bf16[768,1536]{1,0:T(8,128)(2,1)S(1)}, u32[]{:S(2)}) %copy-start.6) | copy-done | bytes 2359320
  66.6 0.0 collective-permute-done.9.refs_7_
  66.6 10.5 %shard_map.106 = (f32[4,768,256]{2,1,0:T(8,128)S(1)}, f32[16,8,256]{2,1,0:T(8,128)}, bf16[4,96,256]{2,1,0:T(8,128)(2,1)S(1)}) custom-call(s32[6]{0:T(128)S(1)} %stack.27.ids_ref, bf16[4,400,256]{2,1,0:T(8,128)(2,1)} %copy-done.5, bf16[4,400,256]{2,1,0:T(8,128)(2,1)} %copy-done.20, bf16[4,400,256]{2,1,0:T(8,128)(2,1)} %copy-done.19, ...), custom_call_target="tpu_custom_call" | custom-call | flops 2415919104 | bytes 10000000 | tf_op jit(solution)/shard_map/pallas_call | solution.py:220
  77.2 0.7 copy-done.16
  77.8 3.4 %all-to-all-start.1 = ((f32[16,8,256]{2,1,0:T(8,128)}), f32[16,8,256]{2,1,0:T(8,128)S(1)}, u32[]{:S(2)}, u32[]{:S(2)}) async-start(f32[16,8,256]{2,1,0:T(8,128)} %get-tuple-element.26.stat_ref), calls=%async_computation.1 | async-start | bytes 262144 | tf_op jit(solution)/shard_map/all_to_all | solution.py:297
  81.3 1.7 %copy-done.7 = bf16[768,1536]{1,0:T(8,128)(2,1)S(1)} copy-done((bf16[768,1536]{1,0:T(8,128)(2,1)S(1)}, bf16[768,1536]{1,0:T(8,128)(2,1)}, u32[]{:S(2)}) %copy-start.7) | copy-done | bytes 2359320
  82.9 7.5 %shard_map.107 = (f32[4,768,256]{2,1,0:T(8,128)S(1)}, bf16[4,96,256]{2,1,0:T(8,128)(2,1)S(1)}) custom-call(s32[6]{0:T(128)S(1)} %stack.27.ids_ref, bf16[4,400,256]{2,1,0:T(8,128)(2,1)} %copy-done.5, bf16[4,400,256]{2,1,0:T(8,128)(2,1)} %copy-done.20, bf16[4,400,256]{2,1,0:T(8,128)(2,1)} %copy-done.19, bf16[4,400,256]{2,1,0:T(8,128)(2,1)} %copy-done.18, ...), custom_call_target="tpu_custom_call" | custom-call | flops 2415919104 | bytes 10000000 | tf_op jit(solution)/shard_map/pallas_call | solution.py:220
  90.5 1.7 %copy-done = f32[4,768,256]{2,1,0:T(8,128)} copy-done((f32[4,768,256]{2,1,0:T(8,128)}, f32[4,768,256]{2,1,0:T(8,128)S(1)}, u32[]{:S(2)}) %copy-start) | copy-done | bytes 3145752
  92.2 0.7 copy-done.14
  92.8 1.9 %copy-done.1 = f32[4,768,256]{2,1,0:T(8,128)S(1)} copy-done((f32[4,768,256]{2,1,0:T(8,128)S(1)}, f32[4,768,256]{2,1,0:T(8,128)}, u32[]{:S(2)}) %copy-start.1) | copy-done | bytes 3145752
  94.7 2.2 %shard_map.108 = (f32[16,4,256]{2,1,0:T(4,128)}, f32[4,256]{1,0:T(4,128)S(1)}, bf16[4,768,256]{2,1,0:T(8,128)(2,1)S(1)}) custom-call(f32[4,768,256]{2,1,0:T(8,128)S(1)} %get-tuple-element.23.e_ref, f32[4,768,256]{2,1,0:T(8,128)S(1)} %copy-done.1, f32[16,8,256]{2,1,0:T(8,128)} %get-tuple-element.26.stat_ref, f32[16,8,256]{2,1,0:T(8,128)S(1)} %all-to-all-done.1.all_ref), custom_call_target="tpu_custom_call" | custom-call | flops 3145728 | bytes 8000000 | tf_op jit(solution)/shard_map/pallas_call | solution.py:220
  96.9 1.2 copy-done.9
  98.1 5.7 %all-to-all-start.2 = ((f32[16,4,256]{2,1,0:T(4,128)}), f32[16,4,256]{2,1,0:T(4,128)}, u32[]{:S(2)}, u32[]{:S(2)}) async-start(f32[16,4,256]{2,1,0:T(4,128)} %get-tuple-element.28), calls=%async_computation.2 | async-start | bytes 131072 | tf_op jit(solution)/shard_map/all_to_all | solution.py:316
  103.8 1.7 %copy-done.8 = bf16[768,1536]{1,0:T(8,128)(2,1)S(1)} copy-done((bf16[768,1536]{1,0:T(8,128)(2,1)S(1)}, bf16[768,1536]{1,0:T(8,128)(2,1)}, u32[]{:S(2)}) %copy-start.8) | copy-done | bytes 2359320
  105.5 1.4 %copy-done.10 = bf16[4,768,256]{2,1,0:T(8,128)(2,1)S(1)} copy-done((bf16[4,768,256]{2,1,0:T(8,128)(2,1)S(1)}, bf16[4,768,256]{2,1,0:T(8,128)(2,1)}, u32[]{:S(2)}) %copy-start.10) | copy-done | bytes 1572888
  106.9 0.9 copy-done.15
  107.8 2.2 %shard_map.109 = (f32[64,1536]{1,0:T(8,128)S(1)}, bf16[96,768]{1,0:T(8,128)(2,1)}) custom-call(s32[6]{0:T(128)S(1)} %stack.27.ids_ref, bf16[4,768,256]{2,1,0:T(8,128)(2,1)S(1)} %copy-done.10, bf16[768,1536]{1,0:T(8,128)(2,1)S(1)} %copy-done.8, bf16[4,96,256]{2,1,0:T(8,128)(2,1)S(1)} %copy-done.15), custom_call_target="tpu_custom_call" | custom-call | flops 150994944 | bytes 5000000 | tf_op jit(solution)/shard_map/pallas_call | solution.py:220
  110.0 1.9 %copy-done.2 = f32[4,768,256]{2,1,0:T(8,128)S(1)} copy-done((f32[4,768,256]{2,1,0:T(8,128)S(1)}, f32[4,768,256]{2,1,0:T(8,128)}, u32[]{:S(2)}) %copy-start.2) | copy-done | bytes 3145752
  111.9 1.7 %copy-done.4 = bf16[768,1536]{1,0:T(8,128)(2,1)S(1)} copy-done((bf16[768,1536]{1,0:T(8,128)(2,1)S(1)}, bf16[768,1536]{1,0:T(8,128)(2,1)}, u32[]{:S(2)}) %copy-start.4) | copy-done | bytes 2359320
  113.5 2.3 %shard_map.110 = (f32[1536,128]{1,0:T(8,128)S(1)}, bf16[4,768,256]{2,1,0:T(8,128)(2,1)S(1)}) custom-call(s32[6]{0:T(128)S(1)} %stack.27.ids_ref, f32[4,768,256]{2,1,0:T(8,128)S(1)} %get-tuple-element.23.e_ref, f32[4,768,256]{2,1,0:T(8,128)S(1)} %copy-done.2, f32[4,256]{1,0:T(4,128)S(1)} %get-tuple-element.27.factor_ref, ...), custom_call_target="tpu_custom_call" | custom-call | flops 603979776 | bytes 10000000 | tf_op jit(solution)/shard_map/pallas_call | solution.py:220
  115.8 1.1 copy-done.11
  116.9 0.9 copy-done.13
  117.9 5.9 %all-to-all-start.3 = ((f32[16,96,128]{2,1,0:T(8,128)}), f32[16,96,128]{2,1,0:T(8,128)S(1)}, u32[]{:S(2)}, u32[]{:S(2)}) async-start(f32[16,96,128]{2,1,0:T(8,128)} %bitcast.7), calls=%async_computation.3 | async-start | bytes 1572864 | tf_op jit(solution)/shard_map/all_to_all | solution.py:335
  123.7 0.9 copy-done.17
  124.6 1.3 shard_map.112
  125.9 10.8 %all-to-all-done.3.terms_ref = f32[16,96,128]{2,1,0:T(8,128)S(1)} async-done(((f32[16,96,128]{2,1,0:T(8,128)}), f32[16,96,128]{2,1,0:T(8,128)S(1)}, u32[]{:S(2)}, u32[]{:S(2)}) %all-to-all-start.3) | async-done | bytes 786464 | tf_op jit(solution)/shard_map/all_to_all | solution.py:335
  136.7 0.7 shard_map.111
  (36 shorter events, 0.1 us)
Async XLA Ops:
  0.6 61.4 %copy-start.21 = (s32[768]{0:T(1024)S(1)}, s32[768]{0:T(1024)}, u32[]{:S(2)}) copy-start(s32[768]{0:T(1024)} %param.10) | copy-start | bytes 9220
  24.5 7.5 %collective-permute-start.2 = (bf16[400,256]{1,0:T(8,128)(2,1)S(1)}, bf16[400,256]{1,0:T(8,128)(2,1)S(1)}, u32[]{:S(2)}, u32[]{:S(2)}) collective-permute-start(bf16[400,256]{1,0:T(8,128)(2,1)S(1)} %shard_map.103.refs_0_), channel_id=1, source_target_pairs={{0,3},{1,0},{2,1},{3,2},{16,112},{17,113},{18,114},{19,115},{32,35... | collective-permute-start | bytes 614408 | tf_op jit(solution)/shard_map/ppermute | solution.py:239
  27.1 6.5 %collective-permute-start.1 = (bf16[400,256]{1,0:T(8,128)(2,1)S(1)}, bf16[400,256]{1,0:T(8,128)(2,1)S(1)}, u32[]{:S(2)}, u32[]{:S(2)}) collective-permute-start(bf16[400,256]{1,0:T(8,128)(2,1)S(1)} %shard_map.103.refs_0_), channel_id=1, source_target_pairs={{0,2},{1,3},{2,0},{3,1},{16,80},{17,81},{18,82},{19,83},{32,34},{3... | collective-permute-start | bytes 614408 | tf_op jit(solution)/shard_map/ppermute | solution.py:239
  27.6 8.1 %collective-permute-start = (bf16[400,256]{1,0:T(8,128)(2,1)S(1)}, bf16[400,256]{1,0:T(8,128)(2,1)S(1)}, u32[]{:S(2)}, u32[]{:S(2)}) collective-permute-start(bf16[400,256]{1,0:T(8,128)(2,1)S(1)} %shard_map.103.refs_0_), channel_id=1, source_target_pairs={{0,1},{1,2},{2,3},{3,0},{16,48},{17,49},{18,50},{19,51},{32,33},{3... | collective-permute-start | bytes 614408 | tf_op jit(solution)/shard_map/ppermute | solution.py:239
  35.7 29.3 %copy-start.5 = (bf16[4,400,256]{2,1,0:T(8,128)(2,1)}, bf16[4,400,256]{2,1,0:T(8,128)(2,1)S(1)}, u32[]{:S(2)}) copy-start(bf16[4,400,256]{2,1,0:T(8,128)(2,1)S(1)} %shard_map.104.refs_0_) | copy-start | bytes 2457604
  35.7 20.6 %collective-permute-start.5 = (bf16[4,400,256]{2,1,0:T(8,128)(2,1)S(1)}, bf16[4,400,256]{2,1,0:T(8,128)(2,1)S(1)}, u32[]{:S(2)}, u32[]{:S(2)}) collective-permute-start(bf16[4,400,256]{2,1,0:T(8,128)(2,1)S(1)} %shard_map.104.refs_0_), channel_id=1, source_target_pairs={{0,96},{1,97},{2,98},{3,99},{16,19},{17,16},{18,17},{19,18},{32,0}... | collective-permute-start | bytes 2457608 | tf_op jit(solution)/shard_map/ppermute | solution.py:239
  38.3 19.8 %collective-permute-start.4 = (bf16[4,400,256]{2,1,0:T(8,128)(2,1)S(1)}, bf16[4,400,256]{2,1,0:T(8,128)(2,1)S(1)}, u32[]{:S(2)}, u32[]{:S(2)}) collective-permute-start(bf16[4,400,256]{2,1,0:T(8,128)(2,1)S(1)} %shard_map.104.refs_0_), channel_id=1, source_target_pairs={{0,64},{1,65},{2,66},{3,67},{16,18},{17,19},{18,16},{19,17},{32,96... | collective-permute-start | bytes 2457608 | tf_op jit(solution)/shard_map/ppermute | solution.py:239
  38.6 21.4 %collective-permute-start.3 = (bf16[4,400,256]{2,1,0:T(8,128)(2,1)S(1)}, bf16[4,400,256]{2,1,0:T(8,128)(2,1)S(1)}, u32[]{:S(2)}, u32[]{:S(2)}) collective-permute-start(bf16[4,400,256]{2,1,0:T(8,128)(2,1)S(1)} %shard_map.104.refs_0_), channel_id=1, source_target_pairs={{0,32},{1,33},{2,34},{3,35},{16,17},{17,18},{18,19},{19,16},{32,64... | collective-permute-start | bytes 2457608 | tf_op jit(solution)/shard_map/ppermute | solution.py:239
  39.3 27.3 %collective-permute-start.6 = (bf16[4,400,256]{2,1,0:T(8,128)(2,1)S(1)}, bf16[4,400,256]{2,1,0:T(8,128)(2,1)}, u32[]{:S(2)}, u32[]{:S(2)}) collective-permute-start(bf16[4,400,256]{2,1,0:T(8,128)(2,1)S(1)} %shard_map.104.refs_0_), channel_id=1, source_target_pairs={{0,16},{16,0},{1,17},{17,1},{2,18},{18,2},{3,19},{19,3},{4,20},{20... | collective-permute-start | bytes 2457608 | tf_op jit(solution)/shard_map/ppermute | solution.py:243
  56.3 8.7 %copy-start.18 = (bf16[4,400,256]{2,1,0:T(8,128)(2,1)}, bf16[4,400,256]{2,1,0:T(8,128)(2,1)S(1)}, u32[]{:S(2)}) copy-start(bf16[4,400,256]{2,1,0:T(8,128)(2,1)S(1)} %collective-permute-done.5.refs_3_) | copy-start | bytes 2457604
  56.3 10.3 %collective-permute-start.9 = (bf16[4,400,256]{2,1,0:T(8,128)(2,1)S(1)}, bf16[4,400,256]{2,1,0:T(8,128)(2,1)}, u32[]{:S(2)}, u32[]{:S(2)}) collective-permute-start(bf16[4,400,256]{2,1,0:T(8,128)(2,1)S(1)} %collective-permute-done.5.refs_3_), channel_id=1, source_target_pairs={{0,16},{16,0},{1,17},{17,1},{2,18},{18,2},{3,19},{19,3},{4,20},{20... | collective-permute-start | bytes 2457608 | tf_op jit(solution)/shard_map/ppermute | solution.py:243
  58.1 7.0 %copy-start.19 = (bf16[4,400,256]{2,1,0:T(8,128)(2,1)}, bf16[4,400,256]{2,1,0:T(8,128)(2,1)S(1)}, u32[]{:S(2)}) copy-start(bf16[4,400,256]{2,1,0:T(8,128)(2,1)S(1)} %collective-permute-done.4.refs_2_) | copy-start | bytes 2457604
  58.1 8.5 %collective-permute-start.8 = (bf16[4,400,256]{2,1,0:T(8,128)(2,1)S(1)}, bf16[4,400,256]{2,1,0:T(8,128)(2,1)}, u32[]{:S(2)}, u32[]{:S(2)}) collective-permute-start(bf16[4,400,256]{2,1,0:T(8,128)(2,1)S(1)} %collective-permute-done.4.refs_2_), channel_id=1, source_target_pairs={{0,16},{16,0},{1,17},{17,1},{2,18},{18,2},{3,19},{19,3},{4,20},{20... | collective-permute-start | bytes 2457608 | tf_op jit(solution)/shard_map/ppermute | solution.py:243
  60.0 5.1 %copy-start.20 = (bf16[4,400,256]{2,1,0:T(8,128)(2,1)}, bf16[4,400,256]{2,1,0:T(8,128)(2,1)S(1)}, u32[]{:S(2)}) copy-start(bf16[4,400,256]{2,1,0:T(8,128)(2,1)S(1)} %collective-permute-done.3.refs_1_) | copy-start | bytes 2457604
  60.0 6.6 %collective-permute-start.7 = (bf16[4,400,256]{2,1,0:T(8,128)(2,1)S(1)}, bf16[4,400,256]{2,1,0:T(8,128)(2,1)}, u32[]{:S(2)}, u32[]{:S(2)}) collective-permute-start(bf16[4,400,256]{2,1,0:T(8,128)(2,1)S(1)} %collective-permute-done.3.refs_1_), channel_id=1, source_target_pairs={{0,16},{16,0},{1,17},{17,1},{2,18},{18,2},{3,19},{19,3},{4,20},{20... | collective-permute-start | bytes 2457608 | tf_op jit(solution)/shard_map/ppermute | solution.py:243
  65.1 1.5 %copy-start.6 = (bf16[768,1536]{1,0:T(8,128)(2,1)}, bf16[768,1536]{1,0:T(8,128)(2,1)S(1)}, u32[]{:S(2)}) copy-start(bf16[768,1536]{1,0:T(8,128)(2,1)S(1)} %get-tuple-element.24.refs_8_.value_ref) | copy-start | bytes 7077892
  66.6 10.5 %copy-start.3 = (bf16[768,1536]{1,0:T(8,128)(2,1)}, bf16[768,1536]{1,0:T(8,128)(2,1)S(1)}, u32[]{:S(2)}) copy-start(bf16[768,1536]{1,0:T(8,128)(2,1)S(1)} %get-tuple-element.21.refs_8_.key_ref) | copy-start | bytes 7077892
  77.1 0.7 copy-start.16
  77.8 15.0 %all-to-all-start.1 = ((f32[16,8,256]{2,1,0:T(8,128)}), f32[16,8,256]{2,1,0:T(8,128)S(1)}, u32[]{:S(2)}, u32[]{:S(2)}) async-start(f32[16,8,256]{2,1,0:T(8,128)} %get-tuple-element.26.stat_ref), calls=%async_computation.1 | async-start | bytes 262144 | tf_op jit(solution)/shard_map/all_to_all | solution.py:297
  81.2 1.7 %copy-start.7 = (bf16[768,1536]{1,0:T(8,128)(2,1)S(1)}, bf16[768,1536]{1,0:T(8,128)(2,1)}, u32[]{:S(2)}) copy-start(bf16[768,1536]{1,0:T(8,128)(2,1)} %copy-done.6) | copy-start | bytes 7077892
  90.5 1.7 %copy-start = (f32[4,768,256]{2,1,0:T(8,128)}, f32[4,768,256]{2,1,0:T(8,128)S(1)}, u32[]{:S(2)}) copy-start(f32[4,768,256]{2,1,0:T(8,128)S(1)} %get-tuple-element.25.dw_ref) | copy-start | bytes 9437188
  92.1 0.7 copy-start.14
  92.8 1.9 %copy-start.1 = (f32[4,768,256]{2,1,0:T(8,128)S(1)}, f32[4,768,256]{2,1,0:T(8,128)}, u32[]{:S(2)}) copy-start(f32[4,768,256]{2,1,0:T(8,128)} %copy-done) | copy-start | bytes 9437188
  96.9 1.2 copy-start.9
  98.1 11.9 %all-to-all-start.2 = ((f32[16,4,256]{2,1,0:T(4,128)}), f32[16,4,256]{2,1,0:T(4,128)}, u32[]{:S(2)}, u32[]{:S(2)}) async-start(f32[16,4,256]{2,1,0:T(4,128)} %get-tuple-element.28), calls=%async_computation.2 | async-start | bytes 131072 | tf_op jit(solution)/shard_map/all_to_all | solution.py:316
  103.8 1.7 %copy-start.8 = (bf16[768,1536]{1,0:T(8,128)(2,1)S(1)}, bf16[768,1536]{1,0:T(8,128)(2,1)}, u32[]{:S(2)}) copy-start(bf16[768,1536]{1,0:T(8,128)(2,1)} %copy-done.6) | copy-start | bytes 7077892
  105.4 1.4 %copy-start.10 = (bf16[4,768,256]{2,1,0:T(8,128)(2,1)S(1)}, bf16[4,768,256]{2,1,0:T(8,128)(2,1)}, u32[]{:S(2)}) copy-start(bf16[4,768,256]{2,1,0:T(8,128)(2,1)} %copy-done.9) | copy-start | bytes 4718596
  106.9 0.9 copy-start.15
  110.0 1.9 %copy-start.2 = (f32[4,768,256]{2,1,0:T(8,128)S(1)}, f32[4,768,256]{2,1,0:T(8,128)}, u32[]{:S(2)}) copy-start(f32[4,768,256]{2,1,0:T(8,128)} %copy-done) | copy-start | bytes 9437188
  111.9 1.7 %copy-start.4 = (bf16[768,1536]{1,0:T(8,128)(2,1)S(1)}, bf16[768,1536]{1,0:T(8,128)(2,1)}, u32[]{:S(2)}) copy-start(bf16[768,1536]{1,0:T(8,128)(2,1)} %copy-done.3) | copy-start | bytes 7077892
  115.8 1.2 copy-start.11
  116.9 0.9 copy-start.13
  117.8 5.9 %copy-start.12 = (bf16[4,768,256]{2,1,0:T(8,128)(2,1)S(1)}, bf16[4,768,256]{2,1,0:T(8,128)(2,1)}, u32[]{:S(2)}) copy-start(bf16[4,768,256]{2,1,0:T(8,128)(2,1)} %copy-done.11) | copy-start | bytes 4718596
  117.9 18.8 %all-to-all-start.3 = ((f32[16,96,128]{2,1,0:T(8,128)}), f32[16,96,128]{2,1,0:T(8,128)S(1)}, u32[]{:S(2)}, u32[]{:S(2)}) async-start(f32[16,96,128]{2,1,0:T(8,128)} %bitcast.7), calls=%async_computation.3 | async-start | bytes 1572864 | tf_op jit(solution)/shard_map/all_to_all | solution.py:335
  123.7 0.9 copy-start.17

commit v3 on v2

v3 whole, which is shorter than its diff:
```python
import functools

import jax
import jax.numpy as jnp
from jax import lax
from jax.experimental import pallas as pl
from jax.experimental.pallas import tpu as pltpu
from jax.sharding import Mesh, PartitionSpec as P

BLOCK = 128
D = 1536
TILES = 768
ROWS = 64
FEAT = 96
NB = 6
WIDE = 256
PART = 384
HIGH = 400
PATCH = ("zlo", "x", "core")
LATENT = ("zhi", "y")
SCALE = D ** (-0.5)
F32 = jnp.float32
BF16 = jnp.bfloat16
NT = (((1,), (1,)), ((), ()))
TN = (((0,), (0,)), ((), ()))
MIB = 1024 * 1024


def iota(shape, dim):
    return lax.broadcasted_iota(jnp.int32, shape, dim)


def pack_kernel(list_ref, bias_ref, q_ref, g_ref, out_ref, list_s, bias_s, q_v, g_v, sems):
    copies = [
        pltpu.make_async_copy(src, dst, sems.at[i])
        for i, (src, dst) in enumerate(((list_ref, list_s), (bias_ref, bias_s), (q_ref, q_v), (g_ref, g_v)))
    ]
    for copy in copies:
        copy.start()
    for copy in copies:
        copy.wait()
    lane = iota((1, 128), 1)
    mask = jnp.zeros((1, 128), F32)
    for i in range(list_ref.shape[1]):
        mask = jnp.where(lane == list_s[0, i], 1.0, mask)
    bias = jnp.zeros((1, 128), F32)
    for i in range(16):
        bias = jnp.where(lane == i, bias_s[0, i], bias)
    high = bias.astype(BF16).astype(F32)
    middle = (bias - high).astype(BF16).astype(F32)
    last = bias - high - middle
    kind = iota((16, 128), 0) % 4
    meta = jnp.where(kind == 0, mask, jnp.where(kind == 1, high, jnp.where(kind == 2, middle, last)))
    meta = meta.astype(BF16)
    for to in range(16):
        out_ref[to, 0:64, 0:96] = q_v[...] if to % 2 == 0 else g_v[...]
        out_ref[to, 64:80, :] = meta


def turn_kernel(got_ref, out_ref):
    for part in range(4):
        for pair in range(2):
            both = jnp.concatenate([got_ref[pair * 8 + part, 0:64, :], got_ref[pair * 8 + 4 + part, 0:64, :]], axis=0)
            out_ref[part * FEAT : part * FEAT + FEAT, pair * 128 : pair * 128 + 128] = both.T[:FEAT, :]
    owner = iota((16, 128), 0) // 4
    meta = jnp.zeros((16, 128), F32)
    for zhi in range(4):
        meta = jnp.where(owner == zhi, got_ref[zhi * 4, 64:80, :].astype(F32), meta)
    out_ref[PART:HIGH, 0:128] = meta.astype(BF16)
    out_ref[PART:HIGH, 128:256] = meta.astype(BF16)


def stack_kernel(*refs):
    for k in range(4):
        refs[5 + k // 2][k % 2] = refs[k][...]


def tie_kernel(*refs):
    pass


def add_kernel(first_ref, second_ref, out_ref):
    out_ref[...] = first_ref[...] + second_ref[...]


def prepare_kernel(key_ref, value_ref, region_ref, key_out, value_out, hot_ref, key_v, value_v, sems):
    copies = [
        pltpu.make_async_copy(key_ref, key_v, sems.at[0]),
        pltpu.make_async_copy(value_ref, value_v, sems.at[1]),
    ]
    for copy in copies:
        copy.start()
    for block in range(NB):
        label = iota((256, BLOCK), 0)
        region = region_ref[:, block * BLOCK : (block + 1) * BLOCK]
        at = lax.axis_index(PATCH) * NB + block
        hot = (label == at) | ((label >= 96) & (label < 144) & (label % 16 == region))
        hot_ref[block * BLOCK : (block + 1) * BLOCK, :] = jnp.where(hot, 1.0, 0.0).T.astype(BF16)
    for copy, src, dst in zip(copies, (key_v, value_v), (key_out, value_out)):
        copy.wait()
        for x in range(4):
            low = src[:, x * 192 : x * 192 + 192]
            high = src[:, (4 + x) * 192 : (4 + x) * 192 + 192]
            dst[x] = jnp.concatenate([low, high], axis=1)


def place(back):
    return lax.rem(lax.axis_index("x") + 4 - back, 4), lax.rem(lax.axis_index("y") + 4 - back, 4)


def part(step, q_refs, g_refs, key_ref, value_ref, s_in, s_ref, dw_ref):
    x_at, y_at = place(step)
    total = jnp.zeros((TILES, WIDE), F32)
    for k in range(4):
        at = place(k)[1]
        term = jnp.dot(key_ref[x_at], q_refs[k // 2][k % 2, 0:PART, :], preferred_element_type=F32)
        s_ref[at] = term if s_in is None else s_in[at] + term
        total = total + jnp.dot(value_ref[place(k)[0]], g_refs[k // 2][k % 2, 0:PART, :], preferred_element_type=F32)
    dw_ref[y_at] = total


def by_core(body, planes):
    core = lax.axis_index("core")
    pl.when(core == 0)(lambda: body(planes[:2], planes[2:]))
    pl.when(core == 1)(lambda: body(planes[2:], planes[:2]))


def first_kernel(*refs):
    planes, (key_ref, value_ref, s_ref, dw_ref, table_ref) = refs[:4], refs[4:]
    group = iota((1, WIDE), 1) // ROWS

    def body(q_refs, g_refs):
        for k in range(4):
            meta = q_refs[k // 2][k % 2, PART:HIGH, 0:128].astype(F32).T
            parts = []
            for kind in range(4):
                height = 96 if kind == 0 else 16
                piece = jnp.zeros((height, WIDE), F32)
                for zhi in range(4):
                    piece = jnp.where(group == zhi, meta[:height, zhi * 4 + kind : zhi * 4 + kind + 1], piece)
                parts.append((piece - 1.0) * 1e30 if kind == 0 else piece)
            table = jnp.concatenate(parts + [jnp.zeros((112, WIDE), F32)], axis=0)
            table_ref[place(k)[1]] = table.astype(BF16)
        part(0, q_refs, g_refs, key_ref, value_ref, None, s_ref, dw_ref)

    by_core(body, planes)


def middle_kernel(step, *refs):
    planes, (key_ref, value_ref, s_in, dw_in, s_ref, dw_ref) = refs[:4], refs[4:]
    by_core(lambda q, g: part(step, q, g, key_ref, value_ref, s_in, s_ref, dw_ref), planes)


def end_kernel(*refs):
    planes, (key_ref, value_ref, table_ref, hot_ref, s_in, dw_in, s_ref, dw_ref, stat_ref) = refs[:4], refs[4:]
    by_core(lambda q, g: part(2, q, g, key_ref, value_ref, s_in, s_ref, dw_ref), planes)
    for k in range(4):
        s = s_ref[k] * SCALE + jnp.dot(hot_ref[...], table_ref[k], preferred_element_type=F32)
        top = jnp.max(s, axis=0, keepdims=True)
        e = jnp.where(s > -1e29, jnp.exp(s - top), 0.0)
        s_ref[k] = e
        total = jnp.sum(e, axis=0, keepdims=True)
        for to in range(16):
            stat_ref[to, k : k + 1, :] = top
            stat_ref[to, 4 + k : 5 + k, :] = total


def delta_kernel(e_ref, dw_ref, stat_ref, all_ref, delta_ref, factor_ref):
    tops = all_ref[:, 0:4, :]
    peak = jnp.max(tops, axis=0)
    whole = jnp.sum(all_ref[:, 4:8, :] * jnp.exp(tops - peak[None]), axis=0)
    factor_ref[...] = jnp.exp(stat_ref[0, 0:4, :] - peak) / whole

    def body(k, _):
        low = (e_ref[k] * factor_ref[pl.ds(k, 1), :]).astype(BF16).astype(F32)
        delta = jnp.sum(low * dw_ref[k], axis=0, keepdims=True)
        for to in range(16):
            delta_ref[to, pl.ds(k, 1), :] = delta
        return 0

    lax.fori_loop(0, 4, body, 0)


def own_rows(values_ref, other):
    y, zhi = lax.axis_index("y"), lax.axis_index("zhi")
    lanes = pl.ds(pl.multiple_of(lax.div(zhi, 2) * 128, 128), 128)
    both = lax.dot_general(values_ref[y, :, lanes], other, TN, preferred_element_type=F32)
    return jnp.where(lax.rem(zhi, 2) == 1, both[ROWS:], both[:ROWS])


def back_kernel(*refs):
    planes, refs = refs[:16], refs[16:]
    e_ref, dw_ref, factor_ref, deltas_ref, key_ref, value_ref, keep_ref, give_ref, gk_ref, gv_ref = refs[:10]
    low_ref, ds_ref, qm_ref, gm_ref = refs[10:]
    core, x_now = lax.axis_index("core"), lax.axis_index("x")
    delta = jnp.sum(deltas_ref[...], axis=0)
    for k in range(4):
        w = e_ref[k] * factor_ref[k : k + 1, :]
        low_ref[k] = w.astype(BF16)
        ds_ref[k] = (w * (dw_ref[k] - delta[k : k + 1, :])).astype(BF16)
    for x in range(4):
        mixed = own_rows(low_ref, value_ref[x])
        grads = own_rows(ds_ref, key_ref[x]) * SCALE
        both = jnp.concatenate([mixed, grads], axis=0).T
        for zlo in range(2):
            low, high = both[zlo * 192 : zlo * 192 + FEAT], both[zlo * 192 + FEAT : zlo * 192 + 192]
            keep_ref[zlo * 4 + x] = jnp.where(core == 0, low, high)
            give_ref[zlo * 4 + x] = jnp.where(core == 0, high, low)

    mine = lax.axis_index(LATENT)
    rows = pl.ds(pl.multiple_of((lax.div(mine, 8) * 2 + lax.rem(mine, 2)) * FEAT, 32), FEAT)
    back = lax.rem(x_now + 4 - lax.rem(lax.div(mine, 2), 4), 4)
    for side in range(2):
        for step in range(4):
            pair = planes[step * 4 + side * 2 : step * 4 + side * 2 + 2]

            def take_q(pair=pair):
                for k in range(4):
                    qm_ref[place(k)[1]] = pair[k // 2][k % 2, rows, :]

            def take_g(pair=pair, step=step):
                for half in range(2):

                    def take(half=half):
                        gm_ref[place(step)[1]] = pair[half][lax.rem(back, 2), rows, :]

                    pl.when(lax.div(back, 2) == half)(take)

            pl.when((core == side) & (back == step))(take_q)
            pl.when(core != side)(take_g)
    gk = jnp.zeros((FEAT, TILES), F32)
    gv = jnp.zeros((FEAT, TILES), F32)
    for k in range(4):
        gk = gk + lax.dot_general(qm_ref[k], ds_ref[k], NT, preferred_element_type=F32)
        gv = gv + lax.dot_general(gm_ref[k], low_ref[k], NT, preferred_element_type=F32)
    gk_ref[...] = (gk * SCALE).astype(BF16)
    gv_ref[...] = gv.astype(BF16)


def last_kernel(terms_ref, attended_ref, gq_ref):
    both = jnp.sum(terms_ref[...], axis=0).T
    attended_ref[...] = both[:ROWS].astype(BF16)
    gq_ref[...] = both[ROWS:].astype(BF16)


def call(kernel, outs, ins, args, scratch=(), flops=0, moved=0, limit=16, aliases=None):
    vmem = pl.BlockSpec(memory_space=pltpu.VMEM)
    specs = {"v": vmem, "V": vmem, "H": pl.BlockSpec(memory_space=pl.ANY), "a": pl.BlockSpec(memory_space=pl.ANY)}
    pins = {"V": pltpu.VMEM, "H": pltpu.HBM}
    shapes = [pltpu.VMEM(shape, kind) if c == "V" else jax.ShapeDtypeStruct(shape, kind) for c, shape, kind in outs]
    args = [pltpu.with_memory_space_constraint(a, pins[c]) if c in pins else a for c, a in zip(ins, args)]
    return pl.pallas_call(
        kernel,
        out_shape=shapes,
        in_specs=[specs[c] for c in ins],
        out_specs=[vmem] * len(outs),
        scratch_shapes=list(scratch),
        input_output_aliases=aliases or {},
        compiler_params=pltpu.CompilerParams(vmem_limit_bytes=limit * MIB),
        cost_estimate=pl.CostEstimate(flops=flops, bytes_accessed=moved, transcendentals=0),
    )(*args)


PLANE = [(x, core, y) for x in range(4) for core in range(2) for y in range(4)]


def along(value, stage, step):
    pairs = []
    for i, (x, core, y) in enumerate(PLANE):
        to = (x, core, (y + step) % 4) if core == stage else ((x + step) % 4, core, y)
        pairs.append((i, PLANE.index(to)))
    return lax.ppermute(value, ("x", "core", "y"), pairs)


def swap(value):
    return lax.ppermute(value, "core", [(0, 1), (1, 0)])


def shards(queries, tile_keys, tile_values, region_ids, block_list, region_bias, grad_out):
    dma = pltpu.SemaphoreType.DMA
    wide = (4, TILES, WIDE)
    sides = (4, TILES, PART)

    (packed,) = call(
        pack_kernel,
        [("v", (16, 80, 128), BF16)],
        "HHHH",
        (block_list, region_bias, queries, grad_out),
        [
            pltpu.SMEM(block_list.shape, jnp.int32),
            pltpu.SMEM(region_bias.shape, F32),
            pltpu.VMEM((ROWS, FEAT), BF16),
            pltpu.VMEM((ROWS, FEAT), BF16),
            dma((4,)),
        ],
    )
    got = lax.all_to_all(packed, ("zhi", "zlo", "core"), 0, 0)
    keys, values, hot = call(
        prepare_kernel,
        [("V", sides, BF16), ("V", sides, BF16), ("V", (TILES, 256), BF16)],
        "HHv",
        (tile_keys, tile_values, region_ids.reshape(1, TILES)),
        [pltpu.VMEM((TILES, D), BF16), pltpu.VMEM((TILES, D), BF16), dma((2,))],
        0,
        10_000_000,
    )
    (block,) = call(turn_kernel, [("v", (HIGH, WIDE), BF16)], "v", (got,))
    half = (2, HIGH, WIDE)
    line = call(
        stack_kernel,
        [("v", half, BF16)] * 2,
        "vvvva",
        [block, *(along(block, 0, k) for k in (1, 2, 3)), hot],
    )
    up = [along(piece, 1, 1) for piece in line]
    down = [along(piece, 1, 3) for piece in line]
    flops = 4 * TILES * 256 * D
    moved = 8_000_000
    planes = [[*line, *(swap(piece) for piece in line)]]
    s, dw, table = call(
        first_kernel,
        [("V", wide, F32), ("V", wide, F32), ("V", (4, 256, WIDE), BF16)],
        "vvvvVV",
        (*planes[0], keys, values),
        (),
        flops,
        moved,
    )
    up[0], down[1] = call(tie_kernel, [("V", half, BF16)] * 2, "VVa", (up[0], down[1], s), aliases={0: 0, 1: 1})
    across = [along(up[0], 1, 1), along(down[1], 1, 3)]
    for step, pair in ((1, up), (3, down)):
        planes.append([*pair, *(swap(piece) for piece in pair)])
        s, dw = call(
            functools.partial(middle_kernel, step),
            [("V", wide, F32), ("V", wide, F32)],
            "vvvvVVVV",
            (*planes[-1], keys, values, s, dw),
            (),
            flops,
            moved,
            aliases={6: 0, 7: 1},
        )
    across = call(tie_kernel, [("V", half, BF16)] * 2, "VVa", (*across, s), aliases={0: 0, 1: 1})
    planes.insert(2, [*across, *(swap(piece) for piece in across)])
    e, dw, stat = call(
        end_kernel,
        [("V", wide, F32), ("V", wide, F32), ("v", (16, 8, WIDE), F32)],
        "vvvvVVVVVV",
        (*planes[2], keys, values, table, hot, s, dw),
        (),
        flops,
        moved,
        aliases={8: 0, 9: 1},
    )
    stats = lax.all_to_all(stat, PATCH, 0, 0)
    delta, factor = call(
        delta_kernel,
        [("v", (16, 4, WIDE), F32), ("V", (4, WIDE), F32)],
        "VVvv",
        (e, dw, stat, stats),
        (),
        4 * TILES * 1024,
        8_000_000,
    )
    deltas = lax.all_to_all(delta, PATCH, 0, 0)
    eighth = (8, FEAT, 128)
    keep, give, grad_keys, grad_values = call(
        back_kernel,
        [("V", eighth, F32), ("v", eighth, F32), ("v", (FEAT, TILES), BF16), ("v", (FEAT, TILES), BF16)],
        "v" * 16 + "VVVvVV",
        (*planes[0], *planes[1], *planes[2], *planes[3], e, dw, factor, deltas, keys, values),
        [pltpu.VMEM(wide, BF16), pltpu.VMEM(wide, BF16), pltpu.VMEM((4, FEAT, WIDE), BF16), pltpu.VMEM((4, FEAT, WIDE), BF16)],
        4 * TILES * 1024 * FEAT,
        10_000_000,
    )
    (chip,) = call(add_kernel, [("v", eighth, F32)], "Vv", (keep, swap(give)))
    sums = lax.all_to_all(chip, ("zlo", "x"), 0, 0)
    attended, grad_queries = call(last_kernel, [("v", (ROWS, FEAT), BF16)] * 2, "v", (sums,))
    return (attended, grad_queries, grad_keys, grad_values)


def solution(mesh):
    fine = Mesh(mesh.devices.reshape(2, 4, 2, 4, 4), PATCH + LATENT)
    in_specs = (
        P(LATENT, PATCH),
        P(PATCH, None),
        P(PATCH, None),
        P(PATCH),
        P(LATENT, None),
        P(LATENT, None),
        P(LATENT, PATCH),
    )
    out_specs = (P(LATENT, PATCH),) * 4
    return jax.shard_map(shards, mesh=fine, in_specs=in_specs, out_specs=out_specs, check_vma=False)
```

time: 138 us -> 106 us (0.77)
  blocking collectives: 22.8 us -> 53.2 us
  waiting for transfers between devices: 35.4 us -> 14.2 us
  local copies, waits for them, and re-layouts: 19.9 us -> 0.69 us
  Pallas kernels: 30.7 us -> 19.5 us
  starting transfers between devices: 27.8 us -> 17.1 us
    all_to_all x0 -> x3, blocking collectives: none -> 30.3 us  [the longest x1 11.1 us: shards(): stats = lax.all_to_all(stat, PATCH, 0, 0)]
    unnamed x44 -> x0, local copies, waits for them, and re-layouts: 19.8 us -> none
    all_to_all x3 -> x0, starting transfers between devices: 15 us -> none  [the longest x1 5.86 us: shards(): sums = lax.all_to_all(terms.reshape(16, FEAT, 128), PATCH, 0, 0)]
    ppermute x6 -> x9, waiting for transfers between devices: 24.6 us -> 11 us  [along(): return lax.ppermute(value, ('x', 'core', 'y'), pairs)]
    pallas_call x11 -> x14, Pallas kernels: 30.7 us -> 19.5 us  [call(): pl.pallas_call(kernel, out_shape=shapes, in_specs=[specs[c] for c in ins]...]
    all_to_all x3 -> x0, waiting for transfers between devices: 10.8 us -> none  [the longest x1 10.8 us: shards(): sums = lax.all_to_all(terms.reshape(16, FEAT, 128), PATCH, 0, 0)]
    ppermute x4 -> x9, waiting for transfers between devices: 0.01 us -> 3.24 us  [swap(): return lax.ppermute(value, 'core', [(0, 1), (1, 0)])]
    ppermute x4 -> x9, starting transfers between devices: 5.61 us -> 7.76 us  [swap(): return lax.ppermute(value, 'core', [(0, 1), (1, 0)])]
  transfers between devices with their start and end apart: 13 -> 18, of which waited for: 6 -> 9; matrix products, arithmetic and copies ran while one was open for 0% -> 1% of each run, Pallas kernels for 10% -> 8%
where the time goes in v3:
time: 106 us; the launch traced here: 105 us
  blocking collectives  53.2 us (50%)
  Pallas kernels  19.5 us (18%)
  starting transfers between devices  17.1 us (16%)
  waiting for transfers between devices  14.2 us (13%)
    all_to_all x1, blocking collectives, shards(): got = lax.all_to_all(packed, ('zhi', 'zlo', 'core'), 0, 0)  22.8 us
    pallas_call x14, Pallas kernels, call(): pl.pallas_call(kernel, out_shape=shapes, in_specs=[specs[c] for c in ins]...  19.5 us
    all_to_all x1, blocking collectives, shards(): stats = lax.all_to_all(stat, PATCH, 0, 0)  11.1 us
    ppermute x9, waiting for transfers between devices, along(): return lax.ppermute(value, ('x', 'core', 'y'), pairs)  11 us
    all_to_all x1, blocking collectives, shards(): sums = lax.all_to_all(chip, ('zlo', 'x'), 0, 0)  10.3 us
    ppermute x9, starting transfers between devices, along(): return lax.ppermute(value, ('x', 'core', 'y'), pairs)  9.34 us
    all_to_all x1, blocking collectives, shards(): deltas = lax.all_to_all(delta, PATCH, 0, 0)  8.95 us
    ppermute x9, starting transfers between devices, swap(): return lax.ppermute(value, 'core', [(0, 1), (1, 0)])  7.76 us
  transfers between devices with their start and end apart: 18, of which 9 were waited for; matrix products, arithmetic and copies ran while one was open for 1% of the time, Pallas kernels for 8%

profile of v3, /device:TPU:1, one launch (start us, length us, event | category | flops | bytes accessed | tf_op | source)
XLA Modules:
  0.0 105.4 jit_solution(5889989113282291310)
XLA Ops:
  0.6 0.8 shard_map.102
  1.5 22.8 %all_to_all.20.got_ref = bf16[16,80,128]{2,1,0:T(8,128)(2,1)S(1)} all-to-all(bf16[16,80,128]{2,1,0:T(8,128)(2,1)S(1)} %shard_map.102), channel_id=1, replica_groups=mesh['zlo'=2,'x'=4,'core'=2,'zhi'=4,'y'=4] {'zhi','zlo','core'}, dimensions={0} | all-to-all | bytes 655360 | tf_op jit(solution)/shard_map/all_to_all | solution.py:297
  24.3 0.1 shard_map.103.refs_0_
  24.4 2.6 %collective-permute-start.2 = (bf16[400,256]{1,0:T(8,128)(2,1)S(1)}, bf16[400,256]{1,0:T(8,128)(2,1)S(1)}, u32[]{:S(2)}, u32[]{:S(2)}) collective-permute-start(bf16[400,256]{1,0:T(8,128)(2,1)S(1)} %shard_map.103.refs_0_), channel_id=1, source_target_pairs={{0,3},{1,0},{2,1},{3,2},{16,112},{17,113},{18,114},{19,115},{32,35... | collective-permute-start | bytes 614408 | tf_op jit(solution)/shard_map/ppermute | solution.py:272
  27.0 0.5 collective-permute-start.1
  27.5 0.6 collective-permute-start
  28.1 0.7 reshape.11.region_ref
  28.8 2.9 %shard_map.104 = (bf16[4,768,384]{2,1,0:T(8,128)(2,1)S(1)}, bf16[4,768,384]{2,1,0:T(8,128)(2,1)S(1)}, bf16[768,256]{1,0:T(8,128)(2,1)S(1)}) custom-call(bf16[768,1536]{1,0:T(8,128)(2,1)} %key_ref.1, bf16[768,1536]{1,0:T(8,128)(2,1)} %value_ref.1, s32[1,768]{1,0:T(1,128)S(1)} %reshape.11.region_ref), custom_call_target="tpu_custom_call" | custom-call | bytes 10000000 | tf_op jit(solution)/shard_map/pallas_call | solution.py:252
  31.7 0.2 collective-permute-done.2.refs_3_
  31.9 1.6 %collective-permute-done.1.refs_2_ = bf16[400,256]{1,0:T(8,128)(2,1)S(1)} collective-permute-done((bf16[400,256]{1,0:T(8,128)(2,1)S(1)}, bf16[400,256]{1,0:T(8,128)(2,1)S(1)}, u32[]{:S(2)}, u32[]{:S(2)}) %collective-permute-start.1) | collective-permute-done | bytes 204832 | tf_op jit(solution)/shard_map/ppermute | solution.py:272
  33.4 2.2 %collective-permute-done.refs_1_ = bf16[400,256]{1,0:T(8,128)(2,1)S(1)} collective-permute-done((bf16[400,256]{1,0:T(8,128)(2,1)S(1)}, bf16[400,256]{1,0:T(8,128)(2,1)S(1)}, u32[]{:S(2)}, u32[]{:S(2)}) %collective-permute-start) | collective-permute-done | bytes 204832 | tf_op jit(solution)/shard_map/ppermute | solution.py:272
  35.6 0.1 shard_map.105
  35.7 0.9 collective-permute-start.3
  36.6 0.3 collective-permute-start.7
  36.8 1.3 %collective-permute-start.4 = (bf16[2,400,256]{2,1,0:T(8,128)(2,1)S(1)}, bf16[2,400,256]{2,1,0:T(8,128)(2,1)S(1)}, u32[]{:S(2)}, u32[]{:S(2)}) collective-permute-start(bf16[2,400,256]{2,1,0:T(8,128)(2,1)S(1)} %get-tuple-element.33.refs_1_), channel_id=1, source_target_pairs={{0,16},{16,0},{1,17},{17,1},{2,18},{18,2},{3,19},{19,3},{4,20},{20... | collective-permute-start | bytes 1228808 | tf_op jit(solution)/shard_map/ppermute | solution.py:276
  38.1 0.0 collective-permute-start.5
  38.1 2.7 %collective-permute-start.6 = (bf16[2,400,256]{2,1,0:T(8,128)(2,1)S(1)}, bf16[2,400,256]{2,1,0:T(8,128)(2,1)S(1)}, u32[]{:S(2)}, u32[]{:S(2)}) collective-permute-start(bf16[2,400,256]{2,1,0:T(8,128)(2,1)S(1)} %get-tuple-element.33.refs_1_), channel_id=1, source_target_pairs={{0,96},{1,97},{2,98},{3,99},{16,19},{17,16},{18,17},{19,18},{32,0}... | collective-permute-start | bytes 1228808 | tf_op jit(solution)/shard_map/ppermute | solution.py:272
  40.8 0.0 collective-permute-done.3.refs_2_
  40.8 0.0 collective-permute-start.12
  40.9 4.0 %collective-permute-done.7.refs_1_.refs_5_ = bf16[2,400,256]{2,1,0:T(8,128)(2,1)S(1)} collective-permute-done((bf16[2,400,256]{2,1,0:T(8,128)(2,1)S(1)}, bf16[2,400,256]{2,1,0:T(8,128)(2,1)S(1)}, u32[]{:S(2)}, u32[]{:S(2)}) %collective-permute-start.7) | collective-permute-done | bytes 409632 | tf_op jit(solution)/shard_map/ppermute | solution.py:272
  44.9 0.9 collective-permute-start.9
  45.8 1.8 %shard_map.106 = (f32[4,768,256]{2,1,0:T(8,128)S(1)}, f32[4,768,256]{2,1,0:T(8,128)S(1)}, bf16[4,256,256]{2,1,0:T(8,128)(2,1)S(1)}) custom-call(bf16[2,400,256]{2,1,0:T(8,128)(2,1)S(1)} %get-tuple-element.32.refs_0_, bf16[2,400,256]{2,1,0:T(8,128)(2,1)S(1)} %get-tuple-element.33.refs_1_, bf16[2,400,256]{2,1,0:T(8,128)(2,1)S(1)} %collective-permute-done.3.refs_2_, ...), custom_call_target="tpu_custom_call" | custom-call | flops 1207959552 | bytes 8000000 | tf_op jit(solution)/shard_map/pallas_call | solution.py:252
  47.6 1.6 %collective-permute-done.5.refs_0_ = bf16[2,400,256]{2,1,0:T(8,128)(2,1)S(1)} collective-permute-done((bf16[2,400,256]{2,1,0:T(8,128)(2,1)S(1)}, bf16[2,400,256]{2,1,0:T(8,128)(2,1)S(1)}, u32[]{:S(2)}, u32[]{:S(2)}) %collective-permute-start.5) | collective-permute-done | bytes 409632 | tf_op jit(solution)/shard_map/ppermute | solution.py:272
  49.3 0.0 collective-permute-done.6.refs_1_
  49.3 0.9 collective-permute-start.8
  50.2 0.0 collective-permute-done.12.refs_0_.refs_12_
  50.2 1.8 %collective-permute-start.13 = (bf16[2,400,256]{2,1,0:T(8,128)(2,1)S(1)}, bf16[2,400,256]{2,1,0:T(8,128)(2,1)S(1)}, u32[]{:S(2)}, u32[]{:S(2)}) collective-permute-start(bf16[2,400,256]{2,1,0:T(8,128)(2,1)S(1)} %collective-permute-done.12.refs_0_.refs_12_), channel_id=1, source_target_pairs={{0,16},{16,0},{1,17},{17,1},{2,18},{18,2},{3,19},{19,3},{4,20},{20... | collective-permute-start | bytes 1228808 | tf_op jit(solution)/shard_map/ppermute | solution.py:276
  52.0 0.0 collective-permute-start.14
  52.0 0.0 collective-permute-start.10
  52.0 2.7 %collective-permute-start.11 = (bf16[2,400,256]{2,1,0:T(8,128)(2,1)S(1)}, bf16[2,400,256]{2,1,0:T(8,128)(2,1)S(1)}, u32[]{:S(2)}, u32[]{:S(2)}) collective-permute-start(bf16[2,400,256]{2,1,0:T(8,128)(2,1)S(1)} %get-tuple-element.38.refs_1_.refs_13_), channel_id=1, source_target_pairs={{0,96},{1,97},{2,98},{3,99},{16,19},{17,16},{18,17},{19,18},{32,0}... | collective-permute-start | bytes 1228808 | tf_op jit(solution)/shard_map/ppermute | solution.py:272
  54.7 2.1 %shard_map.108 = (f32[4,768,256]{2,1,0:T(8,128)S(1)}, f32[4,768,256]{2,1,0:T(8,128)S(1)}) custom-call(bf16[2,400,256]{2,1,0:T(8,128)(2,1)S(1)} %get-tuple-element.37.refs_0_.refs_4_, bf16[2,400,256]{2,1,0:T(8,128)(2,1)S(1)} %collective-permute-done.7.refs_1_.refs_5_, ...), custom_call_target="tpu_custom_call", output_to_operand_aliasing={{0}: (6, {}), {1}: (7, {})} | custom-call | flops 1207959552 | bytes 8000000 | tf_op jit(solution)/shard_map/pallas_call | solution.py:252
  56.8 0.0 collective-permute-done.14.refs_3_.refs_15_
  56.8 2.1 %shard_map.109 = (f32[4,768,256]{2,1,0:T(8,128)S(1)}, f32[4,768,256]{2,1,0:T(8,128)S(1)}) custom-call(bf16[2,400,256]{2,1,0:T(8,128)(2,1)S(1)} %collective-permute-done.12.refs_0_.refs_12_, bf16[2,400,256]{2,1,0:T(8,128)(2,1)S(1)} %get-tuple-element.38.refs_1_.refs_13_, ...), custom_call_target="tpu_custom_call", output_to_operand_aliasing={{0}: (6, {}), {1}: (7, {})} | custom-call | flops 1207959552 | bytes 8000000 | tf_op jit(solution)/shard_map/pallas_call | solution.py:252
  58.9 1.4 %collective-permute-done.10.refs_0_ = bf16[2,400,256]{2,1,0:T(8,128)(2,1)S(1)} collective-permute-done((bf16[2,400,256]{2,1,0:T(8,128)(2,1)S(1)}, bf16[2,400,256]{2,1,0:T(8,128)(2,1)S(1)}, u32[]{:S(2)}, u32[]{:S(2)}) %collective-permute-start.10) | collective-permute-done | bytes 409632 | tf_op jit(solution)/shard_map/ppermute | solution.py:272
  60.3 0.0 collective-permute-done.11.refs_1_
  60.3 1.4 %collective-permute-start.15 = (bf16[2,400,256]{2,1,0:T(8,128)(2,1)S(1)}, bf16[2,400,256]{2,1,0:T(8,128)(2,1)S(1)}, u32[]{:S(2)}, u32[]{:S(2)}) collective-permute-start(bf16[2,400,256]{2,1,0:T(8,128)(2,1)S(1)} %get-tuple-element.43.refs_0_.refs_8_), channel_id=1, source_target_pairs={{0,16},{16,0},{1,17},{17,1},{2,18},{18,2},{3,19},{19,3},{4,20},{20... | collective-permute-start | bytes 1228808 | tf_op jit(solution)/shard_map/ppermute | solution.py:276
  61.7 0.1 collective-permute-start.16
  61.7 1.3 %collective-permute-done.15.refs_2_.refs_10_ = bf16[2,400,256]{2,1,0:T(8,128)(2,1)S(1)} collective-permute-done((bf16[2,400,256]{2,1,0:T(8,128)(2,1)S(1)}, bf16[2,400,256]{2,1,0:T(8,128)(2,1)S(1)}, u32[]{:S(2)}, u32[]{:S(2)}) %collective-permute-start.15) | collective-permute-done | bytes 409632 | tf_op jit(solution)/shard_map/ppermute | solution.py:276
  63.0 0.6 collective-permute-done.16.refs_3_.refs_11_
  63.6 3.7 %shard_map.111 = (f32[4,768,256]{2,1,0:T(8,128)S(1)}, f32[4,768,256]{2,1,0:T(8,128)S(1)}, f32[16,8,256]{2,1,0:T(8,128)S(1)}) custom-call(bf16[2,400,256]{2,1,0:T(8,128)(2,1)S(1)} %get-tuple-element.43.refs_0_.refs_8_, bf16[2,400,256]{2,1,0:T(8,128)(2,1)S(1)} %get-tuple-element.44.refs_1_.refs_9_, ...), custom_call_target="tpu_custom_call", output_to_operand_aliasing={{0}: (8, {}), {1}: (9, {})} | custom-call | flops 1207959552 | bytes 8000000 | tf_op jit(solution)/shard_map/pallas_call | solution.py:252
  67.4 11.1 %all_to_all.21.all_ref = f32[16,8,256]{2,1,0:T(8,128)S(1)} all-to-all(f32[16,8,256]{2,1,0:T(8,128)S(1)} %get-tuple-element.49.stat_ref), channel_id=1, replica_groups=mesh['zlo'=2,'x'=4,'core'=2,'zhi'=4,'y'=4] {'zlo','x','core'}, dimensions={0} | all-to-all | bytes 262144 | tf_op jit(solution)/shard_map/all_to_all | solution.py:355
  78.4 1.2 %shard_map.112 = (f32[16,4,256]{2,1,0:T(4,128)S(1)}, f32[4,256]{1,0:T(4,128)S(1)}) custom-call(f32[4,768,256]{2,1,0:T(8,128)S(1)} %get-tuple-element.47.e_ref.refs_16_, f32[4,768,256]{2,1,0:T(8,128)S(1)} %get-tuple-element.48.dw_ref.refs_17_, f32[16,8,256]{2,1,0:T(8,128)S(1)} %get-tuple-element.49.stat_ref, f32[16,8,256]{2,1,0:T(8,128)S(1)} %all_to_all.21.all_ref), custom_call_target="tpu_custom_call" | custom-call | flops 3145728 | bytes 8000000 | tf_op jit(solution)/shard_map/pallas_call | solution.py:252
  79.6 8.9 %all_to_all.22.refs_19_ = f32[16,4,256]{2,1,0:T(4,128)S(1)} all-to-all(f32[16,4,256]{2,1,0:T(4,128)S(1)} %get-tuple-element.51), channel_id=1, replica_groups=mesh['zlo'=2,'x'=4,'core'=2,'zhi'=4,'y'=4] {'zlo','x','core'}, dimensions={0} | all-to-all | bytes 131072 | tf_op jit(solution)/shard_map/all_to_all | solution.py:365
  88.6 4.0 %shard_map.113 = (f32[8,96,128]{2,1,0:T(8,128)S(1)}, f32[8,96,128]{2,1,0:T(8,128)S(1)}, bf16[96,768]{1,0:T(8,128)(2,1)}, bf16[96,768]{1,0:T(8,128)(2,1)}) custom-call(bf16[2,400,256]{2,1,0:T(8,128)(2,1)S(1)} %get-tuple-element.32.refs_0_, bf16[2,400,256]{2,1,0:T(8,128)(2,1)S(1)} %get-tuple-element.33.refs_1_, ...), custom_call_target="tpu_custom_call" | custom-call | flops 301989888 | bytes 10000000 | tf_op jit(solution)/shard_map/pallas_call | solution.py:252
  92.6 0.4 collective-permute-start.17
  93.0 1.3 %collective-permute-done.17.second_ref = f32[8,96,128]{2,1,0:T(8,128)S(1)} collective-permute-done((f32[8,96,128]{2,1,0:T(8,128)S(1)}, f32[8,96,128]{2,1,0:T(8,128)S(1)}, u32[]{:S(2)}, u32[]{:S(2)}) %collective-permute-start.17) | collective-permute-done | bytes 393248 | tf_op jit(solution)/shard_map/ppermute | solution.py:276
  94.4 10.3 %all_to_all.23.terms_ref = f32[8,96,128]{2,1,0:T(8,128)S(1)} all-to-all(f32[8,96,128]{2,1,0:T(8,128)S(1)} %shard_map.114), channel_id=1, replica_groups=mesh['zlo'=2,'x'=4,'core'=2,'zhi'=4,'y'=4] {'zlo','x'}, dimensions={0} | all-to-all | bytes 786432 | tf_op jit(solution)/shard_map/all_to_all | solution.py:377
  104.7 0.7 shard_map.115
  (7 shorter events, 0.1 us)
Async XLA Ops:
  24.4 7.5 %collective-permute-start.2 = (bf16[400,256]{1,0:T(8,128)(2,1)S(1)}, bf16[400,256]{1,0:T(8,128)(2,1)S(1)}, u32[]{:S(2)}, u32[]{:S(2)}) collective-permute-start(bf16[400,256]{1,0:T(8,128)(2,1)S(1)} %shard_map.103.refs_0_), channel_id=1, source_target_pairs={{0,3},{1,0},{2,1},{3,2},{16,112},{17,113},{18,114},{19,115},{32,35... | collective-permute-start | bytes 614408 | tf_op jit(solution)/shard_map/ppermute | solution.py:272
  27.0 6.5 %collective-permute-start.1 = (bf16[400,256]{1,0:T(8,128)(2,1)S(1)}, bf16[400,256]{1,0:T(8,128)(2,1)S(1)}, u32[]{:S(2)}, u32[]{:S(2)}) collective-permute-start(bf16[400,256]{1,0:T(8,128)(2,1)S(1)} %shard_map.103.refs_0_), channel_id=1, source_target_pairs={{0,2},{1,3},{2,0},{3,1},{16,80},{17,81},{18,82},{19,83},{32,34},{3... | collective-permute-start | bytes 614408 | tf_op jit(solution)/shard_map/ppermute | solution.py:272
  27.5 8.1 %collective-permute-start = (bf16[400,256]{1,0:T(8,128)(2,1)S(1)}, bf16[400,256]{1,0:T(8,128)(2,1)S(1)}, u32[]{:S(2)}, u32[]{:S(2)}) collective-permute-start(bf16[400,256]{1,0:T(8,128)(2,1)S(1)} %shard_map.103.refs_0_), channel_id=1, source_target_pairs={{0,1},{1,2},{2,3},{3,0},{16,48},{17,49},{18,50},{19,51},{32,33},{3... | collective-permute-start | bytes 614408 | tf_op jit(solution)/shard_map/ppermute | solution.py:272
  35.7 5.2 %collective-permute-start.3 = (bf16[2,400,256]{2,1,0:T(8,128)(2,1)S(1)}, bf16[2,400,256]{2,1,0:T(8,128)(2,1)S(1)}, u32[]{:S(2)}, u32[]{:S(2)}) collective-permute-start(bf16[2,400,256]{2,1,0:T(8,128)(2,1)S(1)} %get-tuple-element.32.refs_0_), channel_id=1, source_target_pairs={{0,16},{16,0},{1,17},{17,1},{2,18},{18,2},{3,19},{19,3},{4,20},{20... | collective-permute-start | bytes 1228808 | tf_op jit(solution)/shard_map/ppermute | solution.py:276
  36.6 8.3 %collective-permute-start.7 = (bf16[2,400,256]{2,1,0:T(8,128)(2,1)S(1)}, bf16[2,400,256]{2,1,0:T(8,128)(2,1)S(1)}, u32[]{:S(2)}, u32[]{:S(2)}) collective-permute-start(bf16[2,400,256]{2,1,0:T(8,128)(2,1)S(1)} %get-tuple-element.33.refs_1_), channel_id=1, source_target_pairs={{0,32},{1,33},{2,34},{3,35},{16,17},{17,18},{18,19},{19,16},{32,64... | collective-permute-start | bytes 1228808 | tf_op jit(solution)/shard_map/ppermute | solution.py:272
  36.8 9.0 %collective-permute-start.4 = (bf16[2,400,256]{2,1,0:T(8,128)(2,1)S(1)}, bf16[2,400,256]{2,1,0:T(8,128)(2,1)S(1)}, u32[]{:S(2)}, u32[]{:S(2)}) collective-permute-start(bf16[2,400,256]{2,1,0:T(8,128)(2,1)S(1)} %get-tuple-element.33.refs_1_), channel_id=1, source_target_pairs={{0,16},{16,0},{1,17},{17,1},{2,18},{18,2},{3,19},{19,3},{4,20},{20... | collective-permute-start | bytes 1228808 | tf_op jit(solution)/shard_map/ppermute | solution.py:276
  38.1 11.1 %collective-permute-start.5 = (bf16[2,400,256]{2,1,0:T(8,128)(2,1)S(1)}, bf16[2,400,256]{2,1,0:T(8,128)(2,1)S(1)}, u32[]{:S(2)}, u32[]{:S(2)}) collective-permute-start(bf16[2,400,256]{2,1,0:T(8,128)(2,1)S(1)} %get-tuple-element.32.refs_0_), channel_id=1, source_target_pairs={{0,32},{1,33},{2,34},{3,35},{16,17},{17,18},{18,19},{19,16},{32,64... | collective-permute-start | bytes 1228808 | tf_op jit(solution)/shard_map/ppermute | solution.py:272
  38.1 11.1 %collective-permute-start.6 = (bf16[2,400,256]{2,1,0:T(8,128)(2,1)S(1)}, bf16[2,400,256]{2,1,0:T(8,128)(2,1)S(1)}, u32[]{:S(2)}, u32[]{:S(2)}) collective-permute-start(bf16[2,400,256]{2,1,0:T(8,128)(2,1)S(1)} %get-tuple-element.33.refs_1_), channel_id=1, source_target_pairs={{0,96},{1,97},{2,98},{3,99},{16,19},{17,16},{18,17},{19,18},{32,0}... | collective-permute-start | bytes 1228808 | tf_op jit(solution)/shard_map/ppermute | solution.py:272
  40.8 9.4 %collective-permute-start.12 = (bf16[2,400,256]{2,1,0:T(8,128)(2,1)S(1)}, bf16[2,400,256]{2,1,0:T(8,128)(2,1)S(1)}, u32[]{:S(2)}, u32[]{:S(2)}) collective-permute-start(bf16[2,400,256]{2,1,0:T(8,128)(2,1)S(1)} %get-tuple-element.32.refs_0_), channel_id=1, source_target_pairs={{0,96},{1,97},{2,98},{3,99},{16,19},{17,16},{18,17},{19,18},{32,0}... | collective-permute-start | bytes 1228808 | tf_op jit(solution)/shard_map/ppermute | solution.py:272
  44.9 7.1 %collective-permute-start.9 = (bf16[2,400,256]{2,1,0:T(8,128)(2,1)S(1)}, bf16[2,400,256]{2,1,0:T(8,128)(2,1)S(1)}, u32[]{:S(2)}, u32[]{:S(2)}) collective-permute-start(bf16[2,400,256]{2,1,0:T(8,128)(2,1)S(1)} %collective-permute-done.7.refs_1_.refs_5_), channel_id=1, source_target_pairs={{0,16},{16,0},{1,17},{17,1},{2,18},{18,2},{3,19},{19,3},{4,20},{20... | collective-permute-start | bytes 1228808 | tf_op jit(solution)/shard_map/ppermute | solution.py:276
  49.3 5.4 %collective-permute-start.8 = (bf16[2,400,256]{2,1,0:T(8,128)(2,1)S(1)}, bf16[2,400,256]{2,1,0:T(8,128)(2,1)S(1)}, u32[]{:S(2)}, u32[]{:S(2)}) collective-permute-start(bf16[2,400,256]{2,1,0:T(8,128)(2,1)S(1)} %get-tuple-element.37.refs_0_.refs_4_), channel_id=1, source_target_pairs={{0,16},{16,0},{1,17},{17,1},{2,18},{18,2},{3,19},{19,3},{4,20},{20... | collective-permute-start | bytes 1228808 | tf_op jit(solution)/shard_map/ppermute | solution.py:276
  50.2 6.6 %collective-permute-start.13 = (bf16[2,400,256]{2,1,0:T(8,128)(2,1)S(1)}, bf16[2,400,256]{2,1,0:T(8,128)(2,1)S(1)}, u32[]{:S(2)}, u32[]{:S(2)}) collective-permute-start(bf16[2,400,256]{2,1,0:T(8,128)(2,1)S(1)} %collective-permute-done.12.refs_0_.refs_12_), channel_id=1, source_target_pairs={{0,16},{16,0},{1,17},{17,1},{2,18},{18,2},{3,19},{19,3},{4,20},{20... | collective-permute-start | bytes 1228808 | tf_op jit(solution)/shard_map/ppermute | solution.py:276
  52.0 4.8 %collective-permute-start.14 = (bf16[2,400,256]{2,1,0:T(8,128)(2,1)S(1)}, bf16[2,400,256]{2,1,0:T(8,128)(2,1)S(1)}, u32[]{:S(2)}, u32[]{:S(2)}) collective-permute-start(bf16[2,400,256]{2,1,0:T(8,128)(2,1)S(1)} %get-tuple-element.38.refs_1_.refs_13_), channel_id=1, source_target_pairs={{0,16},{16,0},{1,17},{17,1},{2,18},{18,2},{3,19},{19,3},{4,20},{20... | collective-permute-start | bytes 1228808 | tf_op jit(solution)/shard_map/ppermute | solution.py:276
  52.0 8.3 %collective-permute-start.10 = (bf16[2,400,256]{2,1,0:T(8,128)(2,1)S(1)}, bf16[2,400,256]{2,1,0:T(8,128)(2,1)S(1)}, u32[]{:S(2)}, u32[]{:S(2)}) collective-permute-start(bf16[2,400,256]{2,1,0:T(8,128)(2,1)S(1)} %get-tuple-element.37.refs_0_.refs_4_), channel_id=1, source_target_pairs={{0,32},{1,33},{2,34},{3,35},{16,17},{17,18},{18,19},{19,16},{32,64... | collective-permute-start | bytes 1228808 | tf_op jit(solution)/shard_map/ppermute | solution.py:272
  52.0 8.3 %collective-permute-start.11 = (bf16[2,400,256]{2,1,0:T(8,128)(2,1)S(1)}, bf16[2,400,256]{2,1,0:T(8,128)(2,1)S(1)}, u32[]{:S(2)}, u32[]{:S(2)}) collective-permute-start(bf16[2,400,256]{2,1,0:T(8,128)(2,1)S(1)} %get-tuple-element.38.refs_1_.refs_13_), channel_id=1, source_target_pairs={{0,96},{1,97},{2,98},{3,99},{16,19},{17,16},{18,17},{19,18},{32,0}... | collective-permute-start | bytes 1228808 | tf_op jit(solution)/shard_map/ppermute | solution.py:272
  60.3 2.7 %collective-permute-start.15 = (bf16[2,400,256]{2,1,0:T(8,128)(2,1)S(1)}, bf16[2,400,256]{2,1,0:T(8,128)(2,1)S(1)}, u32[]{:S(2)}, u32[]{:S(2)}) collective-permute-start(bf16[2,400,256]{2,1,0:T(8,128)(2,1)S(1)} %get-tuple-element.43.refs_0_.refs_8_), channel_id=1, source_target_pairs={{0,16},{16,0},{1,17},{17,1},{2,18},{18,2},{3,19},{19,3},{4,20},{20... | collective-permute-start | bytes 1228808 | tf_op jit(solution)/shard_map/ppermute | solution.py:276
  61.7 2.0 %collective-permute-start.16 = (bf16[2,400,256]{2,1,0:T(8,128)(2,1)S(1)}, bf16[2,400,256]{2,1,0:T(8,128)(2,1)S(1)}, u32[]{:S(2)}, u32[]{:S(2)}) collective-permute-start(bf16[2,400,256]{2,1,0:T(8,128)(2,1)S(1)} %get-tuple-element.44.refs_1_.refs_9_), channel_id=1, source_target_pairs={{0,16},{16,0},{1,17},{17,1},{2,18},{18,2},{3,19},{19,3},{4,20},{20... | collective-permute-start | bytes 1228808 | tf_op jit(solution)/shard_map/ppermute | solution.py:276
  92.6 1.8 %collective-permute-start.17 = (f32[8,96,128]{2,1,0:T(8,128)S(1)}, f32[8,96,128]{2,1,0:T(8,128)S(1)}, u32[]{:S(2)}, u32[]{:S(2)}) collective-permute-start(f32[8,96,128]{2,1,0:T(8,128)S(1)} %get-tuple-element.53), channel_id=1, source_target_pairs={{0,16},{16,0},{1,17},{17,1},{2,18},{18,2},{3,19},{19,3},{4,20},{20... | collective-permute-start | bytes 1179656 | tf_op jit(solution)/shard_map/ppermute | solution.py:276

commit v4 on v3

v4 whole, which is shorter than its diff:
```python
import functools

import jax
import jax.numpy as jnp
from jax import lax
from jax.experimental import pallas as pl
from jax.experimental.pallas import tpu as pltpu
from jax.sharding import Mesh, PartitionSpec as P

BLOCK = 128
D = 1536
TILES = 768
ROWS = 64
FEAT = 96
NB = 6
WIDE = 256
PART = 384
SENT = 200
PATCH = ("zlo", "x", "core")
LATENT = ("zhi", "y")
SCALE = D ** (-0.5)
F32 = jnp.float32
BF16 = jnp.bfloat16
NT = (((1,), (1,)), ((), ()))
TN = (((0,), (0,)), ((), ()))
MIB = 1024 * 1024


def iota(shape, dim):
    return lax.broadcasted_iota(jnp.int32, shape, dim)


def pack_kernel(list_ref, bias_ref, q_ref, g_ref, out_ref, list_s, bias_s, q_v, g_v, sems):
    copies = [
        pltpu.make_async_copy(src, dst, sems.at[i])
        for i, (src, dst) in enumerate(((list_ref, list_s), (bias_ref, bias_s), (q_ref, q_v), (g_ref, g_v)))
    ]
    for copy in copies:
        copy.start()
    for copy in copies:
        copy.wait()
    lane = iota((1, 128), 1)
    mask = jnp.zeros((1, 128), F32)
    for i in range(list_ref.shape[1]):
        mask = jnp.where(lane == list_s[0, i], 1.0, mask)
    bias = jnp.zeros((1, 128), F32)
    for i in range(16):
        bias = jnp.where(lane == i, bias_s[0, i], bias)
    high = bias.astype(BF16).astype(F32)
    middle = (bias - high).astype(BF16).astype(F32)
    last = bias - high - middle
    kind = iota((16, 128), 0) % 4
    meta = jnp.where(kind == 0, mask, jnp.where(kind == 1, high, jnp.where(kind == 2, middle, last)))
    meta = meta.astype(BF16)
    for core, ref in ((0, q_v), (1, g_v)):
        tail = ref[48:64, :]
        side = jnp.concatenate([tail[:, 0:32], tail[:, 32:64], tail[:, 64:96]], axis=0)
        rows = jnp.concatenate([ref[0:48, :], side], axis=1)
        for to in range(core, 16, 2):
            out_ref[to, 0:48, :] = rows
            out_ref[to, 48:64, :] = meta


def turn_kernel(got_ref, out_ref, meta_ref):
    def opened(at):
        side = got_ref[at, 0:48, 96:128]
        tail = jnp.concatenate([side[0:16], side[16:32], side[32:48]], axis=1)
        return [got_ref[at, 0:48, 0:96], tail]

    for part in range(4):
        for pair in range(2):
            both = jnp.concatenate(opened(pair * 8 + part) + opened(pair * 8 + 4 + part), axis=0)
            out_ref[part * FEAT : part * FEAT + FEAT, pair * 128 : pair * 128 + 128] = both.T
    owner = iota((16, 128), 0) // 4
    meta = jnp.zeros((16, 128), F32)
    for zhi in range(4):
        meta = jnp.where(owner == zhi, got_ref[zhi * 4, 48:64, :].astype(F32), meta)
    meta_ref[...] = meta


def tie_kernel(*refs):
    pass


def prepare_kernel(key_ref, value_ref, region_ref, key_out, value_out, hot_ref, key_v, value_v, sems):
    copies = [
        pltpu.make_async_copy(key_ref, key_v, sems.at[0]),
        pltpu.make_async_copy(value_ref, value_v, sems.at[1]),
    ]
    for copy in copies:
        copy.start()
    for block in range(NB):
        label = iota((256, BLOCK), 0)
        region = region_ref[:, block * BLOCK : (block + 1) * BLOCK]
        at = lax.axis_index(PATCH) * NB + block
        hot = (label == at) | ((label >= 96) & (label < 144) & (label % 16 == region))
        hot_ref[block * BLOCK : (block + 1) * BLOCK, :] = jnp.where(hot, 1.0, 0.0).T.astype(BF16)
    for copy, src, dst in zip(copies, (key_v, value_v), (key_out, value_out)):
        copy.wait()
        for x in range(4):
            low = src[:, x * 192 : x * 192 + 192]
            high = src[:, (4 + x) * 192 : (4 + x) * 192 + 192]
            dst[x] = jnp.concatenate([low, high], axis=1)


def x_back(back):
    return lax.rem(lax.axis_index("x") + 4 - back, 4)


def products(table_ref, planes):
    total = jnp.zeros((TILES, WIDE), F32)
    for k in range(4):
        total = total + jnp.dot(table_ref[x_back(k)], planes[k][...], preferred_element_type=F32)
    return total


def own_slices(planes, out_ref):
    zhi = lax.axis_index("zhi")
    rows = pl.ds(pl.multiple_of(lax.div(zhi, 2) * 192, 64), 192)
    for half in range(2):
        back = lax.rem(lax.axis_index("x") + 4 - lax.rem(zhi, 2) * 2 - half, 4)
        for k in range(4):

            def take(k=k, half=half):
                out_ref[half] = planes[k][rows, :]

            pl.when(back == k)(take)


def near_kernel(*refs):
    planes, (key_ref, value_ref, acc_ref, mine_ref) = refs[:4], refs[4:]
    own_slices(planes, mine_ref)
    core = lax.axis_index("core")

    def work(table_ref):
        acc_ref[...] = products(table_ref, planes)

    pl.when(core == 0)(lambda: work(key_ref))
    pl.when(core == 1)(lambda: work(value_ref))


def far_kernel(*refs):
    planes, refs = refs[:4], refs[4:]
    key_ref, value_ref, hot_ref, meta_ref, acc_ref, mine_ref, e_ref, dw_ref, stat_ref, far_ref = refs
    own_slices(planes, far_ref)
    group = iota((1, WIDE), 1) // ROWS
    meta = meta_ref[...].T
    parts = []
    for kind in range(4):
        height = 96 if kind == 0 else 16
        piece = jnp.zeros((height, WIDE), F32)
        for zhi in range(4):
            piece = jnp.where(group == zhi, meta[:height, zhi * 4 + kind : zhi * 4 + kind + 1], piece)
        parts.append((piece - 1.0) * 1e30 if kind == 0 else piece)
    table = jnp.concatenate(parts + [jnp.zeros((112, WIDE), F32)], axis=0).astype(BF16)
    core = lax.axis_index("core")

    def work(table_ref, old_ref, new_ref):
        old_ref[...] = acc_ref[...]
        new_ref[...] = products(table_ref, planes)

    pl.when(core == 0)(lambda: work(value_ref, e_ref, dw_ref))
    pl.when(core == 1)(lambda: work(key_ref, dw_ref, e_ref))
    s = e_ref[...] * SCALE + jnp.dot(hot_ref[...], table, preferred_element_type=F32)
    top = jnp.max(s, axis=0, keepdims=True)
    e = jnp.where(s > -1e29, jnp.exp(s - top), 0.0)
    e_ref[...] = e
    dw = dw_ref[...]

    def down(value):
        return jnp.sum(value, axis=0, keepdims=True)

    first = jnp.max(e, axis=0, keepdims=True)
    second = jnp.max(jnp.where(e == first, 0.0, e), axis=0, keepdims=True)
    first_dw = down(jnp.where(e == first, dw, 0.0))
    second_dw = down(jnp.where(e == second, dw, 0.0))
    sent = [top, down(e), down(e * dw), first, first_dw, second, second_dw]
    for to in range(16):
        for i in range(7):
            stat_ref[to, i : i + 1, :] = sent[i]


def y_terms(mine_ref, weights_ref, terms_ref, which, own_ref, outs, scale):
    for half in range(2):
        both = lax.dot_general(mine_ref[half], weights_ref[...], NT, preferred_element_type=F32) * scale
        terms_ref[half * 2] = both[:FEAT]
        terms_ref[half * 2 + 1] = both[FEAT:]
    own_ref[which] = terms_ref[lax.axis_index("y")]
    largest = jnp.max(jnp.max(jnp.abs(terms_ref[...]), axis=0), axis=0, keepdims=True)
    largest = jnp.maximum(jnp.max(largest, axis=1, keepdims=True), 1e-30)
    exponent = jnp.ceil(jnp.log2(largest)) - 15.0
    factor = jnp.exp2(-exponent)
    for k in range(3):
        outs[k][which * FEAT : which * FEAT + FEAT, :] = terms_ref[lax.rem(lax.axis_index("y") + k + 1, 4)] * factor
    return exponent


def term_kernel(e_ref, dw_ref, stat_ref, all_ref, near_ref, far_ref, low_ref, ds_ref, *refs):
    tops, totals, products_, one, one_dw, two, two_dw = [all_ref[:, i, :] for i in range(7)]
    peak = jnp.max(tops, axis=0, keepdims=True)
    scale = jnp.exp(tops - peak)
    whole = jnp.sum(totals * scale, axis=0, keepdims=True)
    scale = scale / whole

    def rounding(value):
        weight = value * scale
        return weight.astype(BF16).astype(F32) - weight

    delta = products_ * scale + rounding(one) * one_dw + rounding(two) * two_dw
    delta = jnp.sum(delta, axis=0, keepdims=True)
    factor = jnp.exp(stat_ref[0, 0:1, :] - peak) / whole
    w = e_ref[...] * factor
    low_ref[...] = w.astype(BF16)
    ds_ref[...] = (w * (dw_ref[...] - delta)).astype(BF16)
    core = lax.axis_index("core")
    for i in range(2):
        refs[5][i] = jnp.where(core == 0, near_ref[i], far_ref[i])
        refs[6][i] = jnp.where(core == 0, far_ref[i], near_ref[i])
    first = y_terms(refs[5], ds_ref, refs[4], 0, refs[0], refs[1:4], SCALE)
    second = y_terms(refs[6], low_ref, refs[4], 1, refs[0], refs[1:4], 1.0)
    row = iota((8, TILES), 0)
    for k in range(3):
        refs[k + 1][2 * FEAT : SENT, :] = jnp.where(row == 0, first, jnp.where(row == 1, second, 0.0))


def own_rows(values_ref):
    zhi = lax.axis_index("zhi")
    lanes = pl.ds(pl.multiple_of(lax.div(zhi, 2) * 128, 128), 128)
    both = values_ref[:, lanes].T
    return jnp.where(lax.rem(zhi, 2) == 1, both[ROWS:], both[:ROWS])


def row_kernel(low_ref, ds_ref, key_ref, value_ref, keep_ref, give_ref):
    first = lax.axis_index("core") == 0
    own_low, own_ds = own_rows(low_ref), own_rows(ds_ref)
    for x in range(4):
        mixed = jnp.dot(own_low, value_ref[x], preferred_element_type=F32)
        grads = jnp.dot(own_ds, key_ref[x], preferred_element_type=F32) * SCALE
        both = jnp.concatenate([mixed, grads], axis=0).T
        for zlo in range(2):
            low, high = both[zlo * 192 : zlo * 192 + FEAT], both[zlo * 192 + FEAT : zlo * 192 + 192]
            keep_ref[zlo * 4 + x] = jnp.where(first, low, high)
            give_ref[zlo * 4 + x] = jnp.where(first, high, low)


def halve_kernel(keep_ref, got_ref, next_keep, next_give):
    zlo = lax.axis_index("zlo")
    for i in range(4):
        kept, given = zlo * 4 + i, 4 - zlo * 4 + i
        next_keep[i] = keep_ref[kept] + got_ref[kept]
        next_give[i] = keep_ref[given] + got_ref[given]


def quarter_kernel(keep_ref, got_ref, *outs):
    for k in range(4):
        at = lax.rem(lax.axis_index("x") + k, 4)
        outs[k][...] = keep_ref[at] + got_ref[at]


def last_kernel(own_ref, a_ref, b_ref, c_ref, *refs):
    rows, (attended_ref, gq_ref, gk_ref, gv_ref) = refs[:4], refs[4:]
    for which, out_ref in ((0, gk_ref), (1, gv_ref)):
        total = own_ref[which]
        for ref in (a_ref, b_ref, c_ref):
            scale = jnp.exp2(ref[2 * FEAT + which : 2 * FEAT + which + 1, :])
            total = total + ref[which * FEAT : which * FEAT + FEAT, :] * scale
        out_ref[...] = total.astype(BF16)
    both = (rows[0][...] + rows[1][...] + rows[2][...] + rows[3][...]).T
    attended_ref[...] = both[:ROWS].astype(BF16)
    gq_ref[...] = both[ROWS:].astype(BF16)


def call(kernel, outs, ins, args, scratch=(), flops=0, moved=0, limit=16, aliases=None):
    vmem = pl.BlockSpec(memory_space=pltpu.VMEM)
    specs = {"v": vmem, "V": vmem, "H": pl.BlockSpec(memory_space=pl.ANY), "a": pl.BlockSpec(memory_space=pl.ANY)}
    pins = {"V": pltpu.VMEM, "H": pltpu.HBM}
    shapes = [pltpu.VMEM(shape, kind) if c == "V" else jax.ShapeDtypeStruct(shape, kind) for c, shape, kind in outs]
    args = [pltpu.with_memory_space_constraint(a, pins[c]) if c in pins else a for c, a in zip(ins, args)]
    return pl.pallas_call(
        kernel,
        out_shape=shapes,
        in_specs=[specs[c] for c in ins],
        out_specs=[vmem] * len(outs),
        scratch_shapes=list(scratch),
        input_output_aliases=aliases or {},
        compiler_params=pltpu.CompilerParams(vmem_limit_bytes=limit * MIB),
        cost_estimate=pl.CostEstimate(flops=flops, bytes_accessed=moved, transcendentals=0),
    )(*args)


MOVES = [[(i, (i + k) % 4) for i in range(4)] for k in (1, 2, 3)]


def ring(value, axis):
    return [lax.ppermute(value, axis, move) for move in MOVES]


def swap(value):
    return lax.ppermute(value, "core", [(0, 1), (1, 0)])


def tie(arrays, after):
    outs = [("V", array.shape, array.dtype) for array in arrays]
    ins = "V" * len(arrays) + "a" * len(after)
    return call(tie_kernel, outs, ins, (*arrays, *after), aliases={i: i for i in range(len(arrays))})


def y_sends(terms):
    sent = [lax.ppermute(value.astype(jnp.float16), "y", move).astype(F32) for value, move in zip(terms, MOVES)]
    return [sent[i] for i in (0, 2, 1)]


def shards(queries, tile_keys, tile_values, region_ids, block_list, region_bias, grad_out):
    dma = pltpu.SemaphoreType.DMA
    wide = (TILES, WIDE)
    sides = (4, TILES, PART)
    flops = 2 * TILES * WIDE * D

    (packed,) = call(
        pack_kernel,
        [("v", (16, 64, 128), BF16)],
        "HHHH",
        (block_list, region_bias, queries, grad_out),
        [
            pltpu.SMEM(block_list.shape, jnp.int32),
            pltpu.SMEM(region_bias.shape, F32),
            pltpu.VMEM((ROWS, FEAT), BF16),
            pltpu.VMEM((ROWS, FEAT), BF16),
            dma((4,)),
        ],
    )
    got = lax.all_to_all(packed, ("zhi", "zlo", "core"), 0, 0)
    keys, values, hot = call(
        prepare_kernel,
        [("V", sides, BF16), ("V", sides, BF16), ("V", (TILES, 256), BF16)],
        "HHv",
        (tile_keys, tile_values, region_ids.reshape(1, TILES)),
        [pltpu.VMEM((TILES, D), BF16), pltpu.VMEM((TILES, D), BF16), dma((2,))],
        flops,
        10_000_000,
    )
    block, meta = call(turn_kernel, [("V", (PART, WIDE), BF16), ("V", (16, 128), F32)], "v", (got,))
    near = [block, *ring(block, "x")]
    (near[3],) = tie([near[3]], [hot])
    far = [swap(plane) for plane in near]

    slices = (2, 192, WIDE)
    term = (2, FEAT, TILES)
    acc, near_mine = call(
        near_kernel,
        [("V", wide, F32), ("V", slices, BF16)],
        "v" * 4 + "VV",
        (*near, keys, values),
        (),
        flops,
        5_000_000,
    )
    e, dw, stat, far_mine = call(
        far_kernel,
        [("V", wide, F32), ("V", wide, F32), ("v", (16, 7, WIDE), F32), ("V", slices, BF16)],
        "v" * 4 + "VVVVVV",
        (*far, keys, values, hot, meta, acc, near_mine),
        (),
        flops,
        5_000_000,
    )
    stats = lax.all_to_all(stat, PATCH, 0, 0)
    low, ds, own, *terms = call(
        term_kernel,
        [("V", wide, BF16), ("V", wide, BF16), ("V", (2, FEAT, TILES), F32)] + [("V", (SENT, TILES), F32)] * 3,
        "VVvvVV",
        (e, dw, stat, stats, near_mine, far_mine),
        [pltpu.VMEM((4, FEAT, TILES), F32), pltpu.VMEM(slices, BF16), pltpu.VMEM(slices, BF16)],
        flops // 2,
        8_000_000,
    )
    terms = y_sends(terms)
    keep, give = call(
        row_kernel,
        [("V", (8, FEAT, 128), F32), ("V", (8, FEAT, 128), F32)],
        "VVVV",
        (low, ds, keys, values),
        (),
        flops // 4,
        4_000_000,
    )
    half = ("V", (4, FEAT, 128), F32)
    keep, give = call(halve_kernel, [half, half], "VV", (keep, swap(give)))
    got = lax.ppermute(give, "zlo", [(0, 1), (1, 0)])
    rows = call(quarter_kernel, [("V", (FEAT, 128), F32)] * 4, "VV", (keep, got))
    rows = [rows[0]] + [lax.ppermute(value, "x", move) for value, move in zip(rows[1:], MOVES)]
    attended, grad_queries, grad_keys, grad_values = call(
        last_kernel,
        [("v", (ROWS, FEAT), BF16)] * 2 + [("v", (FEAT, TILES), BF16)] * 2,
        "VvvvVVVV",
        (own, *terms, *rows),
    )
    return (attended, grad_queries, grad_keys, grad_values)


def solution(mesh):
    fine = Mesh(mesh.devices.reshape(2, 4, 2, 4, 4), PATCH + LATENT)
    in_specs = (
        P(LATENT, PATCH),
        P(PATCH, None),
        P(PATCH, None),
        P(PATCH),
        P(LATENT, None),
        P(LATENT, None),
        P(LATENT, PATCH),
    )
    out_specs = (P(LATENT, PATCH),) * 4
    return jax.shard_map(shards, mesh=fine, in_specs=in_specs, out_specs=out_specs, check_vma=False)
```

time: 106 us -> 72 us (0.68)
  blocking collectives: 53.2 us -> 31.5 us
  Pallas kernels: 19.5 us -> 10.5 us
  starting transfers between devices: 17.1 us -> 15.1 us
  waiting for transfers between devices: 14.2 us -> 12.8 us
    all_to_all x2 -> x0, blocking collectives: 19.3 us -> none  [the longest x1 10.3 us: shards(): sums = lax.all_to_all(chip, ('zlo', 'x'), 0, 0)]
    pallas_call x14 -> x11, Pallas kernels: 19.5 us -> 10.5 us  [call(): pl.pallas_call(kernel, out_shape=shapes, in_specs=[specs[c] for c in ins]...]
    ppermute x9 -> x5, starting transfers between devices: 7.76 us -> 1.88 us  [swap(): return lax.ppermute(value, 'core', [(0, 1), (1, 0)])]
    ppermute x9 -> x10, starting transfers between devices: 9.34 us -> 13.2 us  [the longest x3 5.51 us: ring(): return [lax.ppermute(value, axis, move) for move in MOVES]]
    ppermute x9 -> x5, waiting for transfers between devices: 3.24 us -> 0.33 us  [swap(): return lax.ppermute(value, 'core', [(0, 1), (1, 0)])]
    ppermute x9 -> x10, waiting for transfers between devices: 11 us -> 12.5 us  [the longest x1 5.28 us: shards(): got = lax.ppermute(give, 'zlo', [(0, 1), (1, 0)])]
    all_to_all x1, blocking collectives: 22.8 us -> 21.5 us  [shards(): got = lax.all_to_all(packed, ('zhi', 'zlo', 'core'), 0, 0)]
    all_to_all x1, blocking collectives: 11.1 us -> 9.98 us  [shards(): stats = lax.all_to_all(stat, PATCH, 0, 0)]
  transfers between devices with their start and end apart: 18 -> 15, of which waited for: 9 -> 4; matrix products, arithmetic and copies ran while one was open for 1% -> 1% of each run, Pallas kernels for 8% -> 5%
where the time goes in v4:
time: 72 us; the launch traced here: 71.7 us
  blocking collectives  31.5 us (44%)
  starting transfers between devices  15.1 us (21%)
  waiting for transfers between devices  12.8 us (18%)
  Pallas kernels  10.5 us (15%)
  between operations  0.79 us (1%)
    all_to_all x1, blocking collectives, shards(): got = lax.all_to_all(packed, ('zhi', 'zlo', 'core'), 0, 0)  21.5 us
    pallas_call x11, Pallas kernels, call(): pl.pallas_call(kernel, out_shape=shapes, in_specs=[specs[c] for c in ins]...  10.5 us
    all_to_all x1, blocking collectives, shards(): stats = lax.all_to_all(stat, PATCH, 0, 0)  9.98 us
    ppermute x3, starting transfers between devices, ring(): return [lax.ppermute(value, axis, move) for move in MOVES]  5.51 us
    ppermute x1, waiting for transfers between devices, shards(): got = lax.ppermute(give, 'zlo', [(0, 1), (1, 0)])  5.28 us
    ppermute x3, starting transfers between devices, y_sends(): lax.ppermute(value.astype(jnp.float16), 'y', move).astype(F32)  4.62 us
    ppermute x3, waiting for transfers between devices, y_sends(): lax.ppermute(value.astype(jnp.float16), 'y', move).astype(F32)  4.23 us
    ppermute x3, waiting for transfers between devices, ring(): return [lax.ppermute(value, axis, move) for move in MOVES]  3 us
  transfers between devices with their start and end apart: 15, of which 4 were waited for; matrix products, arithmetic and copies ran while one was open for 1% of the time, Pallas kernels for 5%

profile of v4, /device:TPU:1, one launch (start us, length us, event | category | flops | bytes accessed | tf_op | source)
XLA Modules:
  0.0 71.7 jit_solution(18081645589923263117)
XLA Ops:
  0.6 0.9 %shard_map.102 = bf16[16,64,128]{2,1,0:T(8,128)(2,1)S(1)} custom-call(s32[1,80]{1,0:T(1,128)} %list_ref.1, f32[1,16]{1,0:T(1,128)} %bias_ref.1, bf16[64,96]{1,0:T(8,128)(2,1)} %q_ref.1, bf16[64,96]{1,0:T(8,128)(2,1)} %g_ref.1), custom_call_target="tpu_custom_call" | custom-call | tf_op jit(solution)/shard_map/pallas_call | solution.py:279
  1.6 21.5 %all_to_all.10.got_ref = bf16[16,64,128]{2,1,0:T(8,128)(2,1)S(1)} all-to-all(bf16[16,64,128]{2,1,0:T(8,128)(2,1)S(1)} %shard_map.102), channel_id=1, replica_groups=mesh['zlo'=2,'x'=4,'core'=2,'zhi'=4,'y'=4] {'zhi','zlo','core'}, dimensions={0} | all-to-all | bytes 524288 | tf_op jit(solution)/shard_map/all_to_all | solution.py:332
  23.1 0.3 shard_map.103
  23.3 2.8 %collective-permute-start.3 = (bf16[384,256]{1,0:T(8,128)(2,1)S(1)}, bf16[384,256]{1,0:T(8,128)(2,1)S(1)}, u32[]{:S(2)}, u32[]{:S(2)}) collective-permute-start(bf16[384,256]{1,0:T(8,128)(2,1)S(1)} %get-tuple-element.29.refs_0_), channel_id=1, source_target_pairs={{0,64},{32,96},{64,0},{96,32},{1,65},{33,97},{65,1},{97,33},{2,66}... | collective-permute-start | bytes 589832 | tf_op jit(solution)/shard_map/ppermute | solution.py:295
  26.1 0.3 collective-permute-start.1
  26.5 2.4 %collective-permute-start.5 = (bf16[384,256]{1,0:T(8,128)(2,1)S(1)}, bf16[384,256]{1,0:T(8,128)(2,1)S(1)}, u32[]{:S(2)}, u32[]{:S(2)}) collective-permute-start(bf16[384,256]{1,0:T(8,128)(2,1)S(1)} %get-tuple-element.29.refs_0_), channel_id=1, source_target_pairs={{0,96},{32,0},{64,32},{96,64},{1,97},{33,1},{65,33},{97,65},{2,98}... | collective-permute-start | bytes 589832 | tf_op jit(solution)/shard_map/ppermute | solution.py:295
  28.8 0.7 reshape.11.region_ref
  29.5 2.9 %shard_map.104 = (bf16[4,768,384]{2,1,0:T(8,128)(2,1)S(1)}, bf16[4,768,384]{2,1,0:T(8,128)(2,1)S(1)}, bf16[768,256]{1,0:T(8,128)(2,1)S(1)}) custom-call(bf16[768,1536]{1,0:T(8,128)(2,1)} %key_ref.1, bf16[768,1536]{1,0:T(8,128)(2,1)} %value_ref.1, s32[1,768]{1,0:T(1,128)S(1)} %reshape.11.region_ref), custom_call_target="tpu_custom_call" | custom-call | flops 603979776 | bytes 10000000 | tf_op jit(solution)/shard_map/pallas_call | solution.py:279
  32.4 0.5 collective-permute-start
  32.9 0.0 collective-permute-done.3.refs_2_
  32.9 0.1 collective-permute-start.4
  33.0 3.0 %collective-permute-done.1.refs_1_ = bf16[384,256]{1,0:T(8,128)(2,1)S(1)} collective-permute-done((bf16[384,256]{1,0:T(8,128)(2,1)S(1)}, bf16[384,256]{1,0:T(8,128)(2,1)S(1)}, u32[]{:S(2)}, u32[]{:S(2)}) %collective-permute-start.1) | collective-permute-done | bytes 196640 | tf_op jit(solution)/shard_map/ppermute | solution.py:295
  36.0 0.4 collective-permute-start.2
  36.4 0.0 collective-permute-done.5.refs_0_
  36.4 0.1 collective-permute-start.6
  36.5 1.0 %shard_map.106 = (f32[768,256]{1,0:T(8,128)S(1)}, bf16[2,192,256]{2,1,0:T(8,128)(2,1)S(1)}) custom-call(bf16[384,256]{1,0:T(8,128)(2,1)S(1)} %get-tuple-element.29.refs_0_, bf16[384,256]{1,0:T(8,128)(2,1)S(1)} %collective-permute-done.1.refs_1_, bf16[384,256]{1,0:T(8,128)(2,1)S(1)} %collective-permute-done.3.refs_2_, ...), custom_call_target="tpu_custom_call" | custom-call | flops 603979776 | bytes 5000000 | tf_op jit(solution)/shard_map/pallas_call | solution.py:279
  37.5 0.0 collective-permute-done.refs_0_
  37.5 0.0 collective-permute-done.4.refs_2_
  37.6 0.0 collective-permute-done.2.refs_1_
  37.6 0.3 collective-permute-done.6.refs_3_
  37.9 2.2 %shard_map.107 = (f32[768,256]{1,0:T(8,128)S(1)}, f32[768,256]{1,0:T(8,128)S(1)}, f32[16,7,256]{2,1,0:T(8,128)S(1)}, bf16[2,192,256]{2,1,0:T(8,128)(2,1)S(1)}) custom-call(bf16[384,256]{1,0:T(8,128)(2,1)S(1)} %collective-permute-done.refs_0_, bf16[384,256]{1,0:T(8,128)(2,1)S(1)} %collective-permute-done.2.refs_1_, ...), custom_call_target="tpu_custom_call" | custom-call | flops 603979776 | bytes 5000000 | tf_op jit(solution)/shard_map/pallas_call | solution.py:279
  40.1 10.0 %all_to_all.11.all_ref = f32[16,7,256]{2,1,0:T(8,128)S(1)} all-to-all(f32[16,7,256]{2,1,0:T(8,128)S(1)} %get-tuple-element.38.stat_ref), channel_id=1, replica_groups=mesh['zlo'=2,'x'=4,'core'=2,'zhi'=4,'y'=4] {'zlo','x','core'}, dimensions={0} | all-to-all | bytes 229376 | tf_op jit(solution)/shard_map/all_to_all | solution.py:367
  50.1 1.2 %shard_map.108 = (bf16[768,256]{1,0:T(8,128)(2,1)S(1)}, bf16[768,256]{1,0:T(8,128)(2,1)S(1)}, f32[2,96,768]{2,1,0:T(8,128)S(1)}, f32[200,768]{1,0:T(8,128)S(1)},...) custom-call(f32[768,256]{1,0:T(8,128)S(1)} %get-tuple-element.36.e_ref, f32[768,256]{1,0:T(8,128)S(1)} %get-tuple-element.37.dw_ref, ...), custom_call_target="tpu_custom_call" | custom-call | flops 301989888 | bytes 8000000 | tf_op jit(solution)/shard_map/pallas_call | solution.py:279
  51.3 1.0 %shard_map.109 = (f32[8,96,128]{2,1,0:T(8,128)S(1)}, f32[8,96,128]{2,1,0:T(8,128)S(1)}) custom-call(bf16[768,256]{1,0:T(8,128)(2,1)S(1)} %get-tuple-element.44.low_ref, bf16[768,256]{1,0:T(8,128)(2,1)S(1)} %get-tuple-element.45.ds_ref, bf16[4,768,384]{2,1,0:T(8,128)(2,1)S(1)} %get-tuple-element.31.refs_4_.key_ref, ...), custom_call_target="tpu_custom_call" | custom-call | flops 150994944 | bytes 4000000 | tf_op jit(solution)/shard_map/pallas_call | solution.py:279
  52.4 0.8 %collective-permute-start.10 = (f32[8,96,128]{2,1,0:T(8,128)S(1)}, f32[8,96,128]{2,1,0:T(8,128)S(1)}, u32[]{:S(2)}, u32[]{:S(2)}) collective-permute-start(f32[8,96,128]{2,1,0:T(8,128)S(1)} %get-tuple-element.47), channel_id=1, source_target_pairs={{0,16},{16,0},{1,17},{17,1},{2,18},{18,2},{3,19},{19,3},{4,20},{20... | collective-permute-start | bytes 1179656 | tf_op jit(solution)/shard_map/ppermute | solution.py:299
  53.2 3.0 %collective-permute-start.9 = (f16[200,768]{1,0:T(8,128)(2,1)S(1)}, f16[200,768]{1,0:T(8,128)(2,1)S(1)}, u32[]{:S(2)}, u32[]{:S(2)}) collective-permute-start(f16[200,768]{1,0:T(8,128)(2,1)S(1)} %convert_element_type.22), channel_id=1, source_target_pairs={{0,2},{1,3},{2,0},{3,1},{4,6},{5,7},{6,4},{7,5},{8,10},{9,11},{10,... | collective-permute-start | bytes 921608 | tf_op jit(solution)/shard_map/ppermute | solution.py:309
  56.2 0.8 %collective-permute-start.8 = (f16[200,768]{1,0:T(8,128)(2,1)S(1)}, f16[200,768]{1,0:T(8,128)(2,1)S(1)}, u32[]{:S(2)}, u32[]{:S(2)}) collective-permute-start(f16[200,768]{1,0:T(8,128)(2,1)S(1)} %convert_element_type.20), channel_id=1, source_target_pairs={{0,3},{1,0},{2,1},{3,2},{4,7},{5,4},{6,5},{7,6},{8,11},{9,8},{10,9... | collective-permute-start | bytes 921608 | tf_op jit(solution)/shard_map/ppermute | solution.py:309
  57.1 0.8 %collective-permute-start.7 = (f16[200,768]{1,0:T(8,128)(2,1)S(1)}, f16[200,768]{1,0:T(8,128)(2,1)S(1)}, u32[]{:S(2)}, u32[]{:S(2)}) collective-permute-start(f16[200,768]{1,0:T(8,128)(2,1)S(1)} %convert_element_type.18), channel_id=1, source_target_pairs={{0,1},{1,2},{2,3},{3,0},{4,5},{5,6},{6,7},{7,4},{8,9},{9,10},{10,1... | collective-permute-start | bytes 921608 | tf_op jit(solution)/shard_map/ppermute | solution.py:309
  57.9 0.0 collective-permute-done.10.got_ref
  57.9 0.4 collective-permute-start.11
  58.3 5.3 %collective-permute-done.11.got_ref = f32[4,96,128]{2,1,0:T(8,128)S(1)} collective-permute-done((f32[4,96,128]{2,1,0:T(8,128)S(1)}, f32[4,96,128]{2,1,0:T(8,128)S(1)}, u32[]{:S(2)}, u32[]{:S(2)}) %collective-permute-start.11) | collective-permute-done | bytes 196640 | tf_op jit(solution)/shard_map/ppermute | solution.py:389
  63.6 0.1 collective-permute-start.12
  63.7 1.8 %collective-permute-start.13 = (f32[96,128]{1,0:T(8,128)S(1)}, f32[96,128]{1,0:T(8,128)S(1)}, u32[]{:S(2)}, u32[]{:S(2)}) collective-permute-start(f32[96,128]{1,0:T(8,128)S(1)} %get-tuple-element.52), channel_id=1, source_target_pairs={{0,64},{32,96},{64,0},{96,32},{1,65},{33,97},{65,1},{97,33},{2,66}... | collective-permute-start | bytes 147464 | tf_op jit(solution)/shard_map/ppermute | solution.py:391
  65.5 0.0 collective-permute-done.9
  65.5 0.9 %collective-permute-start.14 = (f32[96,128]{1,0:T(8,128)S(1)}, f32[96,128]{1,0:T(8,128)S(1)}, u32[]{:S(2)}, u32[]{:S(2)}) collective-permute-start(f32[96,128]{1,0:T(8,128)S(1)} %get-tuple-element.53), channel_id=1, source_target_pairs={{0,96},{32,0},{64,32},{96,64},{1,97},{33,1},{65,33},{97,65},{2,98}... | collective-permute-start | bytes 147464 | tf_op jit(solution)/shard_map/ppermute | solution.py:391
  66.4 4.2 %collective-permute-done.8 = f16[200,768]{1,0:T(8,128)(2,1)S(1)} collective-permute-done((f16[200,768]{1,0:T(8,128)(2,1)S(1)}, f16[200,768]{1,0:T(8,128)(2,1)S(1)}, u32[]{:S(2)}, u32[]{:S(2)}) %collective-permute-start.8) | collective-permute-done | bytes 307232 | tf_op jit(solution)/shard_map/ppermute | solution.py:309
  70.7 0.0 collective-permute-done.7
  70.7 0.0 collective-permute-done.12.refs_1_
  70.7 0.0 collective-permute-done.13.refs_2_
  70.8 0.0 collective-permute-done.14.refs_3_
  70.8 0.9 %shard_map.112 = (bf16[64,96]{1,0:T(8,128)(2,1)}, bf16[64,96]{1,0:T(8,128)(2,1)}, bf16[96,768]{1,0:T(8,128)(2,1)}, bf16[96,768]{1,0:T(8,128)(2,1)}) custom-call(f32[2,96,768]{2,1,0:T(8,128)S(1)} %get-tuple-element.40.own_ref, f32[200,768]{1,0:T(8,128)S(1)} %convert_element_type.19.a_ref, f32[200,768]{1,0:T(8,128)S(1)} %convert_element_type.21.b_ref, ...), custom_call_target="tpu_custom_call" | custom-call | tf_op jit(solution)/shard_map/pallas_call | solution.py:279
  (9 shorter events, 0.3 us)
Async XLA Ops:
  23.3 9.6 %collective-permute-start.3 = (bf16[384,256]{1,0:T(8,128)(2,1)S(1)}, bf16[384,256]{1,0:T(8,128)(2,1)S(1)}, u32[]{:S(2)}, u32[]{:S(2)}) collective-permute-start(bf16[384,256]{1,0:T(8,128)(2,1)S(1)} %get-tuple-element.29.refs_0_), channel_id=1, source_target_pairs={{0,64},{32,96},{64,0},{96,32},{1,65},{33,97},{65,1},{97,33},{2,66}... | collective-permute-start | bytes 589832 | tf_op jit(solution)/shard_map/ppermute | solution.py:295
  26.1 9.9 %collective-permute-start.1 = (bf16[384,256]{1,0:T(8,128)(2,1)S(1)}, bf16[384,256]{1,0:T(8,128)(2,1)S(1)}, u32[]{:S(2)}, u32[]{:S(2)}) collective-permute-start(bf16[384,256]{1,0:T(8,128)(2,1)S(1)} %get-tuple-element.29.refs_0_), channel_id=1, source_target_pairs={{0,32},{32,64},{64,96},{96,0},{1,33},{33,65},{65,97},{97,1},{2,34}... | collective-permute-start | bytes 589832 | tf_op jit(solution)/shard_map/ppermute | solution.py:295
  26.5 10.0 %collective-permute-start.5 = (bf16[384,256]{1,0:T(8,128)(2,1)S(1)}, bf16[384,256]{1,0:T(8,128)(2,1)S(1)}, u32[]{:S(2)}, u32[]{:S(2)}) collective-permute-start(bf16[384,256]{1,0:T(8,128)(2,1)S(1)} %get-tuple-element.29.refs_0_), channel_id=1, source_target_pairs={{0,96},{32,0},{64,32},{96,64},{1,97},{33,1},{65,33},{97,65},{2,98}... | collective-permute-start | bytes 589832 | tf_op jit(solution)/shard_map/ppermute | solution.py:295
  32.4 5.1 %collective-permute-start = (bf16[384,256]{1,0:T(8,128)(2,1)S(1)}, bf16[384,256]{1,0:T(8,128)(2,1)S(1)}, u32[]{:S(2)}, u32[]{:S(2)}) collective-permute-start(bf16[384,256]{1,0:T(8,128)(2,1)S(1)} %get-tuple-element.29.refs_0_), channel_id=1, source_target_pairs={{0,16},{16,0},{1,17},{17,1},{2,18},{18,2},{3,19},{19,3},{4,20},{20... | collective-permute-start | bytes 589832 | tf_op jit(solution)/shard_map/ppermute | solution.py:299
  32.9 4.6 %collective-permute-start.4 = (bf16[384,256]{1,0:T(8,128)(2,1)S(1)}, bf16[384,256]{1,0:T(8,128)(2,1)S(1)}, u32[]{:S(2)}, u32[]{:S(2)}) collective-permute-start(bf16[384,256]{1,0:T(8,128)(2,1)S(1)} %collective-permute-done.3.refs_2_), channel_id=1, source_target_pairs={{0,16},{16,0},{1,17},{17,1},{2,18},{18,2},{3,19},{19,3},{4,20},{20... | collective-permute-start | bytes 589832 | tf_op jit(solution)/shard_map/ppermute | solution.py:299
  36.0 1.5 %collective-permute-start.2 = (bf16[384,256]{1,0:T(8,128)(2,1)S(1)}, bf16[384,256]{1,0:T(8,128)(2,1)S(1)}, u32[]{:S(2)}, u32[]{:S(2)}) collective-permute-start(bf16[384,256]{1,0:T(8,128)(2,1)S(1)} %collective-permute-done.1.refs_1_), channel_id=1, source_target_pairs={{0,16},{16,0},{1,17},{17,1},{2,18},{18,2},{3,19},{19,3},{4,20},{20... | collective-permute-start | bytes 589832 | tf_op jit(solution)/shard_map/ppermute | solution.py:299
  36.4 1.4 %collective-permute-start.6 = (bf16[384,256]{1,0:T(8,128)(2,1)S(1)}, bf16[384,256]{1,0:T(8,128)(2,1)S(1)}, u32[]{:S(2)}, u32[]{:S(2)}) collective-permute-start(bf16[384,256]{1,0:T(8,128)(2,1)S(1)} %shard_map.105.refs_3_), channel_id=1, source_target_pairs={{0,16},{16,0},{1,17},{17,1},{2,18},{18,2},{3,19},{19,3},{4,20},{20... | collective-permute-start | bytes 589832 | tf_op jit(solution)/shard_map/ppermute | solution.py:299
  52.4 5.5 %collective-permute-start.10 = (f32[8,96,128]{2,1,0:T(8,128)S(1)}, f32[8,96,128]{2,1,0:T(8,128)S(1)}, u32[]{:S(2)}, u32[]{:S(2)}) collective-permute-start(f32[8,96,128]{2,1,0:T(8,128)S(1)} %get-tuple-element.47), channel_id=1, source_target_pairs={{0,16},{16,0},{1,17},{17,1},{2,18},{18,2},{3,19},{19,3},{4,20},{20... | collective-permute-start | bytes 1179656 | tf_op jit(solution)/shard_map/ppermute | solution.py:299
  53.2 12.3 %collective-permute-start.9 = (f16[200,768]{1,0:T(8,128)(2,1)S(1)}, f16[200,768]{1,0:T(8,128)(2,1)S(1)}, u32[]{:S(2)}, u32[]{:S(2)}) collective-permute-start(f16[200,768]{1,0:T(8,128)(2,1)S(1)} %convert_element_type.22), channel_id=1, source_target_pairs={{0,2},{1,3},{2,0},{3,1},{4,6},{5,7},{6,4},{7,5},{8,10},{9,11},{10,... | collective-permute-start | bytes 921608 | tf_op jit(solution)/shard_map/ppermute | solution.py:309
  56.2 14.4 %collective-permute-start.8 = (f16[200,768]{1,0:T(8,128)(2,1)S(1)}, f16[200,768]{1,0:T(8,128)(2,1)S(1)}, u32[]{:S(2)}, u32[]{:S(2)}) collective-permute-start(f16[200,768]{1,0:T(8,128)(2,1)S(1)} %convert_element_type.20), channel_id=1, source_target_pairs={{0,3},{1,0},{2,1},{3,2},{4,7},{5,4},{6,5},{7,6},{8,11},{9,8},{10,9... | collective-permute-start | bytes 921608 | tf_op jit(solution)/shard_map/ppermute | solution.py:309
  57.1 13.6 %collective-permute-start.7 = (f16[200,768]{1,0:T(8,128)(2,1)S(1)}, f16[200,768]{1,0:T(8,128)(2,1)S(1)}, u32[]{:S(2)}, u32[]{:S(2)}) collective-permute-start(f16[200,768]{1,0:T(8,128)(2,1)S(1)} %convert_element_type.18), channel_id=1, source_target_pairs={{0,1},{1,2},{2,3},{3,0},{4,5},{5,6},{6,7},{7,4},{8,9},{9,10},{10,1... | collective-permute-start | bytes 921608 | tf_op jit(solution)/shard_map/ppermute | solution.py:309
  57.9 5.6 %collective-permute-start.11 = (f32[4,96,128]{2,1,0:T(8,128)S(1)}, f32[4,96,128]{2,1,0:T(8,128)S(1)}, u32[]{:S(2)}, u32[]{:S(2)}) collective-permute-start(f32[4,96,128]{2,1,0:T(8,128)S(1)} %get-tuple-element.49), channel_id=1, source_target_pairs={{0,128},{128,0},{1,129},{129,1},{2,130},{130,2},{3,131},{131,3},{4... | collective-permute-start | bytes 589832 | tf_op jit(solution)/shard_map/ppermute | solution.py:389
  63.6 7.1 %collective-permute-start.12 = (f32[96,128]{1,0:T(8,128)S(1)}, f32[96,128]{1,0:T(8,128)S(1)}, u32[]{:S(2)}, u32[]{:S(2)}) collective-permute-start(f32[96,128]{1,0:T(8,128)S(1)} %get-tuple-element.51), channel_id=1, source_target_pairs={{0,32},{32,64},{64,96},{96,0},{1,33},{33,65},{65,97},{97,1},{2,34}... | collective-permute-start | bytes 147464 | tf_op jit(solution)/shard_map/ppermute | solution.py:391
  63.7 7.1 %collective-permute-start.13 = (f32[96,128]{1,0:T(8,128)S(1)}, f32[96,128]{1,0:T(8,128)S(1)}, u32[]{:S(2)}, u32[]{:S(2)}) collective-permute-start(f32[96,128]{1,0:T(8,128)S(1)} %get-tuple-element.52), channel_id=1, source_target_pairs={{0,64},{32,96},{64,0},{96,32},{1,65},{33,97},{65,1},{97,33},{2,66}... | collective-permute-start | bytes 147464 | tf_op jit(solution)/shard_map/ppermute | solution.py:391
  65.5 5.3 %collective-permute-start.14 = (f32[96,128]{1,0:T(8,128)S(1)}, f32[96,128]{1,0:T(8,128)S(1)}, u32[]{:S(2)}, u32[]{:S(2)}) collective-permute-start(f32[96,128]{1,0:T(8,128)S(1)} %get-tuple-element.53), channel_id=1, source_target_pairs={{0,96},{32,0},{64,32},{96,64},{1,97},{33,1},{65,33},{97,65},{2,98}... | collective-permute-start | bytes 147464 | tf_op jit(solution)/shard_map/ppermute | solution.py:391
